TPU v7x, 512 devices: a whole 4x8x8 slice. The times are simulated.
512 devices in a mesh: seq: 32 (over y, x_lo, core), chan: 16 (over z, x_hi).
Axes of the slice: x: 4 (x_hi: 2, x_lo: 2; x = x_hi * 2 + x_lo), y: 8, z: 8, core: 2. Of those that a mesh axis runs over, the one named last changes fastest.
Arguments:
- projected: bfloat16 [3, 4096, 4096], P(None, 'chan', 'seq'), may hold values from -6 to 6
- filters: float32 [4096, 4096], P('chan', 'seq'), may hold values from -8 to 8
- skip: float32 [4096], P('chan'), may hold values from -1 to 1
- out_weight: bfloat16 [4096, 8192], P(None, 'chan'), may hold values from -0.09375 to 0.09375
- cotangent: bfloat16 [4096, 8192], P('seq', 'chan'), may hold values from -1.5 to 1.5
Outputs:
- output: bfloat16 [4096, 8192], P('seq', 'chan')
- grads: bfloat16 [3, 4096, 4096], P(None, 'chan', 'seq')
All inputs are finite; a program needn't handle non-finite values.
Results may differ from a plain program's by a relative error of at most 0.0049.
Values may be sent and summed in bfloat16 or wider, within the bound.
No kernel may reach another device: no remote copies, remote signals or barrier semaphores. Data moves between devices by JAX's collectives and lax.ppermute only.
A program may use at most 64 MiB of HBM per device.

v0:
```python
import math

import jax
import jax.numpy as jnp
from jax import lax
from jax.sharding import PartitionSpec as P

HIGHEST_PRECISION = lax.Precision.HIGHEST


def partner_2(array, axis, apart):
    return lax.ppermute(array, axis, [(i, i ^ 1 << apart) for i in range(lax.axis_size(axis))])


def twiddle_factors(count):
    index = jnp.arange(count, dtype=jnp.int32)
    phase = index[:, None] * index[None, :] % count
    angle = phase.astype(jnp.float32) * (2.0 * math.pi / count)
    return (jnp.cos(angle), jnp.sin(angle))


def rotate(values, angle):
    cosine = jnp.cos(angle)
    sine = jnp.sin(angle)
    return jnp.stack([values[0] * cosine - values[1] * sine, values[0] * sine + values[1] * cosine])


def product(left, right):
    return jnp.stack(
        [left[0] * right[0] - left[1] * right[1], left[0] * right[1] + left[1] * right[0]]
    )


def product_conjugate(left, right):
    return jnp.stack(
        [left[0] * right[0] + left[1] * right[1], left[1] * right[0] - left[0] * right[1]]
    )


def local_transform(values, cosine, sine, inverse):
    shape = values.shape
    flat = values.reshape(-1, shape[-1])
    first = jnp.dot(flat, cosine, precision=HIGHEST_PRECISION).reshape(shape)
    second = jnp.dot(flat, sine, precision=HIGHEST_PRECISION).reshape(shape)
    if inverse:
        return jnp.stack([first[0] - second[1], first[1] + second[0]])
    return jnp.stack([first[0] + second[1], first[1] - second[0]])


def bit_reverse(place, levels):
    result = jnp.zeros_like(place)
    for digit in range(levels):
        result = result | (place >> digit & 1) << levels - 1 - digit
    return result


def layout(count):
    place = lax.axis_index("seq")
    devices = lax.axis_size("seq")
    levels = devices.bit_length() - 1
    length = count * devices
    offsets = jnp.arange(count, dtype=jnp.int32)
    position = (place * count + offsets).astype(jnp.float32)
    return (place, levels, length, offsets, position)


def forward_spectrum(signal, cosine, sine):
    count = signal.shape[-1]
    place, levels, length, offsets, position = layout(count)
    turn = position * (-math.pi / length)
    zeros = jnp.zeros_like(signal)
    values = jnp.stack(
        [
            jnp.stack([signal, signal * jnp.cos(turn)], axis=1),
            jnp.stack([zeros, signal * jnp.sin(turn)], axis=1),
        ]
    )
    for section in range(levels):
        digit = levels - 1 - section
        partner = partner_2(values, "seq", digit)
        upper = place >> digit & 1 == 1
        lower = (place & (1 << digit) - 1).astype(jnp.float32)
        values = jnp.where(
            upper,
            rotate(partner - values, lower * (-2.0 * math.pi / (2 << digit))),
            values + partner,
        )
    column = bit_reverse(place, levels)
    phase = (offsets * column % length).astype(jnp.float32) * (-2.0 * math.pi / length)
    return (local_transform(rotate(values, phase), cosine, sine, False), column)


def signal_back(spectrum, column, cosine, sine):
    count = spectrum.shape[-1]
    place, levels, length, offsets, position = layout(count)
    phase = (offsets * column % length).astype(jnp.float32) * (2.0 * math.pi / length)
    values = rotate(local_transform(spectrum, cosine, sine, True), phase)
    for digit in range(levels):
        partner = partner_2(values, "seq", digit)
        upper = place >> digit & 1 == 1
        lower = (place & (1 << digit) - 1).astype(jnp.float32)
        turn_angle = lower * (2.0 * math.pi / (2 << digit))
        values = jnp.where(
            upper, partner - rotate(values, turn_angle), values + rotate(partner, turn_angle)
        )
    turn = position * (math.pi / length)
    merged_result = (
        values[0][:, 0] + values[0][:, 1] * jnp.cos(turn) - values[1][:, 1] * jnp.sin(turn)
    )
    return merged_result / (2.0 * length)


def per_device(projected, filters, skip, out_weight, cotangent):
    count = cotangent.shape[0]
    query = projected[0].astype(jnp.float32)
    key_in = projected[1].astype(jnp.float32)
    value = projected[2].astype(jnp.float32)
    mixed_in = key_in * value
    cosine, sine = twiddle_factors(count)
    spectra, column = forward_spectrum(jnp.stack([mixed_in, filters]), cosine, sine)
    filter_spectrum = spectra[:, 1:2]
    conv = signal_back(product(spectra[:, 0:1], filter_spectrum), column, cosine, sine)[0]
    inner = conv + skip[:, None] * mixed_in
    gated = (query * inner).astype(jnp.bfloat16)
    block = out_weight
    output = lax.dot_general(
        lax.all_gather(gated, "chan", axis=0, tiled=True),
        block,
        (((0,), (0,)), ((), ())),
        preferred_element_type=jnp.float32,
    ).astype(jnp.bfloat16)
    block = out_weight
    grad_gated = lax.psum_scatter(
        lax.dot_general(
            block, cotangent, (((1,), (1,)), ((), ())), preferred_element_type=jnp.float32
        ),
        "chan",
        scatter_dimension=0,
        tiled=True,
    )
    grad_inner = grad_gated * query
    grad_spectrum, grad_column = forward_spectrum(grad_inner[None], cosine, sine)
    adjoint = signal_back(
        product_conjugate(grad_spectrum, filter_spectrum), grad_column, cosine, sine
    )[0]
    grad_mixed = adjoint + skip[:, None] * grad_inner
    grads = jnp.stack([grad_gated * inner, grad_mixed * value, grad_mixed * key_in]).astype(
        jnp.bfloat16
    )
    return (output, grads)


def solution(mesh):
    in_specs = (
        P(None, "chan", "seq"),
        P("chan", "seq"),
        P("chan"),
        P(None, "chan"),
        P("seq", "chan"),
    )
    out_specs = (P("seq", "chan"), P(None, "chan", "seq"))
    return jax.shard_map(
        per_device, mesh=mesh, in_specs=in_specs, out_specs=out_specs, check_vma=False
    )
```

profile of v0, /device:TPU:1, one launch (start us, length us, event | category | flops | bytes accessed | tf_op | source)
XLA Modules:
  0.0 569.4 jit_solution(14320175104337709408)
XLA Ops:
  8.3 1.2 fusion.11
  10.6 8.3 %collective-permute-start = (f32[2,2,2,256,128]{4,3,2,1,0:T(8,128)S(1)}, f32[2,2,2,256,128]{4,3,2,1,0:T(8,128)S(1)}, u32[]{:S(2)}, u32[]{:S(2)}) collective-permute-start(f32[2,2,2,256,128]{4,3,2,1,0:T(8,128)S(1)} %pad_maximum_fusion), channel_id=1, source_target_pairs={{0,256},{16,272},{32,288},{48,304},{64,320},{80,336},{96,352},{112... | collective-permute-start | bytes 3145736 | tf_op jit(solution)/shard_map/ppermute | solution.py:12
  18.9 2.6 fusion.102
  21.7 31.1 %collective-permute-done = f32[2,2,2,256,128]{4,3,2,1,0:T(8,128)S(1)} collective-permute-done((f32[2,2,2,256,128]{4,3,2,1,0:T(8,128)S(1)}, f32[2,2,2,256,128]{4,3,2,1,0:T(8,128)S(1)}, u32[]{:S(2)}, u32[]{:S(2)}) %collective-permute-start) | collective-permute-done | bytes 1048608 | tf_op jit(solution)/shard_map/ppermute | solution.py:12
  53.0 1.3 maximum_select_fusion
  54.3 16.2 %collective-permute-start.1 = (f32[2,2,2,256,128]{4,3,2,1,0:T(8,128)}, f32[2,2,2,256,128]{4,3,2,1,0:T(8,128)}, u32[]{:S(2)}, u32[]{:S(2)}) collective-permute-start(f32[2,2,2,256,128]{4,3,2,1,0:T(8,128)} %maximum_select_fusion), channel_id=1, source_target_pairs={{0,128},{16,144},{32,160},{48,176},{64,192},{80,208},{96,224},{112... | collective-permute-start | bytes 3145736 | tf_op jit(solution)/shard_map/ppermute | solution.py:12
  70.6 46.2 %collective-permute-done.1 = f32[2,2,2,256,128]{4,3,2,1,0:T(8,128)} collective-permute-done((f32[2,2,2,256,128]{4,3,2,1,0:T(8,128)}, f32[2,2,2,256,128]{4,3,2,1,0:T(8,128)}, u32[]{:S(2)}, u32[]{:S(2)}) %collective-permute-start.1) | collective-permute-done | bytes 1048608 | tf_op jit(solution)/shard_map/ppermute | solution.py:12
  116.8 1.4 fusion.115
  118.4 1.8 maximum_select_fusion.1
  120.3 1.9 collective-permute-start.2
  122.3 24.1 %collective-permute-done.2 = f32[2,2,2,256,128]{4,3,2,1,0:T(8,128)S(1)} collective-permute-done((f32[2,2,2,256,128]{4,3,2,1,0:T(8,128)S(1)}, f32[2,2,2,256,128]{4,3,2,1,0:T(8,128)S(1)}, u32[]{:S(2)}, u32[]{:S(2)}) %collective-permute-start.2) | collective-permute-done | bytes 1048608 | tf_op jit(solution)/shard_map/ppermute | solution.py:12
  146.9 3.0 collective-permute-start.3
  149.9 81.1 %reduce-scatter.2.cloned.1.call-done = f32[256,128]{1,0:T(8,128)} async-done(((f32[4096,128]{1,0:T(8,128)}), f32[256,128]{1,0:T(8,128)}) %reduce-scatter.2.cloned.1.call-update) | async-done | bytes 131088 | tf_op jit(solution)/shard_map/reduce_scatter | solution.py:133
  232.9 7.1 %collective-permute-start.10 = (f32[2,1,2,256,128]{4,3,2,1,0:T(8,128)}, f32[2,1,2,256,128]{4,3,2,1,0:T(8,128)S(1)}, u32[]{:S(2)}, u32[]{:S(2)}) collective-permute-start(f32[2,1,2,256,128]{4,3,2,1,0:T(8,128)} %pad_maximum_fusion.4), channel_id=1, source_target_pairs={{0,256},{16,272},{32,288},{48,304},{64,320},{80,336},{96,352},{112... | collective-permute-start | bytes 1572872 | tf_op jit(solution)/shard_map/ppermute | solution.py:12
  240.4 12.9 %collective-permute-done.10 = f32[2,1,2,256,128]{4,3,2,1,0:T(8,128)S(1)} collective-permute-done((f32[2,1,2,256,128]{4,3,2,1,0:T(8,128)}, f32[2,1,2,256,128]{4,3,2,1,0:T(8,128)S(1)}, u32[]{:S(2)}, u32[]{:S(2)}) %collective-permute-start.10) | collective-permute-done | bytes 524320 | tf_op jit(solution)/shard_map/ppermute | solution.py:12
  254.3 12.4 %collective-permute-start.11 = (f32[2,1,2,256,128]{4,3,2,1,0:T(8,128)}, f32[2,1,2,256,128]{4,3,2,1,0:T(8,128)}, u32[]{:S(2)}, u32[]{:S(2)}) collective-permute-start(f32[2,1,2,256,128]{4,3,2,1,0:T(8,128)} %maximum_select_fusion.5), channel_id=1, source_target_pairs={{0,128},{16,144},{32,160},{48,176},{64,192},{80,208},{96,224},{112... | collective-permute-start | bytes 1572872 | tf_op jit(solution)/shard_map/ppermute | solution.py:12
  266.7 1.4 maximum_select_fusion.3
  268.1 5.2 collective-permute-start.4
  274.1 15.7 %collective-permute-done.11 = f32[2,1,2,256,128]{4,3,2,1,0:T(8,128)} collective-permute-done((f32[2,1,2,256,128]{4,3,2,1,0:T(8,128)}, f32[2,1,2,256,128]{4,3,2,1,0:T(8,128)}, u32[]{:S(2)}, u32[]{:S(2)}) %collective-permute-start.11) | collective-permute-done | bytes 524320 | tf_op jit(solution)/shard_map/ppermute | solution.py:12
  289.8 1.2 fusion.116
  291.0 1.2 maximum_select_fusion.6
  292.3 1.9 collective-permute-start.12
  294.2 1.3 sub.500
  295.6 1.4 maximum_select_fusion.4
  297.1 9.2 %collective-permute-done.12 = f32[2,1,2,256,128]{4,3,2,1,0:T(8,128)S(1)} collective-permute-done((f32[2,1,2,256,128]{4,3,2,1,0:T(8,128)S(1)}, f32[2,1,2,256,128]{4,3,2,1,0:T(8,128)S(1)}, u32[]{:S(2)}, u32[]{:S(2)}) %collective-permute-start.12) | collective-permute-done | bytes 524320 | tf_op jit(solution)/shard_map/ppermute | solution.py:12
  306.4 3.1 collective-permute-start.13
  309.8 1.2 fusion.48
  311.0 8.5 %collective-permute-done.13 = f32[2,1,2,256,128]{4,3,2,1,0:T(8,128)S(1)} collective-permute-done((f32[2,1,2,256,128]{4,3,2,1,0:T(8,128)S(1)}, f32[2,1,2,256,128]{4,3,2,1,0:T(8,128)S(1)}, u32[]{:S(2)}, u32[]{:S(2)}) %collective-permute-start.13) | collective-permute-done | bytes 524320 | tf_op jit(solution)/shard_map/ppermute | solution.py:12
  319.7 5.3 collective-permute-start.14
  325.0 1.2 fusion.56
  332.2 2.3 collective-permute-start.5
  334.5 2.1 collective-permute-start.15
  336.9 3.1 collective-permute-start.6
  340.2 2.2 collective-permute-start.16
  342.5 9.5 %collective-permute-done.6 = f32[2,1,2,256,128]{4,3,2,1,0:T(8,128)S(1)} collective-permute-done((f32[2,1,2,256,128]{4,3,2,1,0:T(8,128)S(1)}, f32[2,1,2,256,128]{4,3,2,1,0:T(8,128)S(1)}, u32[]{:S(2)}, u32[]{:S(2)}) %collective-permute-start.6) | collective-permute-done | bytes 524320 | tf_op jit(solution)/shard_map/ppermute | solution.py:12
  352.3 2.2 collective-permute-start.7
  354.4 8.8 %collective-permute-done.16 = f32[2,1,2,256,128]{4,3,2,1,0:T(8,128)S(1)} collective-permute-done((f32[2,1,2,256,128]{4,3,2,1,0:T(8,128)S(1)}, f32[2,1,2,256,128]{4,3,2,1,0:T(8,128)S(1)}, u32[]{:S(2)}, u32[]{:S(2)}) %collective-permute-start.16) | collective-permute-done | bytes 524320 | tf_op jit(solution)/shard_map/ppermute | solution.py:12
  363.5 2.2 collective-permute-start.17
  366.0 1.9 collective-permute-start.8
  367.9 16.4 %collective-permute-done.17 = f32[2,1,2,256,128]{4,3,2,1,0:T(8,128)S(1)} collective-permute-done((f32[2,1,2,256,128]{4,3,2,1,0:T(8,128)S(1)}, f32[2,1,2,256,128]{4,3,2,1,0:T(8,128)S(1)}, u32[]{:S(2)}, u32[]{:S(2)}) %collective-permute-start.17) | collective-permute-done | bytes 524320 | tf_op jit(solution)/shard_map/ppermute | solution.py:12
  384.6 1.9 collective-permute-start.18
  386.6 15.5 %collective-permute-done.8 = f32[2,1,2,256,128]{4,3,2,1,0:T(8,128)S(1)} collective-permute-done((f32[2,1,2,256,128]{4,3,2,1,0:T(8,128)S(1)}, f32[2,1,2,256,128]{4,3,2,1,0:T(8,128)S(1)}, u32[]{:S(2)}, u32[]{:S(2)}) %collective-permute-start.8) | collective-permute-done | bytes 524320 | tf_op jit(solution)/shard_map/ppermute | solution.py:12
  402.3 5.2 collective-permute-start.9
  407.5 17.3 %collective-permute-done.18 = f32[2,1,2,256,128]{4,3,2,1,0:T(8,128)S(1)} collective-permute-done((f32[2,1,2,256,128]{4,3,2,1,0:T(8,128)S(1)}, f32[2,1,2,256,128]{4,3,2,1,0:T(8,128)S(1)}, u32[]{:S(2)}, u32[]{:S(2)}) %collective-permute-start.18) | collective-permute-done | bytes 524320 | tf_op jit(solution)/shard_map/ppermute | solution.py:12
  425.0 5.2 collective-permute-start.19
  430.5 33.5 %collective-permute-done.19 = f32[2,1,2,256,128]{4,3,2,1,0:T(8,128)S(1)} collective-permute-done((f32[2,1,2,256,128]{4,3,2,1,0:T(8,128)S(1)}, f32[2,1,2,256,128]{4,3,2,1,0:T(8,128)S(1)}, u32[]{:S(2)}, u32[]{:S(2)}) %collective-permute-start.19) | collective-permute-done | bytes 524320 | tf_op jit(solution)/shard_map/ppermute | solution.py:12
  465.8 92.8 %all-gather.2.cloned.1.call-done = bf16[4096,128]{1,0:T(8,128)(2,1)} async-done(((bf16[256,128]{1,0:T(8,128)(2,1)}), bf16[4096,128]{1,0:T(8,128)(2,1)}) %all-gather.2.cloned.1.call-update) | async-done | bytes 1048592 | tf_op jit(solution)/shard_map/all_gather | solution.py:127
  558.6 3.9 convolution_convert_fusion
  (122 shorter events, 16.8 us)
Async XLA Ops:
  7.2 11.7 %copy-start = (bf16[128,512]{1,0:T(8,128)(2,1)S(1)}, bf16[128,512]{1,0:T(8,128)(2,1)}, u32[]{:S(2)}) copy-start(bf16[128,512]{1,0:T(8,128)(2,1)} %param.9) | copy-start | bytes 393220
  7.2 223.8 %reduce-scatter.2.cloned.1.call-start = ((), (), s32[]{:S(2)}) async-start(), calls=%async_computation.2 | async-start | bytes 2228224 | tf_op jit(solution)/shard_map/reduce_scatter | solution.py:133
  7.2 11.7 %copy-start.2 = (bf16[4096,512]{1,0:T(8,128)(2,1)S(1)}, bf16[4096,512]{1,0:T(8,128)(2,1)}, u32[]{:S(2)}) copy-start(bf16[4096,512]{1,0:T(8,128)(2,1)} %param.8) | copy-start | bytes 12582916
  10.6 42.2 %collective-permute-start = (f32[2,2,2,256,128]{4,3,2,1,0:T(8,128)S(1)}, f32[2,2,2,256,128]{4,3,2,1,0:T(8,128)S(1)}, u32[]{:S(2)}, u32[]{:S(2)}) collective-permute-start(f32[2,2,2,256,128]{4,3,2,1,0:T(8,128)S(1)} %pad_maximum_fusion), channel_id=1, source_target_pairs={{0,256},{16,272},{32,288},{48,304},{64,320},{80,336},{96,352},{112... | collective-permute-start | bytes 3145736 | tf_op jit(solution)/shard_map/ppermute | solution.py:12
  21.5 537.1 %all-gather.2.cloned.1.call-start = ((), (), s32[]{:S(2)}) async-start(), calls=%async_computation.1 | async-start | bytes 1114112 | tf_op jit(solution)/shard_map/all_gather | solution.py:127
  53.0 65.3 %copy-start.3 = (f32[1,2,2,256,128]{4,3,2,1,0:T(8,128)}, f32[1,2,2,256,128]{4,3,2,1,0:T(8,128)S(1)}, u32[]{:S(2)}) copy-start(f32[1,2,2,256,128]{4,3,2,1,0:T(8,128)S(1)} %get-tuple-element.34) | copy-start | bytes 1572868
  53.0 65.3 %copy-start.4 = (f32[1,2,2,256,128]{4,3,2,1,0:T(8,128)}, f32[1,2,2,256,128]{4,3,2,1,0:T(8,128)S(1)}, u32[]{:S(2)}) copy-start(f32[1,2,2,256,128]{4,3,2,1,0:T(8,128)S(1)} %get-tuple-element.35) | copy-start | bytes 1572868
  54.3 62.5 %collective-permute-start.1 = (f32[2,2,2,256,128]{4,3,2,1,0:T(8,128)}, f32[2,2,2,256,128]{4,3,2,1,0:T(8,128)}, u32[]{:S(2)}, u32[]{:S(2)}) collective-permute-start(f32[2,2,2,256,128]{4,3,2,1,0:T(8,128)} %maximum_select_fusion), channel_id=1, source_target_pairs={{0,128},{16,144},{32,160},{48,176},{64,192},{80,208},{96,224},{112... | collective-permute-start | bytes 3145736 | tf_op jit(solution)/shard_map/ppermute | solution.py:12
  120.3 26.2 %collective-permute-start.2 = (f32[2,2,2,256,128]{4,3,2,1,0:T(8,128)S(1)}, f32[2,2,2,256,128]{4,3,2,1,0:T(8,128)S(1)}, u32[]{:S(2)}, u32[]{:S(2)}) collective-permute-start(f32[2,2,2,256,128]{4,3,2,1,0:T(8,128)S(1)} %maximum_select_fusion.1), channel_id=1, source_target_pairs={{0,64},{16,80},{32,96},{48,112},{64,0},{80,16},{96,32},{112,48},{1... | collective-permute-start | bytes 3145736 | tf_op jit(solution)/shard_map/ppermute | solution.py:12
  146.9 93.3 %collective-permute-start.3 = (f32[2,2,2,256,128]{4,3,2,1,0:T(8,128)S(1)}, f32[2,2,2,256,128]{4,3,2,1,0:T(8,128)S(1)}, u32[]{:S(2)}, u32[]{:S(2)}) collective-permute-start(f32[2,2,2,256,128]{4,3,2,1,0:T(8,128)S(1)} %maximum_select_fusion.2), channel_id=1, source_target_pairs={{0,32},{16,48},{32,0},{48,16},{64,96},{80,112},{96,64},{112,80},{1... | collective-permute-start | bytes 3145736 | tf_op jit(solution)/shard_map/ppermute | solution.py:12
  232.9 20.4 %collective-permute-start.10 = (f32[2,1,2,256,128]{4,3,2,1,0:T(8,128)}, f32[2,1,2,256,128]{4,3,2,1,0:T(8,128)S(1)}, u32[]{:S(2)}, u32[]{:S(2)}) collective-permute-start(f32[2,1,2,256,128]{4,3,2,1,0:T(8,128)} %pad_maximum_fusion.4), channel_id=1, source_target_pairs={{0,256},{16,272},{32,288},{48,304},{64,320},{80,336},{96,352},{112... | collective-permute-start | bytes 1572872 | tf_op jit(solution)/shard_map/ppermute | solution.py:12
  240.2 14.2 %copy-start.5 = (f32[2,2,2,256,128]{4,3,2,1,0:T(8,128)}, f32[2,2,2,256,128]{4,3,2,1,0:T(8,128)S(1)}, u32[]{:S(2)}) copy-start(f32[2,2,2,256,128]{4,3,2,1,0:T(8,128)S(1)} %collective-permute-done.3) | copy-start | bytes 3145732
  253.4 13.3 %copy-start.6 = (f32[1,1,2,256,128]{4,3,2,1,0:T(8,128)}, f32[1,1,2,256,128]{4,3,2,1,0:T(8,128)S(1)}, u32[]{:S(2)}) copy-start(f32[1,1,2,256,128]{4,3,2,1,0:T(8,128)S(1)} %get-tuple-element.71) | copy-start | bytes 786436
  254.3 35.5 %collective-permute-start.11 = (f32[2,1,2,256,128]{4,3,2,1,0:T(8,128)}, f32[2,1,2,256,128]{4,3,2,1,0:T(8,128)}, u32[]{:S(2)}, u32[]{:S(2)}) collective-permute-start(f32[2,1,2,256,128]{4,3,2,1,0:T(8,128)} %maximum_select_fusion.5), channel_id=1, source_target_pairs={{0,128},{16,144},{32,160},{48,176},{64,192},{80,208},{96,224},{112... | collective-permute-start | bytes 1572872 | tf_op jit(solution)/shard_map/ppermute | solution.py:12
  268.1 26.1 %collective-permute-start.4 = (f32[2,2,2,256,128]{4,3,2,1,0:T(8,128)S(1)}, f32[2,2,2,256,128]{4,3,2,1,0:T(8,128)}, u32[]{:S(2)}, u32[]{:S(2)}) collective-permute-start(f32[2,2,2,256,128]{4,3,2,1,0:T(8,128)S(1)} %maximum_select_fusion.3), channel_id=1, source_target_pairs={{0,16},{16,0},{32,48},{48,32},{64,80},{80,64},{96,112},{112,96},{1... | collective-permute-start | bytes 3145736 | tf_op jit(solution)/shard_map/ppermute | solution.py:12
  292.3 14.0 %collective-permute-start.12 = (f32[2,1,2,256,128]{4,3,2,1,0:T(8,128)S(1)}, f32[2,1,2,256,128]{4,3,2,1,0:T(8,128)S(1)}, u32[]{:S(2)}, u32[]{:S(2)}) collective-permute-start(f32[2,1,2,256,128]{4,3,2,1,0:T(8,128)S(1)} %maximum_select_fusion.6), channel_id=1, source_target_pairs={{0,64},{16,80},{32,96},{48,112},{64,0},{80,16},{96,32},{112,48},{1... | collective-permute-start | bytes 1572872 | tf_op jit(solution)/shard_map/ppermute | solution.py:12
  306.4 13.0 %collective-permute-start.13 = (f32[2,1,2,256,128]{4,3,2,1,0:T(8,128)S(1)}, f32[2,1,2,256,128]{4,3,2,1,0:T(8,128)S(1)}, u32[]{:S(2)}, u32[]{:S(2)}) collective-permute-start(f32[2,1,2,256,128]{4,3,2,1,0:T(8,128)S(1)} %maximum_select_fusion.7), channel_id=1, source_target_pairs={{0,32},{16,48},{32,0},{48,16},{64,96},{80,112},{96,64},{112,80},{1... | collective-permute-start | bytes 1572872 | tf_op jit(solution)/shard_map/ppermute | solution.py:12
  319.7 6.6 %collective-permute-start.14 = (f32[2,1,2,256,128]{4,3,2,1,0:T(8,128)S(1)}, f32[2,1,2,256,128]{4,3,2,1,0:T(8,128)S(1)}, u32[]{:S(2)}, u32[]{:S(2)}) collective-permute-start(f32[2,1,2,256,128]{4,3,2,1,0:T(8,128)S(1)} %maximum_select_fusion.8), channel_id=1, source_target_pairs={{0,16},{16,0},{32,48},{48,32},{64,80},{80,64},{96,112},{112,96},{1... | collective-permute-start | bytes 1572872 | tf_op jit(solution)/shard_map/ppermute | solution.py:12
  332.2 4.6 collective-permute-start.5
  334.5 5.5 collective-permute-start.15
  336.9 15.1 %collective-permute-start.6 = (f32[2,1,2,256,128]{4,3,2,1,0:T(8,128)S(1)}, f32[2,1,2,256,128]{4,3,2,1,0:T(8,128)S(1)}, u32[]{:S(2)}, u32[]{:S(2)}) collective-permute-start(f32[2,1,2,256,128]{4,3,2,1,0:T(8,128)S(1)} %fusion), channel_id=1, source_target_pairs={{0,32},{16,48},{32,0},{48,16},{64,96},{80,112},{96,64},{112,80},{1... | collective-permute-start | bytes 1572872 | tf_op jit(solution)/shard_map/ppermute | solution.py:12
  340.2 23.0 %collective-permute-start.16 = (f32[2,1,2,256,128]{4,3,2,1,0:T(8,128)S(1)}, f32[2,1,2,256,128]{4,3,2,1,0:T(8,128)S(1)}, u32[]{:S(2)}, u32[]{:S(2)}) collective-permute-start(f32[2,1,2,256,128]{4,3,2,1,0:T(8,128)S(1)} %fusion.5), channel_id=1, source_target_pairs={{0,32},{16,48},{32,0},{48,16},{64,96},{80,112},{96,64},{112,80},{1... | collective-permute-start | bytes 1572872 | tf_op jit(solution)/shard_map/ppermute | solution.py:12
  352.3 13.6 %collective-permute-start.7 = (f32[2,1,2,256,128]{4,3,2,1,0:T(8,128)S(1)}, f32[2,1,2,256,128]{4,3,2,1,0:T(8,128)S(1)}, u32[]{:S(2)}, u32[]{:S(2)}) collective-permute-start(f32[2,1,2,256,128]{4,3,2,1,0:T(8,128)S(1)} %fusion.1), channel_id=1, source_target_pairs={{0,64},{16,80},{32,96},{48,112},{64,0},{80,16},{96,32},{112,48},{1... | collective-permute-start | bytes 1572872 | tf_op jit(solution)/shard_map/ppermute | solution.py:12
  363.5 20.9 %collective-permute-start.17 = (f32[2,1,2,256,128]{4,3,2,1,0:T(8,128)S(1)}, f32[2,1,2,256,128]{4,3,2,1,0:T(8,128)S(1)}, u32[]{:S(2)}, u32[]{:S(2)}) collective-permute-start(f32[2,1,2,256,128]{4,3,2,1,0:T(8,128)S(1)} %fusion.6), channel_id=1, source_target_pairs={{0,64},{16,80},{32,96},{48,112},{64,0},{80,16},{96,32},{112,48},{1... | collective-permute-start | bytes 1572872 | tf_op jit(solution)/shard_map/ppermute | solution.py:12
  366.0 36.1 %collective-permute-start.8 = (f32[2,1,2,256,128]{4,3,2,1,0:T(8,128)S(1)}, f32[2,1,2,256,128]{4,3,2,1,0:T(8,128)S(1)}, u32[]{:S(2)}, u32[]{:S(2)}) collective-permute-start(f32[2,1,2,256,128]{4,3,2,1,0:T(8,128)S(1)} %fusion.2), channel_id=1, source_target_pairs={{0,128},{16,144},{32,160},{48,176},{64,192},{80,208},{96,224},{112... | collective-permute-start | bytes 1572872 | tf_op jit(solution)/shard_map/ppermute | solution.py:12
  384.6 40.2 %collective-permute-start.18 = (f32[2,1,2,256,128]{4,3,2,1,0:T(8,128)S(1)}, f32[2,1,2,256,128]{4,3,2,1,0:T(8,128)S(1)}, u32[]{:S(2)}, u32[]{:S(2)}) collective-permute-start(f32[2,1,2,256,128]{4,3,2,1,0:T(8,128)S(1)} %fusion.7), channel_id=1, source_target_pairs={{0,128},{16,144},{32,160},{48,176},{64,192},{80,208},{96,224},{112... | collective-permute-start | bytes 1572872 | tf_op jit(solution)/shard_map/ppermute | solution.py:12
  402.3 27.9 %collective-permute-start.9 = (f32[2,1,2,256,128]{4,3,2,1,0:T(8,128)S(1)}, f32[2,1,2,256,128]{4,3,2,1,0:T(8,128)S(1)}, u32[]{:S(2)}, u32[]{:S(2)}) collective-permute-start(f32[2,1,2,256,128]{4,3,2,1,0:T(8,128)S(1)} %fusion.3), channel_id=1, source_target_pairs={{0,256},{16,272},{32,288},{48,304},{64,320},{80,336},{96,352},{112... | collective-permute-start | bytes 1572872 | tf_op jit(solution)/shard_map/ppermute | solution.py:12
  425.0 39.1 %collective-permute-start.19 = (f32[2,1,2,256,128]{4,3,2,1,0:T(8,128)S(1)}, f32[2,1,2,256,128]{4,3,2,1,0:T(8,128)S(1)}, u32[]{:S(2)}, u32[]{:S(2)}) collective-permute-start(f32[2,1,2,256,128]{4,3,2,1,0:T(8,128)S(1)} %fusion.8), channel_id=1, source_target_pairs={{0,256},{16,272},{32,288},{48,304},{64,320},{80,336},{96,352},{112... | collective-permute-start | bytes 1572872 | tf_op jit(solution)/shard_map/ppermute | solution.py:12
  430.3 33.9 %copy-start.7 = (bf16[3,256,128]{2,1,0:T(8,128)(2,1)S(1)}, bf16[3,256,128]{2,1,0:T(8,128)(2,1)}, u32[]{:S(2)}) copy-start(bf16[3,256,128]{2,1,0:T(8,128)(2,1)} %param.5) | copy-start | bytes 589828
  430.4 33.9 %copy-start.8 = (f32[256,128]{1,0:T(8,128)S(1)}, f32[256,128]{1,0:T(8,128)}, u32[]{:S(2)}) copy-start(f32[256,128]{1,0:T(8,128)} %reduce-scatter.2.cloned.1.call-done) | copy-start | bytes 393220
  430.4 33.9 %copy-start.9 = (f32[256]{0:T(256)S(1)}, f32[256]{0:T(256)}, u32[]{:S(2)}) copy-start(f32[256]{0:T(256)} %param.7) | copy-start | bytes 3076
  464.2 98.3 %copy-start.1 = (bf16[128,512]{1,0:T(8,128)(2,1)S(1)}, bf16[128,512]{1,0:T(8,128)(2,1)}, u32[]{:S(2)}) copy-start(bf16[128,512]{1,0:T(8,128)(2,1)} %param.9) | copy-start | bytes 393220
Sparse Core Ops, SparseCore 0:
  21.6 209.3 reduce-scatter.1
  465.2 93.3 all-gather.1
where the time goes:
time: 573 us; the launch traced here: 569 us
  waiting for transfers between devices  423 us (74%)
  starting transfers between devices  92.6 us (16%)
  other arithmetic  24 us (4%)
  between operations  16.3 us (3%)
  matrix products  13.8 us (2%)
    ppermute x20, waiting for transfers between devices, partner_2(): lax.ppermute(array, axis, [(i, i ^ 1 << apart) for i in range(lax.axis_si...  249 us
    all_gather x1, waiting for transfers between devices, per_device(): lax.all_gather(gated, 'chan', axis=0, tiled=True)  92.8 us
    ppermute x20, starting transfers between devices, partner_2(): lax.ppermute(array, axis, [(i, i ^ 1 << apart) for i in range(lax.axis_si...  92.5 us
    reduce_scatter x1, waiting for transfers between devices, per_device(): lax.psum_scatter(lax.dot_general(block, cotangent, (((1,), (1,)), ((), ()...  81.1 us
  transfers between devices with their start and end apart: 22, of which 15 were waited for; matrix products, arithmetic and copies ran while one was open for 4% of the time, Pallas kernels for 0%

commit v1 on v0

v1 whole, which is shorter than its diff:
```python
import jax
import jax.numpy as jnp
from jax import lax
from jax.experimental import pallas as pl
from jax.experimental.pallas import tpu as pltpu
from jax.sharding import PartitionSpec as P

BLOCK = 128
LANES = (((1,), (1,)), ((), ()))
ROWS = (((0,), (0,)), ((), ()))
VMEM_LIMIT = 32 << 20


def partial_half(half, weight, cotangent, received=None):
    planes, _, rows, width = weight.shape
    count = cotangent.shape[0]
    step = 2

    def kernel(half_ref, weight_ref, cotangent_ref, *refs):
        for plane in range(step):
            total = lax.dot_general(
                weight_ref[plane], cotangent_ref[...], LANES, preferred_element_type=jnp.float32
            )
            if received is not None:
                total = total + refs[0][plane].astype(jnp.float32)
            refs[-1][plane] = total.astype(jnp.bfloat16)

    block = pl.BlockSpec((step, rows, count), lambda i, half: (i, 0, 0))
    operands = [weight, cotangent] + ([] if received is None else [received])
    return pl.pallas_call(
        kernel,
        grid_spec=pltpu.PrefetchScalarGridSpec(
            num_scalar_prefetch=1,
            grid=(planes // step,),
            in_specs=[
                pl.BlockSpec((step, None, rows, width), lambda i, half: (i, half[0], 0, 0)),
                pl.BlockSpec((count, width), lambda i, half: (0, 0)),
            ]
            + ([] if received is None else [block]),
            out_specs=block,
        ),
        out_shape=jax.ShapeDtypeStruct((planes, rows, count), jnp.bfloat16),
        compiler_params=pltpu.CompilerParams(vmem_limit_bytes=VMEM_LIMIT),
        cost_estimate=pl.CostEstimate(
            flops=2 * planes * rows * width * count, bytes_accessed=4 << 20, transcendentals=0
        ),
        name="partial_grad_gated",
    )(half, *operands)


def project_half(half, gated, weight, before=None):
    planes, _, rows, width = weight.shape
    count = gated.shape[-1]
    step = 2
    last = planes // step - 1

    def kernel(half_ref, gated_ref, weight_ref, *refs):
        total_ref, out_ref = refs[-1], refs[-2]
        index = pl.program_id(0)

        @pl.when(index == 0)
        def _():
            if before is None:
                total_ref[...] = jnp.zeros_like(total_ref)
            else:
                total_ref[...] = refs[0][...]

        total = total_ref[...]
        for plane in range(step):
            total = total + lax.dot_general(
                gated_ref[plane], weight_ref[plane], ROWS, preferred_element_type=jnp.float32
            )
        total_ref[...] = total

        @pl.when(index == last)
        def _():
            out_ref[...] = total.astype(out_ref.dtype)

    whole = pl.BlockSpec((count, width), lambda i, half: (0, 0))
    operands = [gated, weight] + ([] if before is None else [before])
    return pl.pallas_call(
        kernel,
        grid_spec=pltpu.PrefetchScalarGridSpec(
            num_scalar_prefetch=1,
            grid=(planes // step,),
            in_specs=[
                pl.BlockSpec((step, rows, count), lambda i, half: (i, 0, 0)),
                pl.BlockSpec((step, None, rows, width), lambda i, half: (i, half[0], 0, 0)),
            ]
            + ([] if before is None else [whole]),
            out_specs=whole,
            scratch_shapes=[pltpu.VMEM((count, width), jnp.float32)],
        ),
        out_shape=jax.ShapeDtypeStruct(
            (count, width), jnp.float32 if before is None else jnp.bfloat16
        ),
        compiler_params=pltpu.CompilerParams(vmem_limit_bytes=VMEM_LIMIT),
        cost_estimate=pl.CostEstimate(
            flops=2 * planes * rows * width * count, bytes_accessed=4 << 20, transcendentals=0
        ),
        name="output_half",
    )(half, *operands)


def causal_kernel(
    skip_ref, given_ref, gated_ref, inner_ref, toeplitz_ref, wide, shifted, collected
):
    channel = pl.program_id(0)
    chunks, rows, _ = given_ref.shape
    per = rows // 4

    @pl.when(channel == 0)
    def _():
        wide[...] = given_ref[...].astype(jnp.float32).reshape(chunks * rows, BLOCK)
        shifted[pl.ds(0, chunks), :] = jnp.zeros((chunks, BLOCK), jnp.float32)

    def take(which):
        return wide[pl.ds(which * per + channel, chunks, stride=rows), :]

    query, mixed, taps = take(0), take(1) * take(2), take(3)
    shifted[pl.ds(chunks, chunks), :] = mixed
    upper = lax.broadcasted_iota(jnp.int32, (BLOCK, BLOCK), 1) >= lax.broadcasted_iota(
        jnp.int32, (BLOCK, BLOCK), 0
    )
    before = jnp.zeros((BLOCK, BLOCK), jnp.float32)
    total = jnp.zeros((chunks, BLOCK), jnp.float32)
    for lag in range(0, chunks, 2):
        blocks, signals = [], []
        for one in (lag, lag + 1):
            spread = jnp.broadcast_to(taps[one : one + 1, :], (BLOCK, BLOCK))
            turned = pltpu.roll(spread, 0, 1, stride=1, stride_axis=0)
            block = jnp.where(upper, turned, before).astype(jnp.bfloat16)
            before = turned
            toeplitz_ref[:, one * BLOCK : (one + 1) * BLOCK] = block
            blocks.append(block)
            signals.append(shifted[chunks - one : 2 * chunks - one, :].astype(jnp.bfloat16))
        total = total + jnp.dot(
            jnp.concatenate(signals, axis=1),
            jnp.concatenate(blocks, axis=0),
            preferred_element_type=jnp.float32,
        )
    inner = total + skip_ref[channel] * mixed
    inner_ref[...] = inner
    collected[pl.ds(channel, chunks, stride=per), :] = query * inner

    @pl.when(channel == per - 1)
    def _():
        gated_ref[...] = collected[...].astype(jnp.bfloat16).reshape(gated_ref.shape)


def causal(given, skip):
    chunks, rows, _ = given.shape
    per = rows // 4
    whole = pl.BlockSpec(memory_space=pltpu.SMEM)
    return pl.pallas_call(
        causal_kernel,
        grid=(per,),
        in_specs=[whole, pl.BlockSpec(given.shape, lambda c: (0, 0, 0))],
        out_specs=[
            pl.BlockSpec((chunks // 2, 2 * per, BLOCK), lambda c: (0, 0, 0)),
            pl.BlockSpec((None, chunks, BLOCK), lambda c: (c, 0, 0)),
            pl.BlockSpec((None, BLOCK, chunks * BLOCK), lambda c: (c, 0, 0)),
        ],
        out_shape=[
            jax.ShapeDtypeStruct((chunks // 2, 2 * per, BLOCK), jnp.bfloat16),
            jax.ShapeDtypeStruct((per, chunks, BLOCK), jnp.float32),
            jax.ShapeDtypeStruct((per, BLOCK, chunks * BLOCK), jnp.bfloat16),
        ],
        scratch_shapes=[
            pltpu.VMEM((chunks * rows, BLOCK), jnp.float32),
            pltpu.VMEM((2 * chunks, BLOCK), jnp.float32),
            pltpu.VMEM((chunks * per, BLOCK), jnp.float32),
        ],
        compiler_params=pltpu.CompilerParams(vmem_limit_bytes=VMEM_LIMIT),
        cost_estimate=pl.CostEstimate(
            flops=16 * per * chunks * chunks * BLOCK * BLOCK,
            bytes_accessed=16 << 20,
            transcendentals=0,
        ),
        name="causal_sum",
    )(skip, given)


def adjoint_kernel(
    skip_ref, given_ref, back_ref, inner_ref, toeplitz_ref, out_ref, wide, grads, shifted, collected
):
    channel = pl.program_id(0)
    chunks, rows, _ = given_ref.shape
    per = rows // 4

    @pl.when(channel == 0)
    def _():
        wide[...] = given_ref[...].astype(jnp.float32).reshape(chunks * rows, BLOCK)
        grads[...] = back_ref[...].astype(jnp.float32).reshape(chunks * 2 * per, BLOCK)
        shifted[pl.ds(chunks, chunks), :] = jnp.zeros((chunks, BLOCK), jnp.float32)

    def take(which):
        return wide[pl.ds(which * per + channel, chunks, stride=rows), :]

    query, key_in, value = take(0), take(1), take(2)
    grad_gated = grads[pl.ds(per + channel, chunks, stride=2 * per), :]
    grad_inner = grad_gated * query
    shifted[pl.ds(0, chunks), :] = grad_inner
    total = jnp.zeros((chunks, BLOCK), jnp.float32)
    for lag in range(0, chunks, 2):
        signals = [shifted[one : one + chunks, :] for one in (lag, lag + 1)]
        total = total + lax.dot_general(
            jnp.concatenate(signals, axis=1).astype(jnp.bfloat16),
            toeplitz_ref[:, lag * BLOCK : (lag + 2) * BLOCK],
            LANES,
            preferred_element_type=jnp.float32,
        )
    grad_mixed = total + skip_ref[channel] * grad_inner
    results = (grad_gated * inner_ref[...], grad_mixed * value, grad_mixed * key_in)
    for which, result in enumerate(results):
        collected[pl.ds(which * per + channel, chunks, stride=3 * per), :] = result

    @pl.when(channel == per - 1)
    def _():
        out_ref[...] = collected[...].astype(jnp.bfloat16).reshape(out_ref.shape)


def adjoint(given, back, inner, toeplitz, skip):
    chunks, rows, _ = given.shape
    per = rows // 4
    return pl.pallas_call(
        adjoint_kernel,
        grid=(per,),
        in_specs=[
            pl.BlockSpec(memory_space=pltpu.SMEM),
            pl.BlockSpec(given.shape, lambda c: (0, 0, 0)),
            pl.BlockSpec(back.shape, lambda c: (0, 0, 0)),
            pl.BlockSpec((None, chunks, BLOCK), lambda c: (c, 0, 0)),
            pl.BlockSpec((None, BLOCK, chunks * BLOCK), lambda c: (c, 0, 0)),
        ],
        out_specs=pl.BlockSpec((chunks // 2, 6 * per, BLOCK), lambda c: (0, 0, 0)),
        out_shape=jax.ShapeDtypeStruct((chunks // 2, 6 * per, BLOCK), jnp.bfloat16),
        scratch_shapes=[
            pltpu.VMEM((chunks * rows, BLOCK), jnp.float32),
            pltpu.VMEM((chunks * 2 * per, BLOCK), jnp.float32),
            pltpu.VMEM((2 * chunks, BLOCK), jnp.float32),
            pltpu.VMEM((chunks * 3 * per, BLOCK), jnp.float32),
        ],
        compiler_params=pltpu.CompilerParams(vmem_limit_bytes=VMEM_LIMIT),
        cost_estimate=pl.CostEstimate(
            flops=16 * per * chunks * chunks * BLOCK * BLOCK,
            bytes_accessed=16 << 20,
            transcendentals=0,
        ),
        name="adjoint_sum",
    )(skip, given, back, inner, toeplitz)


def per_device(projected, filters, skip, out_weight, cotangent):
    seq = lax.axis_size("seq")
    chan = lax.axis_size("chan")
    planes = chan // 2
    channels, count = filters.shape
    per = channels // seq
    half = lax.axis_index("chan") & 1
    own, other = half.reshape(1), (1 - half).reshape(1)
    along_z = [[2 * z + h for z in range(planes)] for h in range(2)]
    pairs = [(i, i ^ 1) for i in range(chan)]

    def exchange_seq(array):
        return lax.all_to_all(array, "seq", 0, 0, tiled=True)

    def exchange_z(array):
        return lax.all_to_all(array, "chan", 0, 0, tiled=True, axis_index_groups=along_z)

    weight = out_weight.reshape(planes, 2, channels, out_weight.shape[1])
    received = lax.ppermute(partial_half(other, weight, cotangent), "chan", pairs)
    sent = jnp.concatenate([projected, filters.astype(jnp.bfloat16)[None]]).reshape(
        4, seq, per, count
    )
    given = exchange_seq(sent.transpose(1, 0, 2, 3).reshape(seq, 4 * per, count))
    skip_here = lax.dynamic_slice(skip, (lax.axis_index("seq") * per,), (per,))
    gated, inner, toeplitz = causal(given, skip_here)
    shares = exchange_z(partial_half(own, weight, cotangent, received))
    grad_gated = jnp.sum(shares.astype(jnp.float32), axis=0).astype(jnp.bfloat16)
    middle = exchange_seq(
        jnp.concatenate(
            [gated.reshape(seq, per, count), grad_gated.reshape(seq, per, count)], axis=1
        )
    )
    gated_here = middle[:, :per].reshape(channels, count)
    gated_half = exchange_z(jnp.broadcast_to(gated_here[None], (planes, channels, count)))
    grads_there = adjoint(given, middle, inner, toeplitz, skip_here)
    gated_other = lax.ppermute(gated_half, "chan", pairs)
    grads_there, gated_half = lax.optimization_barrier((grads_there, gated_half))
    grads = exchange_seq(grads_there.reshape(seq, 3 * per, count))
    grads = grads.reshape(seq, 3, per, count).transpose(1, 0, 2, 3).reshape(3, channels, count)
    output = project_half(own, gated_half, weight)
    output = project_half(other, gated_other, weight, output)
    return output, grads


def solution(mesh):
    in_specs = (
        P(None, "chan", "seq"),
        P("chan", "seq"),
        P("chan"),
        P(None, "chan"),
        P("seq", "chan"),
    )
    out_specs = (P("seq", "chan"), P(None, "chan", "seq"))
    return jax.shard_map(
        per_device, mesh=mesh, in_specs=in_specs, out_specs=out_specs, check_vma=False
    )
```

time: 573 us -> 123 us (0.21)
  waiting for transfers between devices: 423 us -> 33.8 us
  starting transfers between devices: 92.6 us -> 35.6 us
  other arithmetic: 24 us -> 1.77 us
  local copies, waits for them, and re-layouts: 0.18 us -> 18.9 us
  Pallas kernels: 0 us -> 17.1 us
  between operations: 16.3 us -> 0.79 us
  blocking collectives: 0 us -> 14.5 us
  matrix products: 13.8 us -> 0 us
    ppermute x20 -> x2, waiting for transfers between devices: 249 us -> 7.51 us  [the longest x1 7.51 us: per_device(): gated_other = lax.ppermute(gated_half, 'chan', pairs)]
    all_gather x1 -> x0, waiting for transfers between devices: 92.8 us -> none  [per_device(): lax.all_gather(gated, 'chan', axis=0, tiled=True)]
    ppermute x20 -> x2, starting transfers between devices: 92.5 us -> 9.83 us  [the longest x1 5.48 us: per_device(): lax.ppermute(partial_half(other, weight, cotangent), 'chan', pairs)]
    reduce_scatter x1 -> x0, waiting for transfers between devices: 81.1 us -> none  [per_device(): lax.psum_scatter(lax.dot_general(block, cotangent, (((1,), (1,)), ((), ()...]
    all_to_all x0 -> x4, waiting for transfers between devices: none -> 26.3 us  [the longest x2 17.8 us: exchange_z(): lax.all_to_all(array, 'chan', 0, 0, tiled=True, axis_index_groups=along_z)]
    all_to_all x0 -> x4, starting transfers between devices: none -> 25.8 us  [the longest x2 13.5 us: exchange_z(): lax.all_to_all(array, 'chan', 0, 0, tiled=True, axis_index_groups=along_z)]
    unnamed x20, local copies, waits for them, and re-layouts: 0.06 us -> 17.2 us
    pallas_call x0 -> x6, Pallas kernels: none -> 17.1 us  [the longest x1 5.25 us: adjoint(): pl.pallas_call(adjoint_kernel, grid=(per,), in_specs=[pl.BlockSpec(memory...]
  transfers between devices with their start and end apart: 22 -> 6, of which waited for: 15 -> 5; matrix products, arithmetic and copies ran while one was open for 4% -> 2% of each run, Pallas kernels for 0% -> 11%
where the time goes in v1:
time: 123 us
  starting transfers between devices  35.6 us (29%)
  waiting for transfers between devices  33.8 us (27%)
  local copies, waits for them, and re-layouts  18.9 us (15%)
  Pallas kernels  17.1 us (14%)
  blocking collectives  14.5 us (12%)
  other arithmetic  1.77 us (1%)
    all_to_all x2, waiting for transfers between devices, exchange_z(): lax.all_to_all(array, 'chan', 0, 0, tiled=True, axis_index_groups=along_z)  17.8 us
    unnamed x20, local copies, waits for them, and re-layouts  17.2 us
    all_to_all x1, blocking collectives, exchange_seq(): return lax.all_to_all(array, 'seq', 0, 0, tiled=True)  14.5 us
    all_to_all x2, starting transfers between devices, exchange_z(): lax.all_to_all(array, 'chan', 0, 0, tiled=True, axis_index_groups=along_z)  13.5 us
    all_to_all x2, starting transfers between devices, exchange_seq(): return lax.all_to_all(array, 'seq', 0, 0, tiled=True)  12.3 us
    all_to_all x2, waiting for transfers between devices, exchange_seq(): return lax.all_to_all(array, 'seq', 0, 0, tiled=True)  8.53 us
    ppermute x1, waiting for transfers between devices, per_device(): gated_other = lax.ppermute(gated_half, 'chan', pairs)  7.51 us
    ppermute x1, starting transfers between devices, per_device(): lax.ppermute(partial_half(other, weight, cotangent), 'chan', pairs)  5.48 us
  transfers between devices with their start and end apart: 6, of which 5 were waited for; matrix products, arithmetic and copies ran while one was open for 2% of the time, Pallas kernels for 11%

profile of v1, /device:TPU:1, one launch (start us, length us, event | category | flops | bytes accessed | tf_op | source)
XLA Modules:
  0.0 122.5 jit_solution(21846712150707646)
XLA Ops:
  0.6 0.0 copy-start
  0.6 0.0 copy-start.9
  0.7 0.0 copy-start.1
  0.7 2.2 %copy-done.1 = bf16[4096,512]{1,0:T(8,128)(2,1)S(1)} copy-done((bf16[4096,512]{1,0:T(8,128)(2,1)S(1)}, bf16[4096,512]{1,0:T(8,128)(2,1)}, u32[]{:S(2)}) %copy-start.1) | copy-done | bytes 4194328
  2.9 0.0 copy-start.7
  2.9 0.9 copy-done.7
  3.8 1.4 %partial_grad_gated.2 = bf16[8,256,128]{2,1,0:T(8,128)(2,1)S(1)} custom-call(s32[1]{0:T(128)} %bitcast.half_ref, bf16[8,2,256,512]{3,2,1,0:T(8,128)(2,1)S(1)} %bitcast.27, bf16[128,512]{1,0:T(8,128)(2,1)S(1)} %copy-done.7), custom_call_target="tpu_custom_call" | custom-call | flops 268435456 | bytes 4194304 | tf_op jit(solution)/shard_map/partial_grad_gated/pallas_call | solution.py:30
  5.2 5.5 %collective-permute-start = (bf16[8,256,128]{2,1,0:T(8,128)(2,1)S(1)}, bf16[8,256,128]{2,1,0:T(8,128)(2,1)S(1)}, u32[]{:S(2)}, u32[]{:S(2)}) collective-permute-start(bf16[8,256,128]{2,1,0:T(8,128)(2,1)S(1)} %partial_grad_gated.2), channel_id=1, source_target_pairs={{0,1},{1,0},{2,3},{3,2},{4,5},{5,4},{6,7},{7,6},{8,9},{9,8},{10,11... | collective-permute-start | bytes 1572872 | tf_op jit(solution)/shard_map/ppermute | solution.py:272
  10.7 0.9 convert_bitcast_fusion
  11.6 0.0 copy-done
  11.6 0.8 maximum_bitcast_fusion
  12.4 8.2 %all-to-all-start = ((bf16[32,32,128]{2,1,0:T(8,128)(2,1)}), bf16[32,32,128]{2,1,0:T(8,128)(2,1)S(1)}, u32[]{:S(2)}, u32[]{:S(2)}) async-start(bf16[32,32,128]{2,1,0:T(8,128)(2,1)} %maximum_bitcast_fusion), calls=%async_computation | async-start | bytes 524288 | tf_op jit(solution)/shard_map/all_to_all | solution.py:266
  20.6 0.0 collective-permute-done.refs_0_
  20.6 0.0 copy-start.2
  20.6 2.2 %copy-done.2 = bf16[4096,512]{1,0:T(8,128)(2,1)S(1)} copy-done((bf16[4096,512]{1,0:T(8,128)(2,1)S(1)}, bf16[4096,512]{1,0:T(8,128)(2,1)}, u32[]{:S(2)}) %copy-start.2) | copy-done | bytes 4194328
  22.8 0.0 copy-start.8
  22.8 0.9 copy-done.8
  23.7 2.3 %partial_grad_gated.3 = bf16[8,256,128]{2,1,0:T(8,128)(2,1)} custom-call(s32[1]{0:T(128)} %bitcast.7.half_ref, bf16[8,2,256,512]{3,2,1,0:T(8,128)(2,1)S(1)} %bitcast.28, bf16[128,512]{1,0:T(8,128)(2,1)S(1)} %copy-done.8, bf16[8,256,128]{2,1,0:T(8,128)(2,1)S(1)} %collective-permute-done.refs_0_), custom_call_target="tpu_custom_call" | custom-call | flops 268435456 | bytes 4194304 | tf_op jit(solution)/shard_map/partial_grad_gated/pallas_call | solution.py:30
  26.1 6.0 %all-to-all-done.given_ref = bf16[32,32,128]{2,1,0:T(8,128)(2,1)S(1)} async-done(((bf16[32,32,128]{2,1,0:T(8,128)(2,1)}), bf16[32,32,128]{2,1,0:T(8,128)(2,1)S(1)}, u32[]{:S(2)}, u32[]{:S(2)}) %all-to-all-start) | async-done | bytes 262176 | tf_op jit(solution)/shard_map/all_to_all | solution.py:266
  32.0 10.1 %all-to-all-start.1 = ((bf16[8,256,128]{2,1,0:T(8,128)(2,1)}), bf16[8,256,128]{2,1,0:T(8,128)(2,1)S(1)}, u32[]{:S(2)}, u32[]{:S(2)}) async-start(bf16[8,256,128]{2,1,0:T(8,128)(2,1)} %partial_grad_gated.3), calls=%async_computation.1 | async-start | bytes 1048576 | tf_op jit(solution)/shard_map/all_to_all | solution.py:269
  42.1 0.0 copy-done.9
  42.1 0.1 dynamic_slice.3.skip_ref
  42.2 4.9 %causal_sum.1 = (bf16[16,16,128]{2,1,0:T(8,128)(2,1)S(1)}, f32[8,32,128]{2,1,0:T(8,128)S(1)}, bf16[8,128,4096]{2,1,0:T(8,128)(2,1)S(1)}) custom-call(f32[8]{0:T(128)S(1)} %dynamic_slice.3.skip_ref, bf16[32,32,128]{2,1,0:T(8,128)(2,1)S(1)} %all-to-all-done.given_ref), custom_call_target="tpu_custom_call" | custom-call | flops 2147483648 | bytes 16777216 | tf_op jit(solution)/shard_map/causal_sum/pallas_call | solution.py:155
  47.1 0.0 copy-start.5
  47.1 3.2 %copy-done.5 = bf16[8,128,4096]{2,1,0:T(8,128)(2,1)} copy-done((bf16[8,128,4096]{2,1,0:T(8,128)(2,1)}, bf16[8,128,4096]{2,1,0:T(8,128)(2,1)S(1)}, u32[]{:S(2)}) %copy-start.5) | copy-done | bytes 8388632
  50.3 8.6 %all-to-all-done.1 = bf16[8,256,128]{2,1,0:T(8,128)(2,1)S(1)} async-done(((bf16[8,256,128]{2,1,0:T(8,128)(2,1)}), bf16[8,256,128]{2,1,0:T(8,128)(2,1)S(1)}, u32[]{:S(2)}, u32[]{:S(2)}) %all-to-all-start.1) | async-done | bytes 524320 | tf_op jit(solution)/shard_map/all_to_all | solution.py:269
  58.9 0.1 reduce_sum.12
  59.0 14.5 %all_to_all.25.back_ref = bf16[32,16,128]{2,1,0:T(8,128)(2,1)S(1)} all-to-all(bf16[32,16,128]{2,1,0:T(8,128)(2,1)S(1)} %pad_maximum_fusion), channel_id=1, replica_groups=mesh['seq'=32,'chan'=16] {'seq'}, dimensions={0} | all-to-all | bytes 262144 | tf_op jit(solution)/shard_map/all_to_all | solution.py:266
  73.5 0.9 broadcast_in_dim.9
  74.4 3.5 %all-to-all-start.3 = ((bf16[8,256,128]{2,1,0:T(8,128)(2,1)}), bf16[8,256,128]{2,1,0:T(8,128)(2,1)S(1)}, u32[]{:S(2)}, u32[]{:S(2)}) async-start(bf16[8,256,128]{2,1,0:T(8,128)(2,1)} %broadcast_in_dim.9), calls=%async_computation.3 | async-start | bytes 1048576 | tf_op jit(solution)/shard_map/all_to_all | solution.py:269
  77.9 0.0 copy-start.6
  77.9 3.4 %copy-done.6 = bf16[8,128,4096]{2,1,0:T(8,128)(2,1)S(1)} copy-done((bf16[8,128,4096]{2,1,0:T(8,128)(2,1)S(1)}, bf16[8,128,4096]{2,1,0:T(8,128)(2,1)}, u32[]{:S(2)}) %copy-start.6) | copy-done | bytes 8388632
  81.3 5.2 %adjoint_sum.1 = bf16[16,48,128]{2,1,0:T(8,128)(2,1)} custom-call(f32[8]{0:T(128)S(1)} %dynamic_slice.3.skip_ref, bf16[32,32,128]{2,1,0:T(8,128)(2,1)S(1)} %all-to-all-done.given_ref, bf16[32,16,128]{2,1,0:T(8,128)(2,1)S(1)} %all_to_all.25.back_ref, f32[8,32,128]{2,1,0:T(8,128)S(1)} %get-tuple-element.8.inner_ref, bf16[8,128,4096]{2,1,0:T(8,128)(2,1)S(1)} %copy-done.6), custom_call_target="tpu_custom_call" | custom-call | flops 2147483648 | bytes 16777216 | tf_op jit(solution)/shard_map/adjoint_sum/pallas_call | solution.py:226
  86.6 9.2 %all-to-all-done.3.gated_ref = bf16[8,256,128]{2,1,0:T(8,128)(2,1)S(1)} async-done(((bf16[8,256,128]{2,1,0:T(8,128)(2,1)}), bf16[8,256,128]{2,1,0:T(8,128)(2,1)S(1)}, u32[]{:S(2)}, u32[]{:S(2)}) %all-to-all-start.3) | async-done | bytes 524320 | tf_op jit(solution)/shard_map/all_to_all | solution.py:269
  95.8 4.0 %all-to-all-start.4 = ((bf16[32,24,128]{2,1,0:T(8,128)(2,1)}), bf16[32,24,128]{2,1,0:T(8,128)(2,1)S(1)}, u32[]{:S(2)}, u32[]{:S(2)}) async-start(bf16[32,24,128]{2,1,0:T(8,128)(2,1)} %bitcast.11), calls=%async_computation.4 | async-start | bytes 393216 | tf_op jit(solution)/shard_map/all_to_all | solution.py:266
  99.8 4.3 %collective-permute-start.1 = (bf16[8,256,128]{2,1,0:T(8,128)(2,1)S(1)}, bf16[8,256,128]{2,1,0:T(8,128)(2,1)S(1)}, u32[]{:S(2)}, u32[]{:S(2)}) collective-permute-start(bf16[8,256,128]{2,1,0:T(8,128)(2,1)S(1)} %all-to-all-done.3.gated_ref), channel_id=1, source_target_pairs={{0,1},{1,0},{2,3},{3,2},{4,5},{5,4},{6,7},{7,6},{8,9},{9,8},{10,11... | collective-permute-start | bytes 1572872 | tf_op jit(solution)/shard_map/ppermute | solution.py:289
  104.2 0.0 copy-start.3
  104.2 2.2 %copy-done.3 = bf16[4096,512]{1,0:T(8,128)(2,1)S(1)} copy-done((bf16[4096,512]{1,0:T(8,128)(2,1)S(1)}, bf16[4096,512]{1,0:T(8,128)(2,1)}, u32[]{:S(2)}) %copy-start.3) | copy-done | bytes 4194328
  106.4 1.3 %output_half.2.refs_0_ = f32[128,512]{1,0:T(8,128)S(1)} custom-call(s32[1]{0:T(128)} %bitcast.7.half_ref, bf16[8,256,128]{2,1,0:T(8,128)(2,1)S(1)} %all-to-all-done.3.gated_ref, bf16[8,2,256,512]{3,2,1,0:T(8,128)(2,1)S(1)} %bitcast.29), custom_call_target="tpu_custom_call" | custom-call | flops 268435456 | bytes 4194304 | tf_op jit(solution)/shard_map/output_half/pallas_call | solution.py:81
  107.6 2.5 %all-to-all-done.4 = bf16[32,24,128]{2,1,0:T(8,128)(2,1)S(1)} async-done(((bf16[32,24,128]{2,1,0:T(8,128)(2,1)}), bf16[32,24,128]{2,1,0:T(8,128)(2,1)S(1)}, u32[]{:S(2)}, u32[]{:S(2)}) %all-to-all-start.4) | async-done | bytes 196640 | tf_op jit(solution)/shard_map/all_to_all | solution.py:266
  110.2 0.7 copy_bitcast_fusion
  110.9 7.5 %collective-permute-done.1.gated_ref = bf16[8,256,128]{2,1,0:T(8,128)(2,1)S(1)} collective-permute-done((bf16[8,256,128]{2,1,0:T(8,128)(2,1)S(1)}, bf16[8,256,128]{2,1,0:T(8,128)(2,1)S(1)}, u32[]{:S(2)}, u32[]{:S(2)}) %collective-permute-start.1) | collective-permute-done | bytes 524320 | tf_op jit(solution)/shard_map/ppermute | solution.py:289
  118.4 0.0 copy-start.4
  118.4 2.2 %copy-done.4 = bf16[4096,512]{1,0:T(8,128)(2,1)S(1)} copy-done((bf16[4096,512]{1,0:T(8,128)(2,1)S(1)}, bf16[4096,512]{1,0:T(8,128)(2,1)}, u32[]{:S(2)}) %copy-start.4) | copy-done | bytes 4194328
  120.6 1.9 %output_half.3 = bf16[128,512]{1,0:T(8,128)(2,1)} custom-call(s32[1]{0:T(128)} %bitcast.half_ref, bf16[8,256,128]{2,1,0:T(8,128)(2,1)S(1)} %collective-permute-done.1.gated_ref, bf16[8,2,256,512]{3,2,1,0:T(8,128)(2,1)S(1)} %bitcast.30, f32[128,512]{1,0:T(8,128)S(1)} %output_half.2.refs_0_), custom_call_target="tpu_custom_call" | custom-call | flops 268435456 | bytes 4194304 | tf_op jit(solution)/shard_map/output_half/pallas_call | solution.py:81
  (2 shorter events, 0.0 us)
Async XLA Ops:
  0.6 11.0 %copy-start = (bf16[3,256,128]{2,1,0:T(8,128)(2,1)S(1)}, bf16[3,256,128]{2,1,0:T(8,128)(2,1)}, u32[]{:S(2)}) copy-start(bf16[3,256,128]{2,1,0:T(8,128)(2,1)} %param.5) | copy-start | bytes 589828
  0.6 41.5 %copy-start.9 = (f32[256]{0:T(256)S(1)}, f32[256]{0:T(256)}, u32[]{:S(2)}) copy-start(f32[256]{0:T(256)} %param.7) | copy-start | bytes 3076
  0.7 2.2 %copy-start.1 = (bf16[4096,512]{1,0:T(8,128)(2,1)S(1)}, bf16[4096,512]{1,0:T(8,128)(2,1)}, u32[]{:S(2)}) copy-start(bf16[4096,512]{1,0:T(8,128)(2,1)} %param.8) | copy-start | bytes 12582916
  2.9 0.9 copy-start.7
  5.2 15.4 %collective-permute-start = (bf16[8,256,128]{2,1,0:T(8,128)(2,1)S(1)}, bf16[8,256,128]{2,1,0:T(8,128)(2,1)S(1)}, u32[]{:S(2)}, u32[]{:S(2)}) collective-permute-start(bf16[8,256,128]{2,1,0:T(8,128)(2,1)S(1)} %partial_grad_gated.2), channel_id=1, source_target_pairs={{0,1},{1,0},{2,3},{3,2},{4,5},{5,4},{6,7},{7,6},{8,9},{9,8},{10,11... | collective-permute-start | bytes 1572872 | tf_op jit(solution)/shard_map/ppermute | solution.py:272
  12.4 19.7 %all-to-all-start = ((bf16[32,32,128]{2,1,0:T(8,128)(2,1)}), bf16[32,32,128]{2,1,0:T(8,128)(2,1)S(1)}, u32[]{:S(2)}, u32[]{:S(2)}) async-start(bf16[32,32,128]{2,1,0:T(8,128)(2,1)} %maximum_bitcast_fusion), calls=%async_computation | async-start | bytes 524288 | tf_op jit(solution)/shard_map/all_to_all | solution.py:266
  20.6 2.2 %copy-start.2 = (bf16[4096,512]{1,0:T(8,128)(2,1)S(1)}, bf16[4096,512]{1,0:T(8,128)(2,1)}, u32[]{:S(2)}) copy-start(bf16[4096,512]{1,0:T(8,128)(2,1)} %param.8) | copy-start | bytes 12582916
  22.8 0.9 copy-start.8
  32.0 26.9 %all-to-all-start.1 = ((bf16[8,256,128]{2,1,0:T(8,128)(2,1)}), bf16[8,256,128]{2,1,0:T(8,128)(2,1)S(1)}, u32[]{:S(2)}, u32[]{:S(2)}) async-start(bf16[8,256,128]{2,1,0:T(8,128)(2,1)} %partial_grad_gated.3), calls=%async_computation.1 | async-start | bytes 1048576 | tf_op jit(solution)/shard_map/all_to_all | solution.py:269
  47.1 3.2 %copy-start.5 = (bf16[8,128,4096]{2,1,0:T(8,128)(2,1)}, bf16[8,128,4096]{2,1,0:T(8,128)(2,1)S(1)}, u32[]{:S(2)}) copy-start(bf16[8,128,4096]{2,1,0:T(8,128)(2,1)S(1)} %get-tuple-element.9.toeplitz_ref) | copy-start | bytes 25165828
  74.4 21.4 %all-to-all-start.3 = ((bf16[8,256,128]{2,1,0:T(8,128)(2,1)}), bf16[8,256,128]{2,1,0:T(8,128)(2,1)S(1)}, u32[]{:S(2)}, u32[]{:S(2)}) async-start(bf16[8,256,128]{2,1,0:T(8,128)(2,1)} %broadcast_in_dim.9), calls=%async_computation.3 | async-start | bytes 1048576 | tf_op jit(solution)/shard_map/all_to_all | solution.py:269
  77.9 3.4 %copy-start.6 = (bf16[8,128,4096]{2,1,0:T(8,128)(2,1)S(1)}, bf16[8,128,4096]{2,1,0:T(8,128)(2,1)}, u32[]{:S(2)}) copy-start(bf16[8,128,4096]{2,1,0:T(8,128)(2,1)} %copy-done.5) | copy-start | bytes 25165828
  95.8 14.4 %all-to-all-start.4 = ((bf16[32,24,128]{2,1,0:T(8,128)(2,1)}), bf16[32,24,128]{2,1,0:T(8,128)(2,1)S(1)}, u32[]{:S(2)}, u32[]{:S(2)}) async-start(bf16[32,24,128]{2,1,0:T(8,128)(2,1)} %bitcast.11), calls=%async_computation.4 | async-start | bytes 393216 | tf_op jit(solution)/shard_map/all_to_all | solution.py:266
  99.8 18.6 %collective-permute-start.1 = (bf16[8,256,128]{2,1,0:T(8,128)(2,1)S(1)}, bf16[8,256,128]{2,1,0:T(8,128)(2,1)S(1)}, u32[]{:S(2)}, u32[]{:S(2)}) collective-permute-start(bf16[8,256,128]{2,1,0:T(8,128)(2,1)S(1)} %all-to-all-done.3.gated_ref), channel_id=1, source_target_pairs={{0,1},{1,0},{2,3},{3,2},{4,5},{5,4},{6,7},{7,6},{8,9},{9,8},{10,11... | collective-permute-start | bytes 1572872 | tf_op jit(solution)/shard_map/ppermute | solution.py:289
  104.2 2.2 %copy-start.3 = (bf16[4096,512]{1,0:T(8,128)(2,1)S(1)}, bf16[4096,512]{1,0:T(8,128)(2,1)}, u32[]{:S(2)}) copy-start(bf16[4096,512]{1,0:T(8,128)(2,1)} %param.8) | copy-start | bytes 12582916
  118.4 2.2 %copy-start.4 = (bf16[4096,512]{1,0:T(8,128)(2,1)S(1)}, bf16[4096,512]{1,0:T(8,128)(2,1)}, u32[]{:S(2)}) copy-start(bf16[4096,512]{1,0:T(8,128)(2,1)} %param.8) | copy-start | bytes 12582916

commit v2 on v0

v2 whole, which is shorter than its diff:
```python
import jax
import jax.numpy as jnp
from jax import lax
from jax.experimental import pallas as pl
from jax.experimental.pallas import tpu as pltpu
from jax.sharding import PartitionSpec as P

BLOCK = 128
LANES = (((1,), (1,)), ((), ()))
ROWS = (((0,), (0,)), ((), ()))
VMEM_LIMIT = 8 << 20
FIRST_LIMIT = 54 << 20
VMEM = pl.BlockSpec(memory_space=pltpu.VMEM)
HBM = pl.BlockSpec(memory_space=pltpu.HBM)
SMEM = pl.BlockSpec(memory_space=pltpu.SMEM)


def call(kernel, in_specs, out_shape, flops, scratch=(), name=None, limit=VMEM_LIMIT):
    return pl.pallas_call(
        kernel,
        in_specs=in_specs,
        out_specs=jax.tree.map(lambda _: VMEM, out_shape),
        out_shape=out_shape,
        scratch_shapes=list(scratch),
        compiler_params=pltpu.CompilerParams(vmem_limit_bytes=limit),
        cost_estimate=pl.CostEstimate(flops=flops, bytes_accessed=4 << 20, transcendentals=0),
        name=name,
    )


def partial_half(half, weight, cotangent, dtype):
    planes, _, rows, width = weight.shape
    count = cotangent.shape[0]

    def kernel(half_ref, weight_ref, cotangent_ref, out_ref):
        for plane in range(planes):
            out_ref[plane] = lax.dot_general(
                weight_ref[plane, half_ref[0]],
                cotangent_ref[...],
                LANES,
                preferred_element_type=jnp.float32,
            ).astype(dtype)

    return call(
        kernel,
        [SMEM, VMEM, VMEM],
        jax.ShapeDtypeStruct((planes, rows, count), dtype),
        2 * planes * rows * width * count,
        name="partial_grad_gated",
    )(half, weight, cotangent)


def total_share(share, received):
    def kernel(share_ref, received_ref, out_ref):
        total = share_ref[...] + received_ref[...].astype(jnp.float32)
        out_ref[...] = total.astype(jnp.bfloat16)

    return call(
        kernel,
        [VMEM, VMEM],
        jax.ShapeDtypeStruct(share.shape, jnp.bfloat16),
        1 << 24,
        name="total_share",
    )(share, received)


def project_half(half, gated, weight, before=None):
    planes, rows, width = weight.shape[0], weight.shape[-2], weight.shape[-1]
    count = gated.shape[-1]
    result = jax.ShapeDtypeStruct((count, width), jnp.float32 if before is None else jnp.bfloat16)

    def early(half_ref, gated_ref, weight_ref, out_ref, kept_ref, moved):
        copy = pltpu.make_async_copy(weight_ref.at[:, 1 - half_ref[0]], kept_ref, moved)
        copy.start()
        total = jnp.zeros((count, width), jnp.float32)
        for plane in range(planes):
            total = total + lax.dot_general(
                gated_ref[plane],
                weight_ref[plane, half_ref[0]],
                ROWS,
                preferred_element_type=jnp.float32,
            )
        out_ref[...] = total
        copy.wait()

    def late(gated_ref, weight_ref, before_ref, out_ref):
        total = before_ref[...]
        for plane in range(planes):
            total = total + lax.dot_general(
                gated_ref[plane], weight_ref[plane], ROWS, preferred_element_type=jnp.float32
            )
        out_ref[...] = total.astype(out_ref.dtype)

    flops = 2 * planes * rows * width * count
    if before is None:
        kept = jax.ShapeDtypeStruct((planes, rows, width), weight.dtype)
        return call(
            early,
            [SMEM, VMEM, VMEM],
            [result, kept],
            flops,
            [pltpu.SemaphoreType.DMA],
            name="output_early",
        )(half, gated, weight)
    return call(late, [VMEM] * 3, result, flops, name="output_late")(gated, weight, before)


def first(half, weight, cotangent, projected, filters, seq):
    planes, _, rows, width = weight.shape
    _, channels, count = projected.shape
    per = channels // seq

    def kernel(
        half_ref,
        weight_ref,
        cotangent_ref,
        projected_ref,
        filters_ref,
        share_ref,
        packed_ref,
        weight_here,
        cotangent_here,
        projected_here,
        filters_here,
        arrived,
    ):
        places = [
            (projected_ref, projected_here),
            (filters_ref, filters_here),
            (cotangent_ref, cotangent_here),
        ]
        places += [
            (weight_ref.at[plane, half_ref[0]], weight_here.at[plane]) for plane in range(planes)
        ]
        copies = [
            pltpu.make_async_copy(source, target, arrived.at[i])
            for i, (source, target) in enumerate(places)
        ]
        for copy in copies:
            copy.start()
        copies[0].wait()
        copies[1].wait()
        parts = [projected_here[which].astype(jnp.float32) for which in range(3)]
        parts = [part.reshape(seq, per, count) for part in parts + [filters_here[...]]]
        packed_ref[...] = jnp.concatenate(parts, axis=1).astype(jnp.bfloat16)
        copies[2].wait()
        for plane in range(planes):
            copies[3 + plane].wait()
            share_ref[plane] = lax.dot_general(
                weight_here[plane], cotangent_here[...], LANES, preferred_element_type=jnp.float32
            ).astype(jnp.bfloat16)

    return call(
        kernel,
        [SMEM, HBM, HBM, HBM, HBM],
        [
            jax.ShapeDtypeStruct((planes, rows, count), jnp.bfloat16),
            jax.ShapeDtypeStruct((seq, 4 * per, count), jnp.bfloat16),
        ],
        2 * planes * rows * width * count,
        [
            pltpu.VMEM((planes, rows, width), weight.dtype),
            pltpu.VMEM(cotangent.shape, cotangent.dtype),
            pltpu.VMEM(projected.shape, projected.dtype),
            pltpu.VMEM(filters.shape, filters.dtype),
            pltpu.SemaphoreType.DMA((planes + 3,)),
        ],
        "first_share",
        FIRST_LIMIT,
    )(half, weight, cotangent, projected, filters)


def pack_middle(gated, shares, seq):
    planes, channels, count = shares.shape
    per = channels // seq

    def kernel(gated_ref, shares_ref, out_ref):
        total = shares_ref[0].astype(jnp.float32)
        for plane in range(1, planes):
            total = total + shares_ref[plane].astype(jnp.float32)
        there = gated_ref[...].astype(jnp.float32).reshape(seq, per, count)
        out_ref[...] = jnp.concatenate(
            [there, total.reshape(seq, per, count)], axis=1
        ).astype(jnp.bfloat16)

    return call(
        kernel,
        [VMEM, VMEM],
        jax.ShapeDtypeStruct((seq, 2 * per, count), jnp.bfloat16),
        1 << 24,
        name="pack_middle",
    )(gated, shares)


def spread(middle, planes):
    seq, rows, count = middle.shape
    per = rows // 2

    def kernel(middle_ref, out_ref):
        gated = middle_ref[...].astype(jnp.float32)[:, :per].reshape(seq * per, count)
        gated = gated.astype(jnp.bfloat16)
        for plane in range(planes):
            out_ref[plane] = gated

    return call(
        kernel,
        [VMEM],
        jax.ShapeDtypeStruct((planes, seq * per, count), jnp.bfloat16),
        1 << 24,
        name="spread_gated",
    )(middle)


def unpack(grads, per):
    pairs, rows, count = grads.shape
    seq = 2 * pairs

    def kernel(grads_ref, out_ref):
        there = grads_ref[...].astype(jnp.float32).reshape(seq, 3, per, count)
        for which in range(3):
            out_ref[which] = there[:, which].reshape(seq * per, count).astype(jnp.bfloat16)

    return call(
        kernel,
        [VMEM],
        jax.ShapeDtypeStruct((3, seq * per, count), jnp.bfloat16),
        1 << 24,
        name="unpack_grads",
    )(grads)


def causal(given, skip):
    chunks, rows, _ = given.shape
    per = rows // 4

    def kernel(skip_ref, given_ref, gated_ref, inner_ref, toeplitz_ref, wide, shifted, collected):
        wide[...] = given_ref[...].astype(jnp.float32).reshape(chunks * rows, BLOCK)
        shifted[pl.ds(0, chunks), :] = jnp.zeros((chunks, BLOCK), jnp.float32)
        upper = lax.broadcasted_iota(jnp.int32, (BLOCK, BLOCK), 1) >= lax.broadcasted_iota(
            jnp.int32, (BLOCK, BLOCK), 0
        )

        @pl.loop(0, per)
        def _(channel):
            def take(which):
                return wide[pl.ds(which * per + channel, chunks, stride=rows), :]

            query, mixed, taps = take(0), take(1) * take(2), take(3)
            shifted[pl.ds(chunks, chunks), :] = mixed
            before = jnp.zeros((BLOCK, BLOCK), jnp.float32)
            total = jnp.zeros((chunks, BLOCK), jnp.float32)
            for lag in range(0, chunks, 2):
                blocks, signals = [], []
                for one in (lag, lag + 1):
                    spread = jnp.broadcast_to(taps[one : one + 1, :], (BLOCK, BLOCK))
                    turned = pltpu.roll(spread, 0, 1, stride=1, stride_axis=0)
                    block = jnp.where(upper, turned, before).astype(jnp.bfloat16)
                    before = turned
                    toeplitz_ref[channel, :, one * BLOCK : (one + 1) * BLOCK] = block
                    blocks.append(block)
                    signals.append(shifted[chunks - one : 2 * chunks - one, :].astype(jnp.bfloat16))
                total = total + jnp.dot(
                    jnp.concatenate(signals, axis=1),
                    jnp.concatenate(blocks, axis=0),
                    preferred_element_type=jnp.float32,
                )
            inner = total + skip_ref[channel] * mixed
            inner_ref[channel] = inner
            collected[pl.ds(channel, chunks, stride=per), :] = query * inner

        gated_ref[...] = collected[...].astype(jnp.bfloat16).reshape(gated_ref.shape)

    return call(
        kernel,
        [SMEM, VMEM],
        [
            jax.ShapeDtypeStruct((chunks // 2, 2 * per, BLOCK), jnp.bfloat16),
            jax.ShapeDtypeStruct((per, chunks, BLOCK), jnp.float32),
            jax.ShapeDtypeStruct((per, BLOCK, chunks * BLOCK), jnp.bfloat16),
        ],
        16 * per * chunks * chunks * BLOCK * BLOCK,
        [
            pltpu.VMEM((chunks * rows, BLOCK), jnp.float32),
            pltpu.VMEM((2 * chunks, BLOCK), jnp.float32),
            pltpu.VMEM((chunks * per, BLOCK), jnp.float32),
        ],
        "causal_sum",
    )(skip, given)


def adjoint(given, back, inner, toeplitz, skip):
    chunks, rows, _ = given.shape
    per = rows // 4

    def kernel(
        skip_ref, given_ref, back_ref, inner_ref, toeplitz_ref, out_ref, wide, grads, shifted, collected
    ):
        wide[...] = given_ref[...].astype(jnp.float32).reshape(chunks * rows, BLOCK)
        grads[...] = back_ref[...].astype(jnp.float32).reshape(chunks * 2 * per, BLOCK)
        shifted[pl.ds(chunks, chunks), :] = jnp.zeros((chunks, BLOCK), jnp.float32)

        @pl.loop(0, per)
        def _(channel):
            def take(which):
                return wide[pl.ds(which * per + channel, chunks, stride=rows), :]

            query, key_in, value = take(0), take(1), take(2)
            grad_gated = grads[pl.ds(per + channel, chunks, stride=2 * per), :]
            grad_inner = grad_gated * query
            shifted[pl.ds(0, chunks), :] = grad_inner
            total = jnp.zeros((chunks, BLOCK), jnp.float32)
            for lag in range(0, chunks, 2):
                signals = [shifted[one : one + chunks, :] for one in (lag, lag + 1)]
                total = total + lax.dot_general(
                    jnp.concatenate(signals, axis=1).astype(jnp.bfloat16),
                    toeplitz_ref[channel, :, lag * BLOCK : (lag + 2) * BLOCK],
                    LANES,
                    preferred_element_type=jnp.float32,
                )
            grad_mixed = total + skip_ref[channel] * grad_inner
            results = (grad_gated * inner_ref[channel], grad_mixed * value, grad_mixed * key_in)
            for which, result in enumerate(results):
                collected[pl.ds(which * per + channel, chunks, stride=3 * per), :] = result

        out_ref[...] = collected[...].astype(jnp.bfloat16).reshape(out_ref.shape)

    return call(
        kernel,
        [SMEM, VMEM, VMEM, VMEM, VMEM],
        jax.ShapeDtypeStruct((chunks // 2, 6 * per, BLOCK), jnp.bfloat16),
        16 * per * chunks * chunks * BLOCK * BLOCK,
        [
            pltpu.VMEM((chunks * rows, BLOCK), jnp.float32),
            pltpu.VMEM((chunks * 2 * per, BLOCK), jnp.float32),
            pltpu.VMEM((2 * chunks, BLOCK), jnp.float32),
            pltpu.VMEM((chunks * 3 * per, BLOCK), jnp.float32),
        ],
        "adjoint_sum",
    )(skip, given, back, inner, toeplitz)


def per_device(projected, filters, skip, out_weight, cotangent):
    seq = lax.axis_size("seq")
    chan = lax.axis_size("chan")
    planes = chan // 2
    channels, count = filters.shape
    per = channels // seq
    half = lax.axis_index("chan") & 1
    own, other = half.reshape(1), (1 - half).reshape(1)
    along_z = [[2 * z + h for z in range(planes)] for h in range(2)]
    pairs = [(i, i ^ 1) for i in range(chan)]

    def exchange_seq(array):
        return lax.all_to_all(array, "seq", 0, 0, tiled=True)

    def exchange_z(array):
        return lax.all_to_all(array, "chan", 0, 0, tiled=True, axis_index_groups=along_z)

    weight = out_weight.reshape(planes, 2, channels, out_weight.shape[1])
    share_other, packed = first(other, weight, cotangent, projected, filters, seq)
    received = lax.ppermute(share_other, "chan", pairs)
    given = exchange_seq(packed)
    share_own = partial_half(own, weight, cotangent, jnp.float32)
    skip_here = lax.dynamic_slice(skip, (lax.axis_index("seq") * per,), (per,))
    gated, inner, toeplitz = causal(given, skip_here)
    shares = exchange_z(total_share(share_own, received))
    middle = exchange_seq(pack_middle(gated, shares, seq))
    gated_half = exchange_z(spread(middle, planes))
    grads_there = adjoint(given, middle, inner, toeplitz, skip_here)
    grads_there, gated_half = lax.optimization_barrier((grads_there, gated_half))
    gated_other = lax.ppermute(gated_half, "chan", pairs)
    output, weight_other = project_half(own, gated_half, weight)
    grads = exchange_seq(grads_there.reshape(seq, 3 * per, count))
    output = project_half(other, gated_other, weight_other, output)
    grads, output = lax.optimization_barrier((grads, output))
    grads = unpack(grads.reshape(seq // 2, 6 * per, count), per)
    return output, grads


def solution(mesh):
    in_specs = (
        P(None, "chan", "seq"),
        P("chan", "seq"),
        P("chan"),
        P(None, "chan"),
        P("seq", "chan"),
    )
    out_specs = (P("seq", "chan"), P(None, "chan", "seq"))
    return jax.shard_map(
        per_device, mesh=mesh, in_specs=in_specs, out_specs=out_specs, check_vma=False
    )
```

time: 573 us -> 115 us (0.20)
  waiting for transfers between devices: 423 us -> 33.7 us
  starting transfers between devices: 92.6 us -> 34.6 us
  other arithmetic: 24 us -> 0 us
  Pallas kernels: 0 us -> 19.2 us
  between operations: 16.3 us -> 0.78 us
  blocking collectives: 0 us -> 14.8 us
  matrix products: 13.8 us -> 0 us
  local copies, waits for them, and re-layouts: 0.18 us -> 11.1 us
    ppermute x20 -> x2, waiting for transfers between devices: 249 us -> 7.98 us  [the longest x1 7.98 us: per_device(): gated_other = lax.ppermute(gated_half, 'chan', pairs)]
    all_gather x1 -> x0, waiting for transfers between devices: 92.8 us -> none  [per_device(): lax.all_gather(gated, 'chan', axis=0, tiled=True)]
    ppermute x20 -> x2, starting transfers between devices: 92.5 us -> 8.53 us  [the longest x1 5.48 us: per_device(): received = lax.ppermute(share_other, 'chan', pairs)]
    reduce_scatter x1 -> x0, waiting for transfers between devices: 81.1 us -> none  [per_device(): lax.psum_scatter(lax.dot_general(block, cotangent, (((1,), (1,)), ((), ()...]
    all_to_all x0 -> x4, starting transfers between devices: none -> 26.1 us  [the longest x2 13.5 us: exchange_z(): lax.all_to_all(array, 'chan', 0, 0, tiled=True, axis_index_groups=along_z)]
    all_to_all x0 -> x4, waiting for transfers between devices: none -> 25.7 us  [the longest x2 18.2 us: exchange_z(): lax.all_to_all(array, 'chan', 0, 0, tiled=True, axis_index_groups=along_z)]
    pallas_call x0 -> x10, Pallas kernels: none -> 19.2 us  [the longest x1 5.07 us: adjoint(): call(kernel, [SMEM, VMEM, VMEM, VMEM, VMEM], jax.ShapeDtypeStruct((chunks...]
    all_to_all x0 -> x1, blocking collectives: none -> 14.8 us  [exchange_seq(): return lax.all_to_all(array, 'seq', 0, 0, tiled=True)]
  transfers between devices with their start and end apart: 22 -> 6, of which waited for: 15 -> 4; matrix products, arithmetic and copies ran while one was open for 4% -> 0% of each run, Pallas kernels for 0% -> 12%
where the time goes in v2:
time: 115 us; the launch traced here: 114 us
  starting transfers between devices  34.6 us (30%)
  waiting for transfers between devices  33.7 us (29%)
  Pallas kernels  19.2 us (17%)
  blocking collectives  14.8 us (13%)
  local copies, waits for them, and re-layouts  11.1 us (10%)
    all_to_all x2, waiting for transfers between devices, exchange_z(): lax.all_to_all(array, 'chan', 0, 0, tiled=True, axis_index_groups=along_z)  18.2 us
    all_to_all x1, blocking collectives, exchange_seq(): return lax.all_to_all(array, 'seq', 0, 0, tiled=True)  14.8 us
    all_to_all x2, starting transfers between devices, exchange_z(): lax.all_to_all(array, 'chan', 0, 0, tiled=True, axis_index_groups=along_z)  13.5 us
    all_to_all x2, starting transfers between devices, exchange_seq(): return lax.all_to_all(array, 'seq', 0, 0, tiled=True)  12.6 us
    unnamed x12, local copies, waits for them, and re-layouts  11 us
    ppermute x1, waiting for transfers between devices, per_device(): gated_other = lax.ppermute(gated_half, 'chan', pairs)  7.98 us
    all_to_all x2, waiting for transfers between devices, exchange_seq(): return lax.all_to_all(array, 'seq', 0, 0, tiled=True)  7.59 us
    ppermute x1, starting transfers between devices, per_device(): received = lax.ppermute(share_other, 'chan', pairs)  5.48 us
  transfers between devices with their start and end apart: 6, of which 4 were waited for; matrix products, arithmetic and copies ran while one was open for 0% of the time, Pallas kernels for 12%

profile of v2, /device:TPU:1, one launch (start us, length us, event | category | flops | bytes accessed | tf_op | source)
XLA Modules:
  0.0 114.3 jit_solution(276520677376524332)
XLA Ops:
  0.6 0.0 copy-start.4
  0.6 4.4 %first_share.1 = (bf16[8,256,128]{2,1,0:T(8,128)(2,1)}, bf16[32,32,128]{2,1,0:T(8,128)(2,1)}) custom-call(s32[1]{0:T(128)} %bitcast.half_ref, bf16[8,2,256,512]{3,2,1,0:T(8,128)(2,1)} %bitcast.5, bf16[128,512]{1,0:T(8,128)(2,1)} %cotangent_ref.3, bf16[3,256,128]{2,1,0:T(8,128)(2,1)} %projected_ref.1, f32[256,128]{1,0:T(8,128)} %filters_ref.1), custom_call_target="tpu_custom_call" | custom-call | flops 268435456 | bytes 4194304 | tf_op jit(solution)/shard_map/first_share/pallas_call | solution.py:153
  5.0 5.5 %collective-permute-start = (bf16[8,256,128]{2,1,0:T(8,128)(2,1)}, bf16[8,256,128]{2,1,0:T(8,128)(2,1)S(1)}, u32[]{:S(2)}, u32[]{:S(2)}) collective-permute-start(bf16[8,256,128]{2,1,0:T(8,128)(2,1)} %get-tuple-element.15), channel_id=1, source_target_pairs={{0,1},{1,0},{2,3},{3,2},{4,5},{5,4},{6,7},{7,6},{8,9},{9,8},{10,11... | collective-permute-start | bytes 1572872 | tf_op jit(solution)/shard_map/ppermute | solution.py:361
  10.5 8.3 %all-to-all-start = ((bf16[32,32,128]{2,1,0:T(8,128)(2,1)}), bf16[32,32,128]{2,1,0:T(8,128)(2,1)S(1)}, u32[]{:S(2)}, u32[]{:S(2)}) async-start(bf16[32,32,128]{2,1,0:T(8,128)(2,1)} %get-tuple-element.13), calls=%async_computation | async-start | bytes 524288 | tf_op jit(solution)/shard_map/all_to_all | solution.py:354
  18.8 0.0 copy-done.4
  18.8 0.0 copy-start
  18.8 2.2 %copy-done = bf16[4096,512]{1,0:T(8,128)(2,1)S(1)} copy-done((bf16[4096,512]{1,0:T(8,128)(2,1)S(1)}, bf16[4096,512]{1,0:T(8,128)(2,1)}, u32[]{:S(2)}) %copy-start) | copy-done | bytes 4194328
  21.0 0.0 copy-start.5
  21.0 0.7 partial_grad_gated.1.share_ref
  21.7 0.0 collective-permute-done.received_ref
  21.7 0.9 total_share.1
  22.6 7.6 %all-to-all-done.given_ref = bf16[32,32,128]{2,1,0:T(8,128)(2,1)S(1)} async-done(((bf16[32,32,128]{2,1,0:T(8,128)(2,1)}), bf16[32,32,128]{2,1,0:T(8,128)(2,1)S(1)}, u32[]{:S(2)}, u32[]{:S(2)}) %all-to-all-start) | async-done | bytes 262176 | tf_op jit(solution)/shard_map/all_to_all | solution.py:354
  30.2 10.0 %all-to-all-start.1 = ((bf16[8,256,128]{2,1,0:T(8,128)(2,1)}), bf16[8,256,128]{2,1,0:T(8,128)(2,1)S(1)}, u32[]{:S(2)}, u32[]{:S(2)}) async-start(bf16[8,256,128]{2,1,0:T(8,128)(2,1)} %total_share.1), calls=%async_computation.1 | async-start | bytes 1048576 | tf_op jit(solution)/shard_map/all_to_all | solution.py:357
  40.2 0.0 copy-done.5
  40.3 0.1 dynamic_slice.3.skip_ref
  40.3 4.7 %causal_sum.1 = (bf16[16,16,128]{2,1,0:T(8,128)(2,1)S(1)}, f32[8,32,128]{2,1,0:T(8,128)S(1)}, bf16[8,128,4096]{2,1,0:T(8,128)(2,1)S(1)}) custom-call(f32[8]{0:T(128)S(1)} %dynamic_slice.3.skip_ref, bf16[32,32,128]{2,1,0:T(8,128)(2,1)S(1)} %all-to-all-done.given_ref), custom_call_target="tpu_custom_call" | custom-call | flops 2147483648 | bytes 4194304 | tf_op jit(solution)/shard_map/causal_sum/pallas_call | solution.py:273
  45.1 0.0 copy-start.2
  45.1 3.2 %copy-done.2 = bf16[8,128,4096]{2,1,0:T(8,128)(2,1)} copy-done((bf16[8,128,4096]{2,1,0:T(8,128)(2,1)}, bf16[8,128,4096]{2,1,0:T(8,128)(2,1)S(1)}, u32[]{:S(2)}) %copy-start.2) | copy-done | bytes 8388632
  48.3 8.8 %all-to-all-done.1.shares_ref = bf16[8,256,128]{2,1,0:T(8,128)(2,1)S(1)} async-done(((bf16[8,256,128]{2,1,0:T(8,128)(2,1)}), bf16[8,256,128]{2,1,0:T(8,128)(2,1)S(1)}, u32[]{:S(2)}, u32[]{:S(2)}) %all-to-all-start.1) | async-done | bytes 524320 | tf_op jit(solution)/shard_map/all_to_all | solution.py:357
  57.0 0.1 pack_middle.1
  57.1 14.8 %all_to_all.25.back_ref.middle_ref = bf16[32,16,128]{2,1,0:T(8,128)(2,1)S(1)} all-to-all(bf16[32,16,128]{2,1,0:T(8,128)(2,1)S(1)} %pack_middle.1), channel_id=1, replica_groups=mesh['seq'=32,'chan'=16] {'seq'}, dimensions={0} | all-to-all | bytes 262144 | tf_op jit(solution)/shard_map/all_to_all | solution.py:354
  72.0 0.9 spread_gated.1
  72.9 3.5 %all-to-all-start.3 = ((bf16[8,256,128]{2,1,0:T(8,128)(2,1)}), bf16[8,256,128]{2,1,0:T(8,128)(2,1)S(1)}, u32[]{:S(2)}, u32[]{:S(2)}) async-start(bf16[8,256,128]{2,1,0:T(8,128)(2,1)} %spread_gated.1), calls=%async_computation.3 | async-start | bytes 1048576 | tf_op jit(solution)/shard_map/all_to_all | solution.py:357
  76.4 0.0 copy-start.3
  76.4 3.4 %copy-done.3 = bf16[8,128,4096]{2,1,0:T(8,128)(2,1)S(1)} copy-done((bf16[8,128,4096]{2,1,0:T(8,128)(2,1)S(1)}, bf16[8,128,4096]{2,1,0:T(8,128)(2,1)}, u32[]{:S(2)}) %copy-start.3) | copy-done | bytes 8388632
  79.8 5.1 %adjoint_sum.1 = bf16[16,48,128]{2,1,0:T(8,128)(2,1)} custom-call(f32[8]{0:T(128)S(1)} %dynamic_slice.3.skip_ref, bf16[32,32,128]{2,1,0:T(8,128)(2,1)S(1)} %all-to-all-done.given_ref, bf16[32,16,128]{2,1,0:T(8,128)(2,1)S(1)} %all_to_all.25.back_ref.middle_ref, f32[8,32,128]{2,1,0:T(8,128)S(1)} %get-tuple-element.16.inner_ref, bf16[8,128,4096]{2,1,0:T(8,128)(2,1)S(1)} %copy-done.3), custom_call_target="tpu_custom_call" | custom-call | flops 2147483648 | bytes 4194304 | tf_op jit(solution)/shard_map/adjoint_sum/pallas_call | solution.py:327
  84.8 9.4 %all-to-all-done.3.gated_ref = bf16[8,256,128]{2,1,0:T(8,128)(2,1)S(1)} async-done(((bf16[8,256,128]{2,1,0:T(8,128)(2,1)}), bf16[8,256,128]{2,1,0:T(8,128)(2,1)S(1)}, u32[]{:S(2)}, u32[]{:S(2)}) %all-to-all-start.3) | async-done | bytes 524320 | tf_op jit(solution)/shard_map/all_to_all | solution.py:357
  94.3 3.0 %collective-permute-start.1 = (bf16[8,256,128]{2,1,0:T(8,128)(2,1)S(1)}, bf16[8,256,128]{2,1,0:T(8,128)(2,1)S(1)}, u32[]{:S(2)}, u32[]{:S(2)}) collective-permute-start(bf16[8,256,128]{2,1,0:T(8,128)(2,1)S(1)} %all-to-all-done.3.gated_ref), channel_id=1, source_target_pairs={{0,1},{1,0},{2,3},{3,2},{4,5},{5,4},{6,7},{7,6},{8,9},{9,8},{10,11... | collective-permute-start | bytes 1572872 | tf_op jit(solution)/shard_map/ppermute | solution.py:371
  97.3 4.3 %all-to-all-start.4 = ((bf16[32,24,128]{2,1,0:T(8,128)(2,1)}), bf16[32,24,128]{2,1,0:T(8,128)(2,1)S(1)}, u32[]{:S(2)}, u32[]{:S(2)}) async-start(bf16[32,24,128]{2,1,0:T(8,128)(2,1)} %bitcast.3), calls=%async_computation.4 | async-start | bytes 393216 | tf_op jit(solution)/shard_map/all_to_all | solution.py:354
  101.6 0.0 copy-start.1
  101.6 2.2 %copy-done.1 = bf16[4096,512]{1,0:T(8,128)(2,1)S(1)} copy-done((bf16[4096,512]{1,0:T(8,128)(2,1)S(1)}, bf16[4096,512]{1,0:T(8,128)(2,1)}, u32[]{:S(2)}) %copy-start.1) | copy-done | bytes 4194328
  103.8 0.6 output_early.1
  104.4 8.0 %collective-permute-done.1.gated_ref = bf16[8,256,128]{2,1,0:T(8,128)(2,1)S(1)} collective-permute-done((bf16[8,256,128]{2,1,0:T(8,128)(2,1)S(1)}, bf16[8,256,128]{2,1,0:T(8,128)(2,1)S(1)}, u32[]{:S(2)}, u32[]{:S(2)}) %collective-permute-start.1) | collective-permute-done | bytes 524320 | tf_op jit(solution)/shard_map/ppermute | solution.py:371
  112.4 1.1 output_late.1
  113.5 0.0 all-to-all-done.4
  113.5 0.7 unpack_grads.1
Async XLA Ops:
  0.6 18.2 %copy-start.4 = (bf16[128,512]{1,0:T(8,128)(2,1)S(1)}, bf16[128,512]{1,0:T(8,128)(2,1)}, u32[]{:S(2)}) copy-start(bf16[128,512]{1,0:T(8,128)(2,1)} %cotangent_ref.3) | copy-start | bytes 393220
  5.0 16.7 %collective-permute-start = (bf16[8,256,128]{2,1,0:T(8,128)(2,1)}, bf16[8,256,128]{2,1,0:T(8,128)(2,1)S(1)}, u32[]{:S(2)}, u32[]{:S(2)}) collective-permute-start(bf16[8,256,128]{2,1,0:T(8,128)(2,1)} %get-tuple-element.15), channel_id=1, source_target_pairs={{0,1},{1,0},{2,3},{3,2},{4,5},{5,4},{6,7},{7,6},{8,9},{9,8},{10,11... | collective-permute-start | bytes 1572872 | tf_op jit(solution)/shard_map/ppermute | solution.py:361
  10.5 19.7 %all-to-all-start = ((bf16[32,32,128]{2,1,0:T(8,128)(2,1)}), bf16[32,32,128]{2,1,0:T(8,128)(2,1)S(1)}, u32[]{:S(2)}, u32[]{:S(2)}) async-start(bf16[32,32,128]{2,1,0:T(8,128)(2,1)} %get-tuple-element.13), calls=%async_computation | async-start | bytes 524288 | tf_op jit(solution)/shard_map/all_to_all | solution.py:354
  18.8 2.2 %copy-start = (bf16[4096,512]{1,0:T(8,128)(2,1)S(1)}, bf16[4096,512]{1,0:T(8,128)(2,1)}, u32[]{:S(2)}) copy-start(bf16[4096,512]{1,0:T(8,128)(2,1)} %param.8) | copy-start | bytes 12582916
  21.0 19.3 %copy-start.5 = (f32[256]{0:T(256)S(1)}, f32[256]{0:T(256)}, u32[]{:S(2)}) copy-start(f32[256]{0:T(256)} %param.7) | copy-start | bytes 3076
  30.2 26.8 %all-to-all-start.1 = ((bf16[8,256,128]{2,1,0:T(8,128)(2,1)}), bf16[8,256,128]{2,1,0:T(8,128)(2,1)S(1)}, u32[]{:S(2)}, u32[]{:S(2)}) async-start(bf16[8,256,128]{2,1,0:T(8,128)(2,1)} %total_share.1), calls=%async_computation.1 | async-start | bytes 1048576 | tf_op jit(solution)/shard_map/all_to_all | solution.py:357
  45.1 3.2 %copy-start.2 = (bf16[8,128,4096]{2,1,0:T(8,128)(2,1)}, bf16[8,128,4096]{2,1,0:T(8,128)(2,1)S(1)}, u32[]{:S(2)}) copy-start(bf16[8,128,4096]{2,1,0:T(8,128)(2,1)S(1)} %get-tuple-element.17.toeplitz_ref) | copy-start | bytes 25165828
  72.9 21.4 %all-to-all-start.3 = ((bf16[8,256,128]{2,1,0:T(8,128)(2,1)}), bf16[8,256,128]{2,1,0:T(8,128)(2,1)S(1)}, u32[]{:S(2)}, u32[]{:S(2)}) async-start(bf16[8,256,128]{2,1,0:T(8,128)(2,1)} %spread_gated.1), calls=%async_computation.3 | async-start | bytes 1048576 | tf_op jit(solution)/shard_map/all_to_all | solution.py:357
  76.4 3.4 %copy-start.3 = (bf16[8,128,4096]{2,1,0:T(8,128)(2,1)S(1)}, bf16[8,128,4096]{2,1,0:T(8,128)(2,1)}, u32[]{:S(2)}) copy-start(bf16[8,128,4096]{2,1,0:T(8,128)(2,1)} %copy-done.2) | copy-start | bytes 25165828
  94.3 18.2 %collective-permute-start.1 = (bf16[8,256,128]{2,1,0:T(8,128)(2,1)S(1)}, bf16[8,256,128]{2,1,0:T(8,128)(2,1)S(1)}, u32[]{:S(2)}, u32[]{:S(2)}) collective-permute-start(bf16[8,256,128]{2,1,0:T(8,128)(2,1)S(1)} %all-to-all-done.3.gated_ref), channel_id=1, source_target_pairs={{0,1},{1,0},{2,3},{3,2},{4,5},{5,4},{6,7},{7,6},{8,9},{9,8},{10,11... | collective-permute-start | bytes 1572872 | tf_op jit(solution)/shard_map/ppermute | solution.py:371
  97.3 16.2 %all-to-all-start.4 = ((bf16[32,24,128]{2,1,0:T(8,128)(2,1)}), bf16[32,24,128]{2,1,0:T(8,128)(2,1)S(1)}, u32[]{:S(2)}, u32[]{:S(2)}) async-start(bf16[32,24,128]{2,1,0:T(8,128)(2,1)} %bitcast.3), calls=%async_computation.4 | async-start | bytes 393216 | tf_op jit(solution)/shard_map/all_to_all | solution.py:354
  101.6 2.2 %copy-start.1 = (bf16[4096,512]{1,0:T(8,128)(2,1)S(1)}, bf16[4096,512]{1,0:T(8,128)(2,1)}, u32[]{:S(2)}) copy-start(bf16[4096,512]{1,0:T(8,128)(2,1)} %param.8) | copy-start | bytes 12582916

commit v3 on v2

--- a/solution.py
+++ b/solution.py
@@ -10,16 +10,18 @@
 ROWS = (((0,), (0,)), ((), ()))
 VMEM_LIMIT = 8 << 20
 FIRST_LIMIT = 54 << 20
+FIRST_SUM = 7
+FIRST_GATED = 5
 VMEM = pl.BlockSpec(memory_space=pltpu.VMEM)
 HBM = pl.BlockSpec(memory_space=pltpu.HBM)
 SMEM = pl.BlockSpec(memory_space=pltpu.SMEM)
 
 
-def call(kernel, in_specs, out_shape, flops, scratch=(), name=None, limit=VMEM_LIMIT):
+def call(kernel, in_specs, out_shape, flops, scratch=(), name=None, limit=VMEM_LIMIT, out=VMEM):
     return pl.pallas_call(
         kernel,
         in_specs=in_specs,
-        out_specs=jax.tree.map(lambda _: VMEM, out_shape),
+        out_specs=jax.tree.map(lambda _: out, out_shape),
         out_shape=out_shape,
         scratch_shapes=list(scratch),
         compiler_params=pltpu.CompilerParams(vmem_limit_bytes=limit),
@@ -50,10 +52,14 @@
     )(half, weight, cotangent)
 
 
-def total_share(share, received):
+def total_share(share, received, first):
+    planes = share.shape[0]
+
     def kernel(share_ref, received_ref, out_ref):
-        total = share_ref[...] + received_ref[...].astype(jnp.float32)
-        out_ref[...] = total.astype(jnp.bfloat16)
+        for place in range(planes):
+            plane = (place + first) % planes
+            total = share_ref[plane] + received_ref[plane].astype(jnp.float32)
+            out_ref[place] = total.astype(jnp.bfloat16)
 
     return call(
         kernel,
@@ -64,7 +70,7 @@
     )(share, received)
 
 
-def project_half(half, gated, weight, before=None):
+def project_half(half, gated, weight, first, before=None):
     planes, rows, width = weight.shape[0], weight.shape[-2], weight.shape[-1]
     count = gated.shape[-1]
     result = jax.ShapeDtypeStruct((count, width), jnp.float32 if before is None else jnp.bfloat16)
@@ -76,7 +82,7 @@
         for plane in range(planes):
             total = total + lax.dot_general(
                 gated_ref[plane],
-                weight_ref[plane, half_ref[0]],
+                weight_ref[(plane + first) % planes, half_ref[0]],
                 ROWS,
                 preferred_element_type=jnp.float32,
             )
@@ -87,7 +93,10 @@
         total = before_ref[...]
         for plane in range(planes):
             total = total + lax.dot_general(
-                gated_ref[plane], weight_ref[plane], ROWS, preferred_element_type=jnp.float32
+                gated_ref[plane],
+                weight_ref[(plane + first) % planes],
+                ROWS,
+                preferred_element_type=jnp.float32,
             )
         out_ref[...] = total.astype(out_ref.dtype)
 
@@ -122,7 +131,10 @@
         cotangent_here,
         projected_here,
         filters_here,
+        share_here,
+        packed_here,
         arrived,
+        left,
     ):
         places = [
             (projected_ref, projected_here),
@@ -142,13 +154,21 @@
         copies[1].wait()
         parts = [projected_here[which].astype(jnp.float32) for which in range(3)]
         parts = [part.reshape(seq, per, count) for part in parts + [filters_here[...]]]
-        packed_ref[...] = jnp.concatenate(parts, axis=1).astype(jnp.bfloat16)
+        packed_here[...] = jnp.concatenate(parts, axis=1).astype(jnp.bfloat16)
+        leaving = [pltpu.make_async_copy(packed_here, packed_ref, left.at[planes])]
+        leaving[0].start()
         copies[2].wait()
         for plane in range(planes):
             copies[3 + plane].wait()
-            share_ref[plane] = lax.dot_general(
+            share_here[plane] = lax.dot_general(
                 weight_here[plane], cotangent_here[...], LANES, preferred_element_type=jnp.float32
             ).astype(jnp.bfloat16)
+            leaving.append(
+                pltpu.make_async_copy(share_here.at[plane], share_ref.at[plane], left.at[plane])
+            )
+            leaving[-1].start()
+        for copy in leaving:
+            copy.wait()
 
     return call(
         kernel,
@@ -163,10 +183,14 @@
             pltpu.VMEM(cotangent.shape, cotangent.dtype),
             pltpu.VMEM(projected.shape, projected.dtype),
             pltpu.VMEM(filters.shape, filters.dtype),
+            pltpu.VMEM((planes, rows, count), jnp.bfloat16),
+            pltpu.VMEM((seq, 4 * per, count), jnp.bfloat16),
             pltpu.SemaphoreType.DMA((planes + 3,)),
+            pltpu.SemaphoreType.DMA((planes + 1,)),
         ],
         "first_share",
         FIRST_LIMIT,
+        HBM,
     )(half, weight, cotangent, projected, filters)
 
 
@@ -196,18 +220,26 @@
     seq, rows, count = middle.shape
     per = rows // 2
 
-    def kernel(middle_ref, out_ref):
-        gated = middle_ref[...].astype(jnp.float32)[:, :per].reshape(seq * per, count)
-        gated = gated.astype(jnp.bfloat16)
-        for plane in range(planes):
-            out_ref[plane] = gated
+    def kernel(middle_ref, out_ref, gated, left):
+        there = middle_ref[...].astype(jnp.float32)[:, :per].reshape(seq * per, count)
+        gated[...] = there.astype(jnp.bfloat16)
+        copies = [
+            pltpu.make_async_copy(gated, out_ref.at[plane], left.at[plane])
+            for plane in range(planes)
+        ]
+        for copy in copies:
+            copy.start()
+        for copy in copies:
+            copy.wait()
 
     return call(
         kernel,
         [VMEM],
         jax.ShapeDtypeStruct((planes, seq * per, count), jnp.bfloat16),
         1 << 24,
-        name="spread_gated",
+        [pltpu.VMEM((seq * per, count), jnp.bfloat16), pltpu.SemaphoreType.DMA((planes,))],
+        "spread_gated",
+        out=HBM,
     )(middle)
 
 
@@ -227,6 +259,11 @@
         1 << 24,
         name="unpack_grads",
     )(grads)
+
+
+def turn(rows):
+    middle = rows.shape[0] // 2
+    return jnp.concatenate([rows[middle:], rows[:middle]], axis=0)
 
 
 def causal(given, skip):
@@ -243,7 +280,7 @@
         @pl.loop(0, per)
         def _(channel):
             def take(which):
-                return wide[pl.ds(which * per + channel, chunks, stride=rows), :]
+                return turn(wide[pl.ds(which * per + channel, chunks, stride=rows), :])
 
             query, mixed, taps = take(0), take(1) * take(2), take(3)
             shifted[pl.ds(chunks, chunks), :] = mixed
@@ -266,7 +303,7 @@
                 )
             inner = total + skip_ref[channel] * mixed
             inner_ref[channel] = inner
-            collected[pl.ds(channel, chunks, stride=per), :] = query * inner
+            collected[pl.ds(channel, chunks, stride=per), :] = turn(query * inner)
 
         gated_ref[...] = collected[...].astype(jnp.bfloat16).reshape(gated_ref.shape)
 
@@ -302,10 +339,10 @@
         @pl.loop(0, per)
         def _(channel):
             def take(which):
-                return wide[pl.ds(which * per + channel, chunks, stride=rows), :]
+                return turn(wide[pl.ds(which * per + channel, chunks, stride=rows), :])
 
             query, key_in, value = take(0), take(1), take(2)
-            grad_gated = grads[pl.ds(per + channel, chunks, stride=2 * per), :]
+            grad_gated = turn(grads[pl.ds(per + channel, chunks, stride=2 * per), :])
             grad_inner = grad_gated * query
             shifted[pl.ds(0, chunks), :] = grad_inner
             total = jnp.zeros((chunks, BLOCK), jnp.float32)
@@ -320,7 +357,7 @@
             grad_mixed = total + skip_ref[channel] * grad_inner
             results = (grad_gated * inner_ref[channel], grad_mixed * value, grad_mixed * key_in)
             for which, result in enumerate(results):
-                collected[pl.ds(which * per + channel, chunks, stride=3 * per), :] = result
+                collected[pl.ds(which * per + channel, chunks, stride=3 * per), :] = turn(result)
 
         out_ref[...] = collected[...].astype(jnp.bfloat16).reshape(out_ref.shape)
 
@@ -350,28 +387,31 @@
     along_z = [[2 * z + h for z in range(planes)] for h in range(2)]
     pairs = [(i, i ^ 1) for i in range(chan)]
 
+    along_seq = [[(place + seq // 2) % seq for place in range(seq)]]
+
     def exchange_seq(array):
-        return lax.all_to_all(array, "seq", 0, 0, tiled=True)
-
-    def exchange_z(array):
-        return lax.all_to_all(array, "chan", 0, 0, tiled=True, axis_index_groups=along_z)
+        return lax.all_to_all(array, "seq", 0, 0, tiled=True, axis_index_groups=along_seq)
+
+    def exchange_z(array, first=0):
+        groups = [group[first:] + group[:first] for group in along_z]
+        return lax.all_to_all(array, "chan", 0, 0, tiled=True, axis_index_groups=groups)
 
     weight = out_weight.reshape(planes, 2, channels, out_weight.shape[1])
     share_other, packed = first(other, weight, cotangent, projected, filters, seq)
     received = lax.ppermute(share_other, "chan", pairs)
     given = exchange_seq(packed)
     share_own = partial_half(own, weight, cotangent, jnp.float32)
-    skip_here = lax.dynamic_slice(skip, (lax.axis_index("seq") * per,), (per,))
+    skip_here = lax.dynamic_slice(skip, ((lax.axis_index("seq") + seq // 2) % seq * per,), (per,))
     gated, inner, toeplitz = causal(given, skip_here)
-    shares = exchange_z(total_share(share_own, received))
+    shares = exchange_z(total_share(share_own, received, FIRST_SUM), FIRST_SUM)
     middle = exchange_seq(pack_middle(gated, shares, seq))
-    gated_half = exchange_z(spread(middle, planes))
+    gated_half = exchange_z(spread(middle, planes), FIRST_GATED)
     grads_there = adjoint(given, middle, inner, toeplitz, skip_here)
     grads_there, gated_half = lax.optimization_barrier((grads_there, gated_half))
     gated_other = lax.ppermute(gated_half, "chan", pairs)
-    output, weight_other = project_half(own, gated_half, weight)
+    output, weight_other = project_half(own, gated_half, weight, FIRST_GATED)
     grads = exchange_seq(grads_there.reshape(seq, 3 * per, count))
-    output = project_half(other, gated_other, weight_other, output)
+    output = project_half(other, gated_other, weight_other, FIRST_GATED, output)
     grads, output = lax.optimization_barrier((grads, output))
     grads = unpack(grads.reshape(seq // 2, 6 * per, count), per)
     return output, grads

time: 115 us -> 107 us (0.930)
  waiting for transfers between devices: 33.7 us -> 13.7 us
  starting transfers between devices: 34.6 us -> 48.1 us
    all_to_all x4, starting transfers between devices: 26.1 us -> 40.2 us  [the longest x2 21.5 us: exchange_seq(): lax.all_to_all(array, 'seq', 0, 0, tiled=True, axis_index_groups=along_seq)]
    all_to_all x4, waiting for transfers between devices: 25.7 us -> 13.7 us  [the longest x2 7.17 us: exchange_z(): lax.all_to_all(array, 'chan', 0, 0, tiled=True, axis_index_groups=groups)]
    ppermute x1, waiting for transfers between devices: 7.98 us -> 0.01 us  [per_device(): gated_other = lax.ppermute(gated_half, 'chan', pairs)]
where the time goes in v3:
time: 107 us
  starting transfers between devices  48.1 us (45%)
  Pallas kernels  19.2 us (18%)
  blocking collectives  13.8 us (13%)
  waiting for transfers between devices  13.7 us (13%)
  local copies, waits for them, and re-layouts  11.1 us (10%)
    all_to_all x2, starting transfers between devices, exchange_seq(): lax.all_to_all(array, 'seq', 0, 0, tiled=True, axis_index_groups=along_seq)  21.5 us
    all_to_all x2, starting transfers between devices, exchange_z(): lax.all_to_all(array, 'chan', 0, 0, tiled=True, axis_index_groups=groups)  18.7 us
    all_to_all x1, blocking collectives, exchange_seq(): lax.all_to_all(array, 'seq', 0, 0, tiled=True, axis_index_groups=along_seq)  13.8 us
    unnamed x12, local copies, waits for them, and re-layouts  11 us
    all_to_all x2, waiting for transfers between devices, exchange_z(): lax.all_to_all(array, 'chan', 0, 0, tiled=True, axis_index_groups=groups)  7.17 us
    all_to_all x2, waiting for transfers between devices, exchange_seq(): lax.all_to_all(array, 'seq', 0, 0, tiled=True, axis_index_groups=along_seq)  6.51 us
    ppermute x1, starting transfers between devices, per_device(): received = lax.ppermute(share_other, 'chan', pairs)  5.48 us
    pallas_call x1, Pallas kernels, adjoint(): call(kernel, [SMEM, VMEM, VMEM, VMEM, VMEM], jax.ShapeDtypeStruct((chunks...  5.08 us
  transfers between devices with their start and end apart: 6, of which 4 were waited for; matrix products, arithmetic and copies ran while one was open for 0% of the time, Pallas kernels for 12%

profile of v3, /device:TPU:1, one launch (start us, length us, event | category | flops | bytes accessed | tf_op | source)
XLA Modules:
  0.0 106.6 jit_solution(9654291117374049912)
XLA Ops:
  0.6 0.0 copy-start.4
  0.6 4.3 %first_share.1 = (bf16[8,256,128]{2,1,0:T(8,128)(2,1)}, bf16[32,32,128]{2,1,0:T(8,128)(2,1)}) custom-call(s32[1]{0:T(128)} %bitcast.half_ref, bf16[8,2,256,512]{3,2,1,0:T(8,128)(2,1)} %bitcast.5, bf16[128,512]{1,0:T(8,128)(2,1)} %cotangent_ref.3, bf16[3,256,128]{2,1,0:T(8,128)(2,1)} %projected_ref.1, f32[256,128]{1,0:T(8,128)} %filters_ref.1), custom_call_target="tpu_custom_call" | custom-call | flops 268435456 | bytes 4194304 | tf_op jit(solution)/shard_map/first_share/pallas_call | solution.py:173
  4.9 5.5 %collective-permute-start = (bf16[8,256,128]{2,1,0:T(8,128)(2,1)}, bf16[8,256,128]{2,1,0:T(8,128)(2,1)S(1)}, u32[]{:S(2)}, u32[]{:S(2)}) collective-permute-start(bf16[8,256,128]{2,1,0:T(8,128)(2,1)} %get-tuple-element.15), channel_id=1, source_target_pairs={{0,1},{1,0},{2,3},{3,2},{4,5},{5,4},{6,7},{7,6},{8,9},{9,8},{10,11... | collective-permute-start | bytes 1572872 | tf_op jit(solution)/shard_map/ppermute | solution.py:401
  10.4 10.3 %all-to-all-start = ((bf16[32,32,128]{2,1,0:T(8,128)(2,1)}), bf16[32,32,128]{2,1,0:T(8,128)(2,1)S(1)}, u32[]{:S(2)}, u32[]{:S(2)}) async-start(bf16[32,32,128]{2,1,0:T(8,128)(2,1)} %get-tuple-element.13), calls=%async_computation | async-start | bytes 524288 | tf_op jit(solution)/shard_map/all_to_all | solution.py:393
  20.8 0.0 copy-done.4
  20.8 0.0 copy-start
  20.8 2.2 %copy-done = bf16[4096,512]{1,0:T(8,128)(2,1)S(1)} copy-done((bf16[4096,512]{1,0:T(8,128)(2,1)S(1)}, bf16[4096,512]{1,0:T(8,128)(2,1)}, u32[]{:S(2)}) %copy-start) | copy-done | bytes 4194328
  23.0 0.0 copy-start.5
  23.0 0.7 partial_grad_gated.1.share_ref
  23.7 0.0 collective-permute-done.received_ref
  23.7 0.9 total_share.1
  24.6 4.1 %all-to-all-done.given_ref = bf16[32,32,128]{2,1,0:T(8,128)(2,1)S(1)} async-done(((bf16[32,32,128]{2,1,0:T(8,128)(2,1)}), bf16[32,32,128]{2,1,0:T(8,128)(2,1)S(1)}, u32[]{:S(2)}, u32[]{:S(2)}) %all-to-all-start) | async-done | bytes 262176 | tf_op jit(solution)/shard_map/all_to_all | solution.py:393
  28.7 11.8 %all-to-all-start.1 = ((bf16[8,256,128]{2,1,0:T(8,128)(2,1)}), bf16[8,256,128]{2,1,0:T(8,128)(2,1)S(1)}, u32[]{:S(2)}, u32[]{:S(2)}) async-start(bf16[8,256,128]{2,1,0:T(8,128)(2,1)} %total_share.1), calls=%async_computation.1 | async-start | bytes 1048576 | tf_op jit(solution)/shard_map/all_to_all | solution.py:397
  40.5 0.0 copy-done.5
  40.5 0.1 dynamic_slice.3.skip_ref
  40.5 4.7 %causal_sum.1 = (bf16[16,16,128]{2,1,0:T(8,128)(2,1)S(1)}, f32[8,32,128]{2,1,0:T(8,128)S(1)}, bf16[8,128,4096]{2,1,0:T(8,128)(2,1)S(1)}) custom-call(f32[8]{0:T(128)S(1)} %dynamic_slice.3.skip_ref, bf16[32,32,128]{2,1,0:T(8,128)(2,1)S(1)} %all-to-all-done.given_ref), custom_call_target="tpu_custom_call" | custom-call | flops 2147483648 | bytes 4194304 | tf_op jit(solution)/shard_map/causal_sum/pallas_call | solution.py:310
  45.3 0.0 copy-start.2
  45.3 3.2 %copy-done.2 = bf16[8,128,4096]{2,1,0:T(8,128)(2,1)} copy-done((bf16[8,128,4096]{2,1,0:T(8,128)(2,1)}, bf16[8,128,4096]{2,1,0:T(8,128)(2,1)S(1)}, u32[]{:S(2)}) %copy-start.2) | copy-done | bytes 8388632
  48.5 5.2 %all-to-all-done.1.shares_ref = bf16[8,256,128]{2,1,0:T(8,128)(2,1)S(1)} async-done(((bf16[8,256,128]{2,1,0:T(8,128)(2,1)}), bf16[8,256,128]{2,1,0:T(8,128)(2,1)S(1)}, u32[]{:S(2)}, u32[]{:S(2)}) %all-to-all-start.1) | async-done | bytes 524320 | tf_op jit(solution)/shard_map/all_to_all | solution.py:397
  53.7 0.1 pack_middle.1
  53.7 13.8 %all_to_all.25.back_ref.middle_ref = bf16[32,16,128]{2,1,0:T(8,128)(2,1)S(1)} all-to-all(bf16[32,16,128]{2,1,0:T(8,128)(2,1)S(1)} %pack_middle.1), channel_id=1, replica_groups={{256,272,288,304,320,336,352,368,384,400,416,432,448,464,480,496,0,16,3..., dimensions={0} | all-to-all | bytes 262144 | tf_op jit(solution)/shard_map/all_to_all | solution.py:393
  67.5 0.9 spread_gated.1
  68.4 6.9 %all-to-all-start.3 = ((bf16[8,256,128]{2,1,0:T(8,128)(2,1)}), bf16[8,256,128]{2,1,0:T(8,128)(2,1)S(1)}, u32[]{:S(2)}, u32[]{:S(2)}) async-start(bf16[8,256,128]{2,1,0:T(8,128)(2,1)} %spread_gated.1), calls=%async_computation.3 | async-start | bytes 1048576 | tf_op jit(solution)/shard_map/all_to_all | solution.py:397
  75.4 0.0 copy-start.3
  75.4 3.4 %copy-done.3 = bf16[8,128,4096]{2,1,0:T(8,128)(2,1)S(1)} copy-done((bf16[8,128,4096]{2,1,0:T(8,128)(2,1)S(1)}, bf16[8,128,4096]{2,1,0:T(8,128)(2,1)}, u32[]{:S(2)}) %copy-start.3) | copy-done | bytes 8388632
  78.7 5.1 %adjoint_sum.1 = bf16[16,48,128]{2,1,0:T(8,128)(2,1)} custom-call(f32[8]{0:T(128)S(1)} %dynamic_slice.3.skip_ref, bf16[32,32,128]{2,1,0:T(8,128)(2,1)S(1)} %all-to-all-done.given_ref, bf16[32,16,128]{2,1,0:T(8,128)(2,1)S(1)} %all_to_all.25.back_ref.middle_ref, f32[8,32,128]{2,1,0:T(8,128)S(1)} %get-tuple-element.16.inner_ref, bf16[8,128,4096]{2,1,0:T(8,128)(2,1)S(1)} %copy-done.3), custom_call_target="tpu_custom_call" | custom-call | flops 2147483648 | bytes 4194304 | tf_op jit(solution)/shard_map/adjoint_sum/pallas_call | solution.py:364
  83.8 2.0 %all-to-all-done.3.gated_ref = bf16[8,256,128]{2,1,0:T(8,128)(2,1)S(1)} async-done(((bf16[8,256,128]{2,1,0:T(8,128)(2,1)}), bf16[8,256,128]{2,1,0:T(8,128)(2,1)S(1)}, u32[]{:S(2)}, u32[]{:S(2)}) %all-to-all-start.3) | async-done | bytes 524320 | tf_op jit(solution)/shard_map/all_to_all | solution.py:397
  85.8 2.5 %collective-permute-start.1 = (bf16[8,256,128]{2,1,0:T(8,128)(2,1)S(1)}, bf16[8,256,128]{2,1,0:T(8,128)(2,1)S(1)}, u32[]{:S(2)}, u32[]{:S(2)}) collective-permute-start(bf16[8,256,128]{2,1,0:T(8,128)(2,1)S(1)} %all-to-all-done.3.gated_ref), channel_id=1, source_target_pairs={{0,1},{1,0},{2,3},{3,2},{4,5},{5,4},{6,7},{7,6},{8,9},{9,8},{10,11... | collective-permute-start | bytes 1572872 | tf_op jit(solution)/shard_map/ppermute | solution.py:411
  88.3 11.1 %all-to-all-start.4 = ((bf16[32,24,128]{2,1,0:T(8,128)(2,1)}), bf16[32,24,128]{2,1,0:T(8,128)(2,1)S(1)}, u32[]{:S(2)}, u32[]{:S(2)}) async-start(bf16[32,24,128]{2,1,0:T(8,128)(2,1)} %bitcast.3), calls=%async_computation.4 | async-start | bytes 393216 | tf_op jit(solution)/shard_map/all_to_all | solution.py:393
  99.5 0.0 copy-start.1
  99.5 2.2 %copy-done.1 = bf16[4096,512]{1,0:T(8,128)(2,1)S(1)} copy-done((bf16[4096,512]{1,0:T(8,128)(2,1)S(1)}, bf16[4096,512]{1,0:T(8,128)(2,1)}, u32[]{:S(2)}) %copy-start.1) | copy-done | bytes 4194328
  101.6 0.6 output_early.1
  102.3 0.0 collective-permute-done.1.gated_ref
  102.3 1.1 %output_late.1 = bf16[128,512]{1,0:T(8,128)(2,1)} custom-call(bf16[8,256,128]{2,1,0:T(8,128)(2,1)S(1)} %collective-permute-done.1.gated_ref, bf16[8,256,512]{2,1,0:T(8,128)(2,1)S(1)} %get-tuple-element.20.weight_ref, f32[128,512]{1,0:T(8,128)S(1)} %get-tuple-element.21.before_ref), custom_call_target="tpu_custom_call" | custom-call | flops 268435456 | bytes 4194304 | tf_op jit(solution)/shard_map/output_late/pallas_call | solution.py:114
  103.4 2.4 %all-to-all-done.4 = bf16[32,24,128]{2,1,0:T(8,128)(2,1)S(1)} async-done(((bf16[32,24,128]{2,1,0:T(8,128)(2,1)}), bf16[32,24,128]{2,1,0:T(8,128)(2,1)S(1)}, u32[]{:S(2)}, u32[]{:S(2)}) %all-to-all-start.4) | async-done | bytes 196640 | tf_op jit(solution)/shard_map/all_to_all | solution.py:393
  105.9 0.7 unpack_grads.1
Async XLA Ops:
  0.6 20.1 %copy-start.4 = (bf16[128,512]{1,0:T(8,128)(2,1)S(1)}, bf16[128,512]{1,0:T(8,128)(2,1)}, u32[]{:S(2)}) copy-start(bf16[128,512]{1,0:T(8,128)(2,1)} %cotangent_ref.3) | copy-start | bytes 393220
  4.9 18.7 %collective-permute-start = (bf16[8,256,128]{2,1,0:T(8,128)(2,1)}, bf16[8,256,128]{2,1,0:T(8,128)(2,1)S(1)}, u32[]{:S(2)}, u32[]{:S(2)}) collective-permute-start(bf16[8,256,128]{2,1,0:T(8,128)(2,1)} %get-tuple-element.15), channel_id=1, source_target_pairs={{0,1},{1,0},{2,3},{3,2},{4,5},{5,4},{6,7},{7,6},{8,9},{9,8},{10,11... | collective-permute-start | bytes 1572872 | tf_op jit(solution)/shard_map/ppermute | solution.py:401
  10.4 18.3 %all-to-all-start = ((bf16[32,32,128]{2,1,0:T(8,128)(2,1)}), bf16[32,32,128]{2,1,0:T(8,128)(2,1)S(1)}, u32[]{:S(2)}, u32[]{:S(2)}) async-start(bf16[32,32,128]{2,1,0:T(8,128)(2,1)} %get-tuple-element.13), calls=%async_computation | async-start | bytes 524288 | tf_op jit(solution)/shard_map/all_to_all | solution.py:393
  20.8 2.2 %copy-start = (bf16[4096,512]{1,0:T(8,128)(2,1)S(1)}, bf16[4096,512]{1,0:T(8,128)(2,1)}, u32[]{:S(2)}) copy-start(bf16[4096,512]{1,0:T(8,128)(2,1)} %param.8) | copy-start | bytes 12582916
  23.0 17.5 %copy-start.5 = (f32[256]{0:T(256)S(1)}, f32[256]{0:T(256)}, u32[]{:S(2)}) copy-start(f32[256]{0:T(256)} %param.7) | copy-start | bytes 3076
  28.7 25.0 %all-to-all-start.1 = ((bf16[8,256,128]{2,1,0:T(8,128)(2,1)}), bf16[8,256,128]{2,1,0:T(8,128)(2,1)S(1)}, u32[]{:S(2)}, u32[]{:S(2)}) async-start(bf16[8,256,128]{2,1,0:T(8,128)(2,1)} %total_share.1), calls=%async_computation.1 | async-start | bytes 1048576 | tf_op jit(solution)/shard_map/all_to_all | solution.py:397
  45.3 3.2 %copy-start.2 = (bf16[8,128,4096]{2,1,0:T(8,128)(2,1)}, bf16[8,128,4096]{2,1,0:T(8,128)(2,1)S(1)}, u32[]{:S(2)}) copy-start(bf16[8,128,4096]{2,1,0:T(8,128)(2,1)S(1)} %get-tuple-element.17.toeplitz_ref) | copy-start | bytes 25165828
  68.4 17.4 %all-to-all-start.3 = ((bf16[8,256,128]{2,1,0:T(8,128)(2,1)}), bf16[8,256,128]{2,1,0:T(8,128)(2,1)S(1)}, u32[]{:S(2)}, u32[]{:S(2)}) async-start(bf16[8,256,128]{2,1,0:T(8,128)(2,1)} %spread_gated.1), calls=%async_computation.3 | async-start | bytes 1048576 | tf_op jit(solution)/shard_map/all_to_all | solution.py:397
  75.4 3.4 %copy-start.3 = (bf16[8,128,4096]{2,1,0:T(8,128)(2,1)S(1)}, bf16[8,128,4096]{2,1,0:T(8,128)(2,1)}, u32[]{:S(2)}) copy-start(bf16[8,128,4096]{2,1,0:T(8,128)(2,1)} %copy-done.2) | copy-start | bytes 25165828
  85.8 16.5 %collective-permute-start.1 = (bf16[8,256,128]{2,1,0:T(8,128)(2,1)S(1)}, bf16[8,256,128]{2,1,0:T(8,128)(2,1)S(1)}, u32[]{:S(2)}, u32[]{:S(2)}) collective-permute-start(bf16[8,256,128]{2,1,0:T(8,128)(2,1)S(1)} %all-to-all-done.3.gated_ref), channel_id=1, source_target_pairs={{0,1},{1,0},{2,3},{3,2},{4,5},{5,4},{6,7},{7,6},{8,9},{9,8},{10,11... | collective-permute-start | bytes 1572872 | tf_op jit(solution)/shard_map/ppermute | solution.py:411
  88.3 17.5 %all-to-all-start.4 = ((bf16[32,24,128]{2,1,0:T(8,128)(2,1)}), bf16[32,24,128]{2,1,0:T(8,128)(2,1)S(1)}, u32[]{:S(2)}, u32[]{:S(2)}) async-start(bf16[32,24,128]{2,1,0:T(8,128)(2,1)} %bitcast.3), calls=%async_computation.4 | async-start | bytes 393216 | tf_op jit(solution)/shard_map/all_to_all | solution.py:393
  99.5 2.2 %copy-start.1 = (bf16[4096,512]{1,0:T(8,128)(2,1)S(1)}, bf16[4096,512]{1,0:T(8,128)(2,1)}, u32[]{:S(2)}) copy-start(bf16[4096,512]{1,0:T(8,128)(2,1)} %param.8) | copy-start | bytes 12582916

commit v4 on v3

--- a/solution.py
+++ b/solution.py
@@ -12,6 +12,9 @@
 FIRST_LIMIT = 54 << 20
 FIRST_SUM = 7
 FIRST_GATED = 5
+FIRST_GIVEN = 18
+FIRST_MIDDLE = 18
+FIRST_BACK = 18
 VMEM = pl.BlockSpec(memory_space=pltpu.VMEM)
 HBM = pl.BlockSpec(memory_space=pltpu.HBM)
 SMEM = pl.BlockSpec(memory_space=pltpu.SMEM)
@@ -76,8 +79,16 @@
     result = jax.ShapeDtypeStruct((count, width), jnp.float32 if before is None else jnp.bfloat16)
 
     def early(half_ref, gated_ref, weight_ref, out_ref, kept_ref, moved):
-        copy = pltpu.make_async_copy(weight_ref.at[:, 1 - half_ref[0]], kept_ref, moved)
-        copy.start()
+        copies = [
+            pltpu.make_async_copy(
+                weight_ref.at[(plane + first) % planes, 1 - half_ref[0]],
+                kept_ref.at[plane],
+                moved.at[plane],
+            )
+            for plane in range(planes)
+        ]
+        for copy in copies:
+            copy.start()
         total = jnp.zeros((count, width), jnp.float32)
         for plane in range(planes):
             total = total + lax.dot_general(
@@ -87,17 +98,16 @@
                 preferred_element_type=jnp.float32,
             )
         out_ref[...] = total
-        copy.wait()
+        for copy in copies:
+            copy.wait()
 
     def late(gated_ref, weight_ref, before_ref, out_ref):
-        total = before_ref[...]
-        for plane in range(planes):
-            total = total + lax.dot_general(
-                gated_ref[plane],
-                weight_ref[(plane + first) % planes],
-                ROWS,
-                preferred_element_type=jnp.float32,
-            )
+        total = before_ref[...] + lax.dot_general(
+            gated_ref[...].reshape(planes * rows, count),
+            weight_ref[...].reshape(planes * rows, width),
+            ROWS,
+            preferred_element_type=jnp.float32,
+        )
         out_ref[...] = total.astype(out_ref.dtype)
 
     flops = 2 * planes * rows * width * count
@@ -108,7 +118,7 @@
             [SMEM, VMEM, VMEM],
             [result, kept],
             flops,
-            [pltpu.SemaphoreType.DMA],
+            [pltpu.SemaphoreType.DMA((planes,))],
             name="output_early",
         )(half, gated, weight)
     return call(late, [VMEM] * 3, result, flops, name="output_late")(gated, weight, before)
@@ -141,8 +151,10 @@
             (filters_ref, filters_here),
             (cotangent_ref, cotangent_here),
         ]
+        group = planes // 2
         places += [
-            (weight_ref.at[plane, half_ref[0]], weight_here.at[plane]) for plane in range(planes)
+            (weight_ref.at[pl.ds(start, group), half_ref[0]], weight_here.at[pl.ds(start, group)])
+            for start in (0, group)
         ]
         copies = [
             pltpu.make_async_copy(source, target, arrived.at[i])
@@ -155,16 +167,24 @@
         parts = [projected_here[which].astype(jnp.float32) for which in range(3)]
         parts = [part.reshape(seq, per, count) for part in parts + [filters_here[...]]]
         packed_here[...] = jnp.concatenate(parts, axis=1).astype(jnp.bfloat16)
-        leaving = [pltpu.make_async_copy(packed_here, packed_ref, left.at[planes])]
+        leaving = [pltpu.make_async_copy(packed_here, packed_ref, left.at[2])]
         leaving[0].start()
         copies[2].wait()
-        for plane in range(planes):
-            copies[3 + plane].wait()
-            share_here[plane] = lax.dot_general(
-                weight_here[plane], cotangent_here[...], LANES, preferred_element_type=jnp.float32
-            ).astype(jnp.bfloat16)
+        for place, start in enumerate((0, group)):
+            copies[3 + place].wait()
+            share = lax.dot_general(
+                weight_here[pl.ds(start, group)].reshape(group * rows, width),
+                cotangent_here[...],
+                LANES,
+                preferred_element_type=jnp.float32,
+            )
+            share_here[pl.ds(start, group)] = share.astype(jnp.bfloat16).reshape(group, rows, count)
             leaving.append(
-                pltpu.make_async_copy(share_here.at[plane], share_ref.at[plane], left.at[plane])
+                pltpu.make_async_copy(
+                    share_here.at[pl.ds(start, group)],
+                    share_ref.at[pl.ds(start, group)],
+                    left.at[place],
+                )
             )
             leaving[-1].start()
         for copy in leaving:
@@ -185,8 +205,8 @@
             pltpu.VMEM(filters.shape, filters.dtype),
             pltpu.VMEM((planes, rows, count), jnp.bfloat16),
             pltpu.VMEM((seq, 4 * per, count), jnp.bfloat16),
-            pltpu.SemaphoreType.DMA((planes + 3,)),
-            pltpu.SemaphoreType.DMA((planes + 1,)),
+            pltpu.SemaphoreType.DMA((5,)),
+            pltpu.SemaphoreType.DMA((3,)),
         ],
         "first_share",
         FIRST_LIMIT,
@@ -204,7 +224,7 @@
             total = total + shares_ref[plane].astype(jnp.float32)
         there = gated_ref[...].astype(jnp.float32).reshape(seq, per, count)
         out_ref[...] = jnp.concatenate(
-            [there, total.reshape(seq, per, count)], axis=1
+            [there, turn(total.reshape(seq, per, count), FIRST_MIDDLE - FIRST_GIVEN)], axis=1
         ).astype(jnp.bfloat16)
 
     return call(
@@ -221,8 +241,8 @@
     per = rows // 2
 
     def kernel(middle_ref, out_ref, gated, left):
-        there = middle_ref[...].astype(jnp.float32)[:, :per].reshape(seq * per, count)
-        gated[...] = there.astype(jnp.bfloat16)
+        there = turn(middle_ref[...].astype(jnp.float32)[:, :per], FIRST_GIVEN - FIRST_MIDDLE)
+        gated[...] = there.reshape(seq * per, count).astype(jnp.bfloat16)
         copies = [
             pltpu.make_async_copy(gated, out_ref.at[plane], left.at[plane])
             for plane in range(planes)
@@ -249,6 +269,7 @@
 
     def kernel(grads_ref, out_ref):
         there = grads_ref[...].astype(jnp.float32).reshape(seq, 3, per, count)
+        there = turn(there, FIRST_GIVEN - FIRST_BACK)
         for which in range(3):
             out_ref[which] = there[:, which].reshape(seq * per, count).astype(jnp.bfloat16)
 
@@ -261,9 +282,9 @@
     )(grads)
 
 
-def turn(rows):
-    middle = rows.shape[0] // 2
-    return jnp.concatenate([rows[middle:], rows[:middle]], axis=0)
+def turn(array, by):
+    by = by % array.shape[0]
+    return array if by == 0 else jnp.concatenate([array[by:], array[:by]], axis=0)
 
 
 def causal(given, skip):
@@ -280,7 +301,7 @@
         @pl.loop(0, per)
         def _(channel):
             def take(which):
-                return turn(wide[pl.ds(which * per + channel, chunks, stride=rows), :])
+                return turn(wide[pl.ds(which * per + channel, chunks, stride=rows), :], -FIRST_GIVEN)
 
             query, mixed, taps = take(0), take(1) * take(2), take(3)
             shifted[pl.ds(chunks, chunks), :] = mixed
@@ -303,7 +324,9 @@
                 )
             inner = total + skip_ref[channel] * mixed
             inner_ref[channel] = inner
-            collected[pl.ds(channel, chunks, stride=per), :] = turn(query * inner)
+            collected[pl.ds(channel, chunks, stride=per), :] = turn(
+                query * inner, FIRST_MIDDLE
+            )
 
         gated_ref[...] = collected[...].astype(jnp.bfloat16).reshape(gated_ref.shape)
 
@@ -339,10 +362,10 @@
         @pl.loop(0, per)
         def _(channel):
             def take(which):
-                return turn(wide[pl.ds(which * per + channel, chunks, stride=rows), :])
+                return turn(wide[pl.ds(which * per + channel, chunks, stride=rows), :], -FIRST_GIVEN)
 
             query, key_in, value = take(0), take(1), take(2)
-            grad_gated = turn(grads[pl.ds(per + channel, chunks, stride=2 * per), :])
+            grad_gated = turn(grads[pl.ds(per + channel, chunks, stride=2 * per), :], -FIRST_MIDDLE)
             grad_inner = grad_gated * query
             shifted[pl.ds(0, chunks), :] = grad_inner
             total = jnp.zeros((chunks, BLOCK), jnp.float32)
@@ -357,7 +380,9 @@
             grad_mixed = total + skip_ref[channel] * grad_inner
             results = (grad_gated * inner_ref[channel], grad_mixed * value, grad_mixed * key_in)
             for which, result in enumerate(results):
-                collected[pl.ds(which * per + channel, chunks, stride=3 * per), :] = turn(result)
+                collected[pl.ds(which * per + channel, chunks, stride=3 * per), :] = turn(
+                    result, FIRST_BACK
+                )
 
         out_ref[...] = collected[...].astype(jnp.bfloat16).reshape(out_ref.shape)
 
@@ -387,10 +412,9 @@
     along_z = [[2 * z + h for z in range(planes)] for h in range(2)]
     pairs = [(i, i ^ 1) for i in range(chan)]
 
-    along_seq = [[(place + seq // 2) % seq for place in range(seq)]]
-
-    def exchange_seq(array):
-        return lax.all_to_all(array, "seq", 0, 0, tiled=True, axis_index_groups=along_seq)
+    def exchange_seq(array, first):
+        groups = [[(place + first) % seq for place in range(seq)]]
+        return lax.all_to_all(array, "seq", 0, 0, tiled=True, axis_index_groups=groups)
 
     def exchange_z(array, first=0):
         groups = [group[first:] + group[:first] for group in along_z]
@@ -399,18 +423,18 @@
     weight = out_weight.reshape(planes, 2, channels, out_weight.shape[1])
     share_other, packed = first(other, weight, cotangent, projected, filters, seq)
     received = lax.ppermute(share_other, "chan", pairs)
-    given = exchange_seq(packed)
+    given = exchange_seq(packed, FIRST_GIVEN)
     share_own = partial_half(own, weight, cotangent, jnp.float32)
-    skip_here = lax.dynamic_slice(skip, ((lax.axis_index("seq") + seq // 2) % seq * per,), (per,))
+    skip_here = lax.dynamic_slice(skip, ((lax.axis_index("seq") - FIRST_GIVEN) % seq * per,), (per,))
     gated, inner, toeplitz = causal(given, skip_here)
     shares = exchange_z(total_share(share_own, received, FIRST_SUM), FIRST_SUM)
-    middle = exchange_seq(pack_middle(gated, shares, seq))
+    middle = exchange_seq(pack_middle(gated, shares, seq), FIRST_MIDDLE)
     gated_half = exchange_z(spread(middle, planes), FIRST_GATED)
     grads_there = adjoint(given, middle, inner, toeplitz, skip_here)
     grads_there, gated_half = lax.optimization_barrier((grads_there, gated_half))
     gated_other = lax.ppermute(gated_half, "chan", pairs)
     output, weight_other = project_half(own, gated_half, weight, FIRST_GATED)
-    grads = exchange_seq(grads_there.reshape(seq, 3 * per, count))
+    grads = exchange_seq(grads_there.reshape(seq, 3 * per, count), FIRST_BACK)
     output = project_half(other, gated_other, weight_other, FIRST_GATED, output)
     grads, output = lax.optimization_barrier((grads, output))
     grads = unpack(grads.reshape(seq // 2, 6 * per, count), per)

time: 107 us -> 106 us (level)
  waiting for transfers between devices: 13.7 us -> 12.2 us
    all_to_all x2, waiting for transfers between devices: 6.51 us -> 5.04 us  [exchange_seq(): lax.all_to_all(array, 'seq', 0, 0, tiled=True, axis_index_groups=groups)]
    ppermute x1, starting transfers between devices: 2.47 us -> 3.63 us  [per_device(): gated_other = lax.ppermute(gated_half, 'chan', pairs)]
  transfers between devices with their start and end apart: 6 -> 6, of which waited for: 4 -> 4; matrix products, arithmetic and copies ran while one was open for 0% -> 0% of each run, Pallas kernels for 12% -> 13%
where the time goes in v4:
time: 106 us; the launch traced here: 105 us
  starting transfers between devices  48.9 us (46%)
  Pallas kernels  18.7 us (18%)
  blocking collectives  13.8 us (13%)
  waiting for transfers between devices  12.2 us (12%)
  local copies, waits for them, and re-layouts  11.1 us (10%)
    all_to_all x2, starting transfers between devices, exchange_seq(): lax.all_to_all(array, 'seq', 0, 0, tiled=True, axis_index_groups=groups)  21.9 us
    all_to_all x2, starting transfers between devices, exchange_z(): lax.all_to_all(array, 'chan', 0, 0, tiled=True, axis_index_groups=groups)  17.8 us
    all_to_all x1, blocking collectives, exchange_seq(): lax.all_to_all(array, 'seq', 0, 0, tiled=True, axis_index_groups=groups)  13.8 us
    unnamed x12, local copies, waits for them, and re-layouts  11 us
    all_to_all x2, waiting for transfers between devices, exchange_z(): lax.all_to_all(array, 'chan', 0, 0, tiled=True, axis_index_groups=groups)  7.18 us
    ppermute x1, starting transfers between devices, per_device(): received = lax.ppermute(share_other, 'chan', pairs)  5.48 us
    pallas_call x1, Pallas kernels, adjoint(): call(kernel, [SMEM, VMEM, VMEM, VMEM, VMEM], jax.ShapeDtypeStruct((chunks...  5.1 us
    all_to_all x2, waiting for transfers between devices, exchange_seq(): lax.all_to_all(array, 'seq', 0, 0, tiled=True, axis_index_groups=groups)  5.04 us
  transfers between devices with their start and end apart: 6, of which 4 were waited for; matrix products, arithmetic and copies ran while one was open for 0% of the time, Pallas kernels for 13%

profile of v4, /device:TPU:1, one launch (start us, length us, event | category | flops | bytes accessed | tf_op | source)
XLA Modules:
  0.0 105.4 jit_solution(10276900564171104762)
XLA Ops:
  0.6 0.0 copy-start.4
  0.6 3.6 %first_share.1 = (bf16[8,256,128]{2,1,0:T(8,128)(2,1)}, bf16[32,32,128]{2,1,0:T(8,128)(2,1)}) custom-call(s32[1]{0:T(128)} %bitcast.half_ref, bf16[8,2,256,512]{3,2,1,0:T(8,128)(2,1)} %bitcast.5, bf16[128,512]{1,0:T(8,128)(2,1)} %cotangent_ref.3, bf16[3,256,128]{2,1,0:T(8,128)(2,1)} %projected_ref.1, f32[256,128]{1,0:T(8,128)} %filters_ref.1), custom_call_target="tpu_custom_call" | custom-call | flops 268435456 | bytes 4194304 | tf_op jit(solution)/shard_map/first_share/pallas_call | solution.py:193
  4.3 5.5 %collective-permute-start = (bf16[8,256,128]{2,1,0:T(8,128)(2,1)}, bf16[8,256,128]{2,1,0:T(8,128)(2,1)S(1)}, u32[]{:S(2)}, u32[]{:S(2)}) collective-permute-start(bf16[8,256,128]{2,1,0:T(8,128)(2,1)} %get-tuple-element.15), channel_id=1, source_target_pairs={{0,1},{1,0},{2,3},{3,2},{4,5},{5,4},{6,7},{7,6},{8,9},{9,8},{10,11... | collective-permute-start | bytes 1572872 | tf_op jit(solution)/shard_map/ppermute | solution.py:425
  9.8 11.2 %all-to-all-start = ((bf16[32,32,128]{2,1,0:T(8,128)(2,1)}), bf16[32,32,128]{2,1,0:T(8,128)(2,1)S(1)}, u32[]{:S(2)}, u32[]{:S(2)}) async-start(bf16[32,32,128]{2,1,0:T(8,128)(2,1)} %get-tuple-element.13), calls=%async_computation | async-start | bytes 524288 | tf_op jit(solution)/shard_map/all_to_all | solution.py:417
  21.0 0.0 copy-done.4
  21.0 0.0 copy-start
  21.0 2.2 %copy-done = bf16[4096,512]{1,0:T(8,128)(2,1)S(1)} copy-done((bf16[4096,512]{1,0:T(8,128)(2,1)S(1)}, bf16[4096,512]{1,0:T(8,128)(2,1)}, u32[]{:S(2)}) %copy-start) | copy-done | bytes 4194328
  23.2 0.0 copy-start.5
  23.2 0.7 partial_grad_gated.1.share_ref
  23.9 0.0 collective-permute-done.received_ref
  23.9 0.9 total_share.1
  24.9 3.3 %all-to-all-done.given_ref = bf16[32,32,128]{2,1,0:T(8,128)(2,1)S(1)} async-done(((bf16[32,32,128]{2,1,0:T(8,128)(2,1)}), bf16[32,32,128]{2,1,0:T(8,128)(2,1)S(1)}, u32[]{:S(2)}, u32[]{:S(2)}) %all-to-all-start) | async-done | bytes 262176 | tf_op jit(solution)/shard_map/all_to_all | solution.py:417
  28.2 10.9 %all-to-all-start.1 = ((bf16[8,256,128]{2,1,0:T(8,128)(2,1)}), bf16[8,256,128]{2,1,0:T(8,128)(2,1)S(1)}, u32[]{:S(2)}, u32[]{:S(2)}) async-start(bf16[8,256,128]{2,1,0:T(8,128)(2,1)} %total_share.1), calls=%async_computation.1 | async-start | bytes 1048576 | tf_op jit(solution)/shard_map/all_to_all | solution.py:421
  39.1 0.0 copy-done.5
  39.1 0.1 dynamic_slice.3.skip_ref
  39.2 4.8 %causal_sum.1 = (bf16[16,16,128]{2,1,0:T(8,128)(2,1)S(1)}, f32[8,32,128]{2,1,0:T(8,128)S(1)}, bf16[8,128,4096]{2,1,0:T(8,128)(2,1)S(1)}) custom-call(f32[8]{0:T(128)S(1)} %dynamic_slice.3.skip_ref, bf16[32,32,128]{2,1,0:T(8,128)(2,1)S(1)} %all-to-all-done.given_ref), custom_call_target="tpu_custom_call" | custom-call | flops 2147483648 | bytes 4194304 | tf_op jit(solution)/shard_map/causal_sum/pallas_call | solution.py:333
  43.9 0.0 copy-start.2
  44.0 3.2 %copy-done.2 = bf16[8,128,4096]{2,1,0:T(8,128)(2,1)} copy-done((bf16[8,128,4096]{2,1,0:T(8,128)(2,1)}, bf16[8,128,4096]{2,1,0:T(8,128)(2,1)S(1)}, u32[]{:S(2)}) %copy-start.2) | copy-done | bytes 8388632
  47.2 5.2 %all-to-all-done.1.shares_ref = bf16[8,256,128]{2,1,0:T(8,128)(2,1)S(1)} async-done(((bf16[8,256,128]{2,1,0:T(8,128)(2,1)}), bf16[8,256,128]{2,1,0:T(8,128)(2,1)S(1)}, u32[]{:S(2)}, u32[]{:S(2)}) %all-to-all-start.1) | async-done | bytes 524320 | tf_op jit(solution)/shard_map/all_to_all | solution.py:421
  52.4 0.1 pack_middle.1
  52.5 13.8 %all_to_all.25.back_ref.middle_ref = bf16[32,16,128]{2,1,0:T(8,128)(2,1)S(1)} all-to-all(bf16[32,16,128]{2,1,0:T(8,128)(2,1)S(1)} %pack_middle.1), channel_id=1, replica_groups={{288,304,320,336,352,368,384,400,416,432,448,464,480,496,0,16,32,48,64,..., dimensions={0} | all-to-all | bytes 262144 | tf_op jit(solution)/shard_map/all_to_all | solution.py:417
  66.3 0.9 spread_gated.1
  67.2 6.9 %all-to-all-start.3 = ((bf16[8,256,128]{2,1,0:T(8,128)(2,1)}), bf16[8,256,128]{2,1,0:T(8,128)(2,1)S(1)}, u32[]{:S(2)}, u32[]{:S(2)}) async-start(bf16[8,256,128]{2,1,0:T(8,128)(2,1)} %spread_gated.1), calls=%async_computation.3 | async-start | bytes 1048576 | tf_op jit(solution)/shard_map/all_to_all | solution.py:421
  74.1 0.0 copy-start.3
  74.1 3.4 %copy-done.3 = bf16[8,128,4096]{2,1,0:T(8,128)(2,1)S(1)} copy-done((bf16[8,128,4096]{2,1,0:T(8,128)(2,1)S(1)}, bf16[8,128,4096]{2,1,0:T(8,128)(2,1)}, u32[]{:S(2)}) %copy-start.3) | copy-done | bytes 8388632
  77.5 5.1 %adjoint_sum.1 = bf16[16,48,128]{2,1,0:T(8,128)(2,1)} custom-call(f32[8]{0:T(128)S(1)} %dynamic_slice.3.skip_ref, bf16[32,32,128]{2,1,0:T(8,128)(2,1)S(1)} %all-to-all-done.given_ref, bf16[32,16,128]{2,1,0:T(8,128)(2,1)S(1)} %all_to_all.25.back_ref.middle_ref, f32[8,32,128]{2,1,0:T(8,128)S(1)} %get-tuple-element.16.inner_ref, bf16[8,128,4096]{2,1,0:T(8,128)(2,1)S(1)} %copy-done.3), custom_call_target="tpu_custom_call" | custom-call | flops 2147483648 | bytes 4194304 | tf_op jit(solution)/shard_map/adjoint_sum/pallas_call | solution.py:389
  82.6 2.0 %all-to-all-done.3.gated_ref = bf16[8,256,128]{2,1,0:T(8,128)(2,1)S(1)} async-done(((bf16[8,256,128]{2,1,0:T(8,128)(2,1)}), bf16[8,256,128]{2,1,0:T(8,128)(2,1)S(1)}, u32[]{:S(2)}, u32[]{:S(2)}) %all-to-all-start.3) | async-done | bytes 524320 | tf_op jit(solution)/shard_map/all_to_all | solution.py:421
  84.6 3.6 %collective-permute-start.1 = (bf16[8,256,128]{2,1,0:T(8,128)(2,1)S(1)}, bf16[8,256,128]{2,1,0:T(8,128)(2,1)S(1)}, u32[]{:S(2)}, u32[]{:S(2)}) collective-permute-start(bf16[8,256,128]{2,1,0:T(8,128)(2,1)S(1)} %all-to-all-done.3.gated_ref), channel_id=1, source_target_pairs={{0,1},{1,0},{2,3},{3,2},{4,5},{5,4},{6,7},{7,6},{8,9},{9,8},{10,11... | collective-permute-start | bytes 1572872 | tf_op jit(solution)/shard_map/ppermute | solution.py:435
  88.2 10.7 %all-to-all-start.4 = ((bf16[32,24,128]{2,1,0:T(8,128)(2,1)}), bf16[32,24,128]{2,1,0:T(8,128)(2,1)S(1)}, u32[]{:S(2)}, u32[]{:S(2)}) async-start(bf16[32,24,128]{2,1,0:T(8,128)(2,1)} %bitcast.3), calls=%async_computation.4 | async-start | bytes 393216 | tf_op jit(solution)/shard_map/all_to_all | solution.py:417
  98.9 0.0 copy-start.1
  98.9 2.2 %copy-done.1 = bf16[4096,512]{1,0:T(8,128)(2,1)S(1)} copy-done((bf16[4096,512]{1,0:T(8,128)(2,1)S(1)}, bf16[4096,512]{1,0:T(8,128)(2,1)}, u32[]{:S(2)}) %copy-start.1) | copy-done | bytes 4194328
  101.1 0.7 output_early.1
  101.8 0.0 collective-permute-done.1.gated_ref
  101.8 1.1 %output_late.1 = bf16[128,512]{1,0:T(8,128)(2,1)} custom-call(bf16[8,256,128]{2,1,0:T(8,128)(2,1)S(1)} %collective-permute-done.1.gated_ref, bf16[8,256,512]{2,1,0:T(8,128)(2,1)S(1)} %get-tuple-element.20.weight_ref, f32[128,512]{1,0:T(8,128)S(1)} %get-tuple-element.21.before_ref), custom_call_target="tpu_custom_call" | custom-call | flops 268435456 | bytes 4194304 | tf_op jit(solution)/shard_map/output_late/pallas_call | solution.py:124
  103.0 1.7 %all-to-all-done.4 = bf16[32,24,128]{2,1,0:T(8,128)(2,1)S(1)} async-done(((bf16[32,24,128]{2,1,0:T(8,128)(2,1)}), bf16[32,24,128]{2,1,0:T(8,128)(2,1)S(1)}, u32[]{:S(2)}, u32[]{:S(2)}) %all-to-all-start.4) | async-done | bytes 196640 | tf_op jit(solution)/shard_map/all_to_all | solution.py:417
  104.7 0.7 unpack_grads.1
Async XLA Ops:
  0.6 20.4 %copy-start.4 = (bf16[128,512]{1,0:T(8,128)(2,1)S(1)}, bf16[128,512]{1,0:T(8,128)(2,1)}, u32[]{:S(2)}) copy-start(bf16[128,512]{1,0:T(8,128)(2,1)} %cotangent_ref.3) | copy-start | bytes 393220
  4.3 19.6 %collective-permute-start = (bf16[8,256,128]{2,1,0:T(8,128)(2,1)}, bf16[8,256,128]{2,1,0:T(8,128)(2,1)S(1)}, u32[]{:S(2)}, u32[]{:S(2)}) collective-permute-start(bf16[8,256,128]{2,1,0:T(8,128)(2,1)} %get-tuple-element.15), channel_id=1, source_target_pairs={{0,1},{1,0},{2,3},{3,2},{4,5},{5,4},{6,7},{7,6},{8,9},{9,8},{10,11... | collective-permute-start | bytes 1572872 | tf_op jit(solution)/shard_map/ppermute | solution.py:425
  9.8 18.4 %all-to-all-start = ((bf16[32,32,128]{2,1,0:T(8,128)(2,1)}), bf16[32,32,128]{2,1,0:T(8,128)(2,1)S(1)}, u32[]{:S(2)}, u32[]{:S(2)}) async-start(bf16[32,32,128]{2,1,0:T(8,128)(2,1)} %get-tuple-element.13), calls=%async_computation | async-start | bytes 524288 | tf_op jit(solution)/shard_map/all_to_all | solution.py:417
  21.0 2.2 %copy-start = (bf16[4096,512]{1,0:T(8,128)(2,1)S(1)}, bf16[4096,512]{1,0:T(8,128)(2,1)}, u32[]{:S(2)}) copy-start(bf16[4096,512]{1,0:T(8,128)(2,1)} %param.8) | copy-start | bytes 12582916
  23.2 15.9 %copy-start.5 = (f32[256]{0:T(256)S(1)}, f32[256]{0:T(256)}, u32[]{:S(2)}) copy-start(f32[256]{0:T(256)} %param.7) | copy-start | bytes 3076
  28.2 24.2 %all-to-all-start.1 = ((bf16[8,256,128]{2,1,0:T(8,128)(2,1)}), bf16[8,256,128]{2,1,0:T(8,128)(2,1)S(1)}, u32[]{:S(2)}, u32[]{:S(2)}) async-start(bf16[8,256,128]{2,1,0:T(8,128)(2,1)} %total_share.1), calls=%async_computation.1 | async-start | bytes 1048576 | tf_op jit(solution)/shard_map/all_to_all | solution.py:421
  43.9 3.2 %copy-start.2 = (bf16[8,128,4096]{2,1,0:T(8,128)(2,1)}, bf16[8,128,4096]{2,1,0:T(8,128)(2,1)S(1)}, u32[]{:S(2)}) copy-start(bf16[8,128,4096]{2,1,0:T(8,128)(2,1)S(1)} %get-tuple-element.17.toeplitz_ref) | copy-start | bytes 25165828
  67.2 17.4 %all-to-all-start.3 = ((bf16[8,256,128]{2,1,0:T(8,128)(2,1)}), bf16[8,256,128]{2,1,0:T(8,128)(2,1)S(1)}, u32[]{:S(2)}, u32[]{:S(2)}) async-start(bf16[8,256,128]{2,1,0:T(8,128)(2,1)} %spread_gated.1), calls=%async_computation.3 | async-start | bytes 1048576 | tf_op jit(solution)/shard_map/all_to_all | solution.py:421
  74.1 3.4 %copy-start.3 = (bf16[8,128,4096]{2,1,0:T(8,128)(2,1)S(1)}, bf16[8,128,4096]{2,1,0:T(8,128)(2,1)}, u32[]{:S(2)}) copy-start(bf16[8,128,4096]{2,1,0:T(8,128)(2,1)} %copy-done.2) | copy-start | bytes 25165828
  84.6 17.2 %collective-permute-start.1 = (bf16[8,256,128]{2,1,0:T(8,128)(2,1)S(1)}, bf16[8,256,128]{2,1,0:T(8,128)(2,1)S(1)}, u32[]{:S(2)}, u32[]{:S(2)}) collective-permute-start(bf16[8,256,128]{2,1,0:T(8,128)(2,1)S(1)} %all-to-all-done.3.gated_ref), channel_id=1, source_target_pairs={{0,1},{1,0},{2,3},{3,2},{4,5},{5,4},{6,7},{7,6},{8,9},{9,8},{10,11... | collective-permute-start | bytes 1572872 | tf_op jit(solution)/shard_map/ppermute | solution.py:435
  88.2 16.5 %all-to-all-start.4 = ((bf16[32,24,128]{2,1,0:T(8,128)(2,1)}), bf16[32,24,128]{2,1,0:T(8,128)(2,1)S(1)}, u32[]{:S(2)}, u32[]{:S(2)}) async-start(bf16[32,24,128]{2,1,0:T(8,128)(2,1)} %bitcast.3), calls=%async_computation.4 | async-start | bytes 393216 | tf_op jit(solution)/shard_map/all_to_all | solution.py:417
  98.9 2.2 %copy-start.1 = (bf16[4096,512]{1,0:T(8,128)(2,1)S(1)}, bf16[4096,512]{1,0:T(8,128)(2,1)}, u32[]{:S(2)}) copy-start(bf16[4096,512]{1,0:T(8,128)(2,1)} %param.8) | copy-start | bytes 12582916

commit v5 on v4

--- a/solution.py
+++ b/solution.py
@@ -12,9 +12,7 @@
 FIRST_LIMIT = 54 << 20
 FIRST_SUM = 7
 FIRST_GATED = 5
-FIRST_GIVEN = 18
-FIRST_MIDDLE = 18
-FIRST_BACK = 18
+FIRST_SEQ = 18
 VMEM = pl.BlockSpec(memory_space=pltpu.VMEM)
 HBM = pl.BlockSpec(memory_space=pltpu.HBM)
 SMEM = pl.BlockSpec(memory_space=pltpu.SMEM)
@@ -147,7 +145,7 @@
         left,
     ):
         places = [
-            (projected_ref, projected_here),
+            (projected_ref.at[pl.ds(1, 2)], projected_here),
             (filters_ref, filters_here),
             (cotangent_ref, cotangent_here),
         ]
@@ -164,7 +162,7 @@
             copy.start()
         copies[0].wait()
         copies[1].wait()
-        parts = [projected_here[which].astype(jnp.float32) for which in range(3)]
+        parts = [projected_here[which].astype(jnp.float32) for which in range(2)]
         parts = [part.reshape(seq, per, count) for part in parts + [filters_here[...]]]
         packed_here[...] = jnp.concatenate(parts, axis=1).astype(jnp.bfloat16)
         leaving = [pltpu.make_async_copy(packed_here, packed_ref, left.at[2])]
@@ -195,16 +193,16 @@
         [SMEM, HBM, HBM, HBM, HBM],
         [
             jax.ShapeDtypeStruct((planes, rows, count), jnp.bfloat16),
-            jax.ShapeDtypeStruct((seq, 4 * per, count), jnp.bfloat16),
+            jax.ShapeDtypeStruct((seq, 3 * per, count), jnp.bfloat16),
         ],
         2 * planes * rows * width * count,
         [
             pltpu.VMEM((planes, rows, width), weight.dtype),
             pltpu.VMEM(cotangent.shape, cotangent.dtype),
-            pltpu.VMEM(projected.shape, projected.dtype),
+            pltpu.VMEM((2, channels, count), projected.dtype),
             pltpu.VMEM(filters.shape, filters.dtype),
             pltpu.VMEM((planes, rows, count), jnp.bfloat16),
-            pltpu.VMEM((seq, 4 * per, count), jnp.bfloat16),
+            pltpu.VMEM((seq, 3 * per, count), jnp.bfloat16),
             pltpu.SemaphoreType.DMA((5,)),
             pltpu.SemaphoreType.DMA((3,)),
         ],
@@ -214,35 +212,38 @@
     )(half, weight, cotangent, projected, filters)
 
 
-def pack_middle(gated, shares, seq):
+def pack_middle(inner, shares, projected, seq):
     planes, channels, count = shares.shape
     per = channels // seq
 
-    def kernel(gated_ref, shares_ref, out_ref):
+    def kernel(inner_ref, shares_ref, projected_ref, out_ref, total_ref):
         total = shares_ref[0].astype(jnp.float32)
         for plane in range(1, planes):
             total = total + shares_ref[plane].astype(jnp.float32)
-        there = gated_ref[...].astype(jnp.float32).reshape(seq, per, count)
-        out_ref[...] = jnp.concatenate(
-            [there, turn(total.reshape(seq, per, count), FIRST_MIDDLE - FIRST_GIVEN)], axis=1
-        ).astype(jnp.bfloat16)
-
-    return call(
-        kernel,
-        [VMEM, VMEM],
-        jax.ShapeDtypeStruct((seq, 2 * per, count), jnp.bfloat16),
+        total_ref[...] = total
+        back = (total * projected_ref[0].astype(jnp.float32)).reshape(seq, per, count)
+        there = inner_ref[...].astype(jnp.float32).reshape(seq, per, count)
+        out_ref[...] = jnp.concatenate([there, back], axis=1).astype(jnp.bfloat16)
+
+    return call(
+        kernel,
+        [VMEM, VMEM, VMEM],
+        [
+            jax.ShapeDtypeStruct((seq, 2 * per, count), jnp.bfloat16),
+            jax.ShapeDtypeStruct((channels, count), jnp.float32),
+        ],
         1 << 24,
         name="pack_middle",
-    )(gated, shares)
-
-
-def spread(middle, planes):
+    )(inner, shares, projected)
+
+
+def spread(middle, projected, planes):
     seq, rows, count = middle.shape
     per = rows // 2
 
-    def kernel(middle_ref, out_ref, gated, left):
-        there = turn(middle_ref[...].astype(jnp.float32)[:, :per], FIRST_GIVEN - FIRST_MIDDLE)
-        gated[...] = there.reshape(seq * per, count).astype(jnp.bfloat16)
+    def kernel(middle_ref, projected_ref, out_ref, gated, left):
+        inner = middle_ref[...].astype(jnp.float32)[:, :per].reshape(seq * per, count)
+        gated[...] = (projected_ref[0].astype(jnp.float32) * inner).astype(jnp.bfloat16)
         copies = [
             pltpu.make_async_copy(gated, out_ref.at[plane], left.at[plane])
             for plane in range(planes)
@@ -254,32 +255,33 @@
 
     return call(
         kernel,
-        [VMEM],
+        [VMEM, VMEM],
         jax.ShapeDtypeStruct((planes, seq * per, count), jnp.bfloat16),
         1 << 24,
         [pltpu.VMEM((seq * per, count), jnp.bfloat16), pltpu.SemaphoreType.DMA((planes,))],
         "spread_gated",
         out=HBM,
-    )(middle)
-
-
-def unpack(grads, per):
-    pairs, rows, count = grads.shape
-    seq = 2 * pairs
-
-    def kernel(grads_ref, out_ref):
-        there = grads_ref[...].astype(jnp.float32).reshape(seq, 3, per, count)
-        there = turn(there, FIRST_GIVEN - FIRST_BACK)
-        for which in range(3):
-            out_ref[which] = there[:, which].reshape(seq * per, count).astype(jnp.bfloat16)
-
-    return call(
-        kernel,
-        [VMEM],
+    )(middle, projected)
+
+
+def last_grads(grad_mixed, middle, grad_gated, projected):
+    seq, rows, count = middle.shape
+    per = rows // 2
+
+    def kernel(grad_mixed_ref, middle_ref, grad_gated_ref, projected_ref, out_ref):
+        inner = middle_ref[...].astype(jnp.float32)[:, :per].reshape(seq * per, count)
+        mixed = grad_mixed_ref[...].astype(jnp.float32).reshape(seq * per, count)
+        out_ref[0] = (grad_gated_ref[...] * inner).astype(jnp.bfloat16)
+        out_ref[1] = (mixed * projected_ref[2].astype(jnp.float32)).astype(jnp.bfloat16)
+        out_ref[2] = (mixed * projected_ref[1].astype(jnp.float32)).astype(jnp.bfloat16)
+
+    return call(
+        kernel,
+        [VMEM, VMEM, VMEM, VMEM],
         jax.ShapeDtypeStruct((3, seq * per, count), jnp.bfloat16),
         1 << 24,
-        name="unpack_grads",
-    )(grads)
+        name="last_grads",
+    )(grad_mixed, middle, grad_gated, projected)
 
 
 def turn(array, by):
@@ -289,11 +291,12 @@
 
 def causal(given, skip):
     chunks, rows, _ = given.shape
-    per = rows // 4
-
-    def kernel(skip_ref, given_ref, gated_ref, inner_ref, toeplitz_ref, wide, shifted, collected):
+    per = rows // 3
+
+    def kernel(skip_ref, given_ref, inner_ref, toeplitz_ref, wide, shifted, collected):
         wide[...] = given_ref[...].astype(jnp.float32).reshape(chunks * rows, BLOCK)
-        shifted[pl.ds(0, chunks), :] = jnp.zeros((chunks, BLOCK), jnp.float32)
+        for part in range(2):
+            shifted[part, pl.ds(0, chunks), :] = jnp.zeros((chunks, BLOCK), jnp.float32)
         upper = lax.broadcasted_iota(jnp.int32, (BLOCK, BLOCK), 1) >= lax.broadcasted_iota(
             jnp.int32, (BLOCK, BLOCK), 0
         )
@@ -301,12 +304,14 @@
         @pl.loop(0, per)
         def _(channel):
             def take(which):
-                return turn(wide[pl.ds(which * per + channel, chunks, stride=rows), :], -FIRST_GIVEN)
-
-            query, mixed, taps = take(0), take(1) * take(2), take(3)
-            shifted[pl.ds(chunks, chunks), :] = mixed
+                return turn(wide[pl.ds(which * per + channel, chunks, stride=rows), :], -FIRST_SEQ)
+
+            mixed, taps = take(0) * take(1), take(2)
+            near = mixed.astype(jnp.bfloat16).astype(jnp.float32)
+            shifted[0, pl.ds(chunks, chunks), :] = near
+            shifted[1, pl.ds(chunks, chunks), :] = mixed - near
             before = jnp.zeros((BLOCK, BLOCK), jnp.float32)
-            total = jnp.zeros((chunks, BLOCK), jnp.float32)
+            total = jnp.zeros((2 * chunks, BLOCK), jnp.float32)
             for lag in range(0, chunks, 2):
                 blocks, signals = [], []
                 for one in (lag, lag + 1):
@@ -316,57 +321,46 @@
                     before = turned
                     toeplitz_ref[channel, :, one * BLOCK : (one + 1) * BLOCK] = block
                     blocks.append(block)
-                    signals.append(shifted[chunks - one : 2 * chunks - one, :].astype(jnp.bfloat16))
+                    parts = [shifted[part, chunks - one : 2 * chunks - one, :] for part in range(2)]
+                    signals.append(jnp.concatenate(parts, axis=0).astype(jnp.bfloat16))
                 total = total + jnp.dot(
                     jnp.concatenate(signals, axis=1),
                     jnp.concatenate(blocks, axis=0),
                     preferred_element_type=jnp.float32,
                 )
-            inner = total + skip_ref[channel] * mixed
-            inner_ref[channel] = inner
-            collected[pl.ds(channel, chunks, stride=per), :] = turn(
-                query * inner, FIRST_MIDDLE
-            )
-
-        gated_ref[...] = collected[...].astype(jnp.bfloat16).reshape(gated_ref.shape)
+            inner = total[:chunks] + total[chunks:] + skip_ref[channel] * mixed
+            collected[pl.ds(channel, chunks, stride=per), :] = turn(inner, FIRST_SEQ)
+
+        inner_ref[...] = collected[...].astype(jnp.bfloat16).reshape(inner_ref.shape)
 
     return call(
         kernel,
         [SMEM, VMEM],
         [
             jax.ShapeDtypeStruct((chunks // 2, 2 * per, BLOCK), jnp.bfloat16),
-            jax.ShapeDtypeStruct((per, chunks, BLOCK), jnp.float32),
             jax.ShapeDtypeStruct((per, BLOCK, chunks * BLOCK), jnp.bfloat16),
         ],
         16 * per * chunks * chunks * BLOCK * BLOCK,
         [
             pltpu.VMEM((chunks * rows, BLOCK), jnp.float32),
-            pltpu.VMEM((2 * chunks, BLOCK), jnp.float32),
+            pltpu.VMEM((2, 2 * chunks, BLOCK), jnp.float32),
             pltpu.VMEM((chunks * per, BLOCK), jnp.float32),
         ],
         "causal_sum",
     )(skip, given)
 
 
-def adjoint(given, back, inner, toeplitz, skip):
-    chunks, rows, _ = given.shape
-    per = rows // 4
-
-    def kernel(
-        skip_ref, given_ref, back_ref, inner_ref, toeplitz_ref, out_ref, wide, grads, shifted, collected
-    ):
-        wide[...] = given_ref[...].astype(jnp.float32).reshape(chunks * rows, BLOCK)
-        grads[...] = back_ref[...].astype(jnp.float32).reshape(chunks * 2 * per, BLOCK)
+def adjoint(back, toeplitz, skip):
+    chunks, rows, _ = back.shape
+    per = rows // 2
+
+    def kernel(skip_ref, back_ref, toeplitz_ref, out_ref, grads, shifted, collected):
+        grads[...] = back_ref[...].astype(jnp.float32).reshape(chunks * rows, BLOCK)
         shifted[pl.ds(chunks, chunks), :] = jnp.zeros((chunks, BLOCK), jnp.float32)
 
         @pl.loop(0, per)
         def _(channel):
-            def take(which):
-                return turn(wide[pl.ds(which * per + channel, chunks, stride=rows), :], -FIRST_GIVEN)
-
-            query, key_in, value = take(0), take(1), take(2)
-            grad_gated = turn(grads[pl.ds(per + channel, chunks, stride=2 * per), :], -FIRST_MIDDLE)
-            grad_inner = grad_gated * query
+            grad_inner = turn(grads[pl.ds(per + channel, chunks, stride=rows), :], -FIRST_SEQ)
             shifted[pl.ds(0, chunks), :] = grad_inner
             total = jnp.zeros((chunks, BLOCK), jnp.float32)
             for lag in range(0, chunks, 2):
@@ -378,27 +372,22 @@
                     preferred_element_type=jnp.float32,
                 )
             grad_mixed = total + skip_ref[channel] * grad_inner
-            results = (grad_gated * inner_ref[channel], grad_mixed * value, grad_mixed * key_in)
-            for which, result in enumerate(results):
-                collected[pl.ds(which * per + channel, chunks, stride=3 * per), :] = turn(
-                    result, FIRST_BACK
-                )
+            collected[pl.ds(channel, chunks, stride=per), :] = turn(grad_mixed, FIRST_SEQ)
 
         out_ref[...] = collected[...].astype(jnp.bfloat16).reshape(out_ref.shape)
 
     return call(
         kernel,
-        [SMEM, VMEM, VMEM, VMEM, VMEM],
-        jax.ShapeDtypeStruct((chunks // 2, 6 * per, BLOCK), jnp.bfloat16),
+        [SMEM, VMEM, VMEM],
+        jax.ShapeDtypeStruct((chunks // 2, 2 * per, BLOCK), jnp.bfloat16),
         16 * per * chunks * chunks * BLOCK * BLOCK,
         [
             pltpu.VMEM((chunks * rows, BLOCK), jnp.float32),
-            pltpu.VMEM((chunks * 2 * per, BLOCK), jnp.float32),
             pltpu.VMEM((2 * chunks, BLOCK), jnp.float32),
-            pltpu.VMEM((chunks * 3 * per, BLOCK), jnp.float32),
+            pltpu.VMEM((chunks * per, BLOCK), jnp.float32),
         ],
         "adjoint_sum",
-    )(skip, given, back, inner, toeplitz)
+    )(skip, back, toeplitz)
 
 
 def per_device(projected, filters, skip, out_weight, cotangent):
@@ -412,8 +401,8 @@
     along_z = [[2 * z + h for z in range(planes)] for h in range(2)]
     pairs = [(i, i ^ 1) for i in range(chan)]
 
-    def exchange_seq(array, first):
-        groups = [[(place + first) % seq for place in range(seq)]]
+    def exchange_seq(array):
+        groups = [[(place + FIRST_SEQ) % seq for place in range(seq)]]
         return lax.all_to_all(array, "seq", 0, 0, tiled=True, axis_index_groups=groups)
 
     def exchange_z(array, first=0):
@@ -423,21 +412,22 @@
     weight = out_weight.reshape(planes, 2, channels, out_weight.shape[1])
     share_other, packed = first(other, weight, cotangent, projected, filters, seq)
     received = lax.ppermute(share_other, "chan", pairs)
-    given = exchange_seq(packed, FIRST_GIVEN)
+    given = exchange_seq(packed)
     share_own = partial_half(own, weight, cotangent, jnp.float32)
-    skip_here = lax.dynamic_slice(skip, ((lax.axis_index("seq") - FIRST_GIVEN) % seq * per,), (per,))
-    gated, inner, toeplitz = causal(given, skip_here)
+    skip_here = lax.dynamic_slice(skip, ((lax.axis_index("seq") - FIRST_SEQ) % seq * per,), (per,))
+    inner, toeplitz = causal(given, skip_here)
     shares = exchange_z(total_share(share_own, received, FIRST_SUM), FIRST_SUM)
-    middle = exchange_seq(pack_middle(gated, shares, seq), FIRST_MIDDLE)
-    gated_half = exchange_z(spread(middle, planes), FIRST_GATED)
-    grads_there = adjoint(given, middle, inner, toeplitz, skip_here)
+    packed, grad_gated = pack_middle(inner, shares, projected, seq)
+    middle = exchange_seq(packed)
+    gated_half = exchange_z(spread(middle, projected, planes), FIRST_GATED)
+    grads_there = adjoint(middle, toeplitz, skip_here)
     grads_there, gated_half = lax.optimization_barrier((grads_there, gated_half))
     gated_other = lax.ppermute(gated_half, "chan", pairs)
     output, weight_other = project_half(own, gated_half, weight, FIRST_GATED)
-    grads = exchange_seq(grads_there.reshape(seq, 3 * per, count), FIRST_BACK)
+    grads = exchange_seq(grads_there.reshape(seq, per, count))
     output = project_half(other, gated_other, weight_other, FIRST_GATED, output)
     grads, output = lax.optimization_barrier((grads, output))
-    grads = unpack(grads.reshape(seq // 2, 6 * per, count), per)
+    grads = last_grads(grads.reshape(seq // 2, 2 * per, count), middle, grad_gated, projected)
     return output, grads
 
 

time: 106 us -> 104 us (0.981)
  waiting for transfers between devices: 12.2 us -> 8.53 us
    all_to_all x2, waiting for transfers between devices: 5.04 us -> 1.91 us  [exchange_seq(): lax.all_to_all(array, 'seq', 0, 0, tiled=True, axis_index_groups=groups)]
    unnamed x12 -> x14, local copies, waits for them, and re-layouts: 11 us -> 11 us
  transfers between devices with their start and end apart: 6 -> 6, of which waited for: 4 -> 3; matrix products, arithmetic and copies ran while one was open for 0% -> 0% of each run, Pallas kernels for 13% -> 13%
where the time goes in v5:
time: 104 us; the launch traced here: 103 us
  starting transfers between devices  49.5 us (48%)
  Pallas kernels  18.9 us (18%)
  blocking collectives  14.2 us (14%)
  local copies, waits for them, and re-layouts  11.1 us (11%)
  waiting for transfers between devices  8.53 us (8%)
    all_to_all x2, starting transfers between devices, exchange_seq(): lax.all_to_all(array, 'seq', 0, 0, tiled=True, axis_index_groups=groups)  22.3 us
    all_to_all x2, starting transfers between devices, exchange_z(): lax.all_to_all(array, 'chan', 0, 0, tiled=True, axis_index_groups=groups)  17.9 us
    all_to_all x1, blocking collectives, exchange_seq(): lax.all_to_all(array, 'seq', 0, 0, tiled=True, axis_index_groups=groups)  14.2 us
    unnamed x14, local copies, waits for them, and re-layouts  11 us
    all_to_all x2, waiting for transfers between devices, exchange_z(): lax.all_to_all(array, 'chan', 0, 0, tiled=True, axis_index_groups=groups)  6.62 us
    ppermute x1, starting transfers between devices, per_device(): received = lax.ppermute(share_other, 'chan', pairs)  5.48 us
    pallas_call x1, Pallas kernels, causal(): call(kernel, [SMEM, VMEM], [jax.ShapeDtypeStruct((chunks // 2, 2 * per, B...  5.08 us
    pallas_call x1, Pallas kernels, adjoint(): call(kernel, [SMEM, VMEM, VMEM], jax.ShapeDtypeStruct((chunks // 2, 2 * p...  4.95 us
  transfers between devices with their start and end apart: 6, of which 3 were waited for; matrix products, arithmetic and copies ran while one was open for 0% of the time, Pallas kernels for 13%

profile of v5, /device:TPU:1, one launch (start us, length us, event | category | flops | bytes accessed | tf_op | source)
XLA Modules:
  0.0 103.0 jit_solution(3567994180708123688)
XLA Ops:
  0.6 0.0 copy-start.5
  0.6 3.6 %first_share.1 = (bf16[8,256,128]{2,1,0:T(8,128)(2,1)}, bf16[32,24,128]{2,1,0:T(8,128)(2,1)}) custom-call(s32[1]{0:T(128)} %bitcast.half_ref, bf16[8,2,256,512]{3,2,1,0:T(8,128)(2,1)} %bitcast.5, bf16[128,512]{1,0:T(8,128)(2,1)} %cotangent_ref.3, bf16[3,256,128]{2,1,0:T(8,128)(2,1)} %projected_ref.7, f32[256,128]{1,0:T(8,128)} %filters_ref.1), custom_call_target="tpu_custom_call" | custom-call | flops 268435456 | bytes 4194304 | tf_op jit(solution)/shard_map/first_share/pallas_call | solution.py:191
  4.3 5.5 %collective-permute-start = (bf16[8,256,128]{2,1,0:T(8,128)(2,1)}, bf16[8,256,128]{2,1,0:T(8,128)(2,1)S(1)}, u32[]{:S(2)}, u32[]{:S(2)}) collective-permute-start(bf16[8,256,128]{2,1,0:T(8,128)(2,1)} %get-tuple-element.16), channel_id=1, source_target_pairs={{0,1},{1,0},{2,3},{3,2},{4,5},{5,4},{6,7},{7,6},{8,9},{9,8},{10,11... | collective-permute-start | bytes 1572872 | tf_op jit(solution)/shard_map/ppermute | solution.py:414
  9.7 11.2 %all-to-all-start = ((bf16[32,24,128]{2,1,0:T(8,128)(2,1)}), bf16[32,24,128]{2,1,0:T(8,128)(2,1)S(1)}, u32[]{:S(2)}, u32[]{:S(2)}) async-start(bf16[32,24,128]{2,1,0:T(8,128)(2,1)} %get-tuple-element.14), calls=%async_computation | async-start | bytes 393216 | tf_op jit(solution)/shard_map/all_to_all | solution.py:406
  21.0 0.0 copy-done.5
  21.0 0.0 copy-start
  21.0 2.2 %copy-done = bf16[4096,512]{1,0:T(8,128)(2,1)S(1)} copy-done((bf16[4096,512]{1,0:T(8,128)(2,1)S(1)}, bf16[4096,512]{1,0:T(8,128)(2,1)}, u32[]{:S(2)}) %copy-start) | copy-done | bytes 4194328
  23.2 0.0 copy-start.6
  23.2 0.7 partial_grad_gated.1.share_ref
  23.9 0.0 collective-permute-done.received_ref
  23.9 0.9 total_share.1
  24.9 1.9 %all-to-all-done.given_ref = bf16[32,24,128]{2,1,0:T(8,128)(2,1)S(1)} async-done(((bf16[32,24,128]{2,1,0:T(8,128)(2,1)}), bf16[32,24,128]{2,1,0:T(8,128)(2,1)S(1)}, u32[]{:S(2)}, u32[]{:S(2)}) %all-to-all-start) | async-done | bytes 196640 | tf_op jit(solution)/shard_map/all_to_all | solution.py:406
  26.8 10.9 %all-to-all-start.1 = ((bf16[8,256,128]{2,1,0:T(8,128)(2,1)}), bf16[8,256,128]{2,1,0:T(8,128)(2,1)S(1)}, u32[]{:S(2)}, u32[]{:S(2)}) async-start(bf16[8,256,128]{2,1,0:T(8,128)(2,1)} %total_share.1), calls=%async_computation.1 | async-start | bytes 1048576 | tf_op jit(solution)/shard_map/all_to_all | solution.py:410
  37.7 0.0 copy-start.4
  37.7 0.0 copy-done.6
  37.7 0.1 dynamic_slice.3.skip_ref
  37.7 5.1 %causal_sum.1 = (bf16[16,16,128]{2,1,0:T(8,128)(2,1)S(1)}, bf16[8,128,4096]{2,1,0:T(8,128)(2,1)S(1)}) custom-call(f32[8]{0:T(128)S(1)} %dynamic_slice.3.skip_ref, bf16[32,24,128]{2,1,0:T(8,128)(2,1)S(1)} %all-to-all-done.given_ref), custom_call_target="tpu_custom_call" | custom-call | flops 2147483648 | bytes 4194304 | tf_op jit(solution)/shard_map/causal_sum/pallas_call | solution.py:336
  42.8 0.0 copy-start.2
  42.8 3.2 %copy-done.2 = bf16[8,128,4096]{2,1,0:T(8,128)(2,1)} copy-done((bf16[8,128,4096]{2,1,0:T(8,128)(2,1)}, bf16[8,128,4096]{2,1,0:T(8,128)(2,1)S(1)}, u32[]{:S(2)}) %copy-start.2) | copy-done | bytes 8388632
  46.1 4.8 %all-to-all-done.1.shares_ref = bf16[8,256,128]{2,1,0:T(8,128)(2,1)S(1)} async-done(((bf16[8,256,128]{2,1,0:T(8,128)(2,1)}), bf16[8,256,128]{2,1,0:T(8,128)(2,1)S(1)}, u32[]{:S(2)}, u32[]{:S(2)}) %all-to-all-start.1) | async-done | bytes 524320 | tf_op jit(solution)/shard_map/all_to_all | solution.py:410
  50.8 0.0 copy-done.4
  50.8 0.1 pack_middle.1
  50.9 14.2 %all_to_all.25.back_ref.middle_ref = bf16[32,16,128]{2,1,0:T(8,128)(2,1)S(1)} all-to-all(bf16[32,16,128]{2,1,0:T(8,128)(2,1)S(1)} %get-tuple-element.17), channel_id=1, replica_groups={{288,304,320,336,352,368,384,400,416,432,448,464,480,496,0,16,32,48,64,..., dimensions={0} | all-to-all | bytes 262144 | tf_op jit(solution)/shard_map/all_to_all | solution.py:406
  65.2 0.9 spread_gated.1
  66.1 7.0 %all-to-all-start.3 = ((bf16[8,256,128]{2,1,0:T(8,128)(2,1)}), bf16[8,256,128]{2,1,0:T(8,128)(2,1)S(1)}, u32[]{:S(2)}, u32[]{:S(2)}) async-start(bf16[8,256,128]{2,1,0:T(8,128)(2,1)} %spread_gated.1), calls=%async_computation.3 | async-start | bytes 1048576 | tf_op jit(solution)/shard_map/all_to_all | solution.py:410
  73.2 0.0 copy-start.3
  73.2 3.4 %copy-done.3 = bf16[8,128,4096]{2,1,0:T(8,128)(2,1)S(1)} copy-done((bf16[8,128,4096]{2,1,0:T(8,128)(2,1)S(1)}, bf16[8,128,4096]{2,1,0:T(8,128)(2,1)}, u32[]{:S(2)}) %copy-start.3) | copy-done | bytes 8388632
  76.6 5.0 %adjoint_sum.1 = bf16[16,16,128]{2,1,0:T(8,128)(2,1)} custom-call(f32[8]{0:T(128)S(1)} %dynamic_slice.3.skip_ref, bf16[32,16,128]{2,1,0:T(8,128)(2,1)S(1)} %all_to_all.25.back_ref.middle_ref, bf16[8,128,4096]{2,1,0:T(8,128)(2,1)S(1)} %copy-done.3), custom_call_target="tpu_custom_call" | custom-call | flops 2147483648 | bytes 4194304 | tf_op jit(solution)/shard_map/adjoint_sum/pallas_call | solution.py:379
  81.5 1.8 %all-to-all-done.3.gated_ref = bf16[8,256,128]{2,1,0:T(8,128)(2,1)S(1)} async-done(((bf16[8,256,128]{2,1,0:T(8,128)(2,1)}), bf16[8,256,128]{2,1,0:T(8,128)(2,1)S(1)}, u32[]{:S(2)}, u32[]{:S(2)}) %all-to-all-start.3) | async-done | bytes 524320 | tf_op jit(solution)/shard_map/all_to_all | solution.py:410
  83.3 3.8 %collective-permute-start.1 = (bf16[8,256,128]{2,1,0:T(8,128)(2,1)S(1)}, bf16[8,256,128]{2,1,0:T(8,128)(2,1)S(1)}, u32[]{:S(2)}, u32[]{:S(2)}) collective-permute-start(bf16[8,256,128]{2,1,0:T(8,128)(2,1)S(1)} %all-to-all-done.3.gated_ref), channel_id=1, source_target_pairs={{0,1},{1,0},{2,3},{3,2},{4,5},{5,4},{6,7},{7,6},{8,9},{9,8},{10,11... | collective-permute-start | bytes 1572872 | tf_op jit(solution)/shard_map/ppermute | solution.py:425
  87.1 11.1 %all-to-all-start.4 = ((bf16[32,8,128]{2,1,0:T(8,128)(2,1)}), bf16[32,8,128]{2,1,0:T(8,128)(2,1)S(1)}, u32[]{:S(2)}, u32[]{:S(2)}) async-start(bf16[32,8,128]{2,1,0:T(8,128)(2,1)} %bitcast.3), calls=%async_computation.4 | async-start | bytes 131072 | tf_op jit(solution)/shard_map/all_to_all | solution.py:406
  98.2 0.0 copy-start.1
  98.3 2.2 %copy-done.1 = bf16[4096,512]{1,0:T(8,128)(2,1)S(1)} copy-done((bf16[4096,512]{1,0:T(8,128)(2,1)S(1)}, bf16[4096,512]{1,0:T(8,128)(2,1)}, u32[]{:S(2)}) %copy-start.1) | copy-done | bytes 4194328
  100.4 0.7 output_early.1
  101.2 0.0 collective-permute-done.1.gated_ref
  101.2 1.1 %output_late.1 = bf16[128,512]{1,0:T(8,128)(2,1)} custom-call(bf16[8,256,128]{2,1,0:T(8,128)(2,1)S(1)} %collective-permute-done.1.gated_ref, bf16[8,256,512]{2,1,0:T(8,128)(2,1)S(1)} %get-tuple-element.21.weight_ref, f32[128,512]{1,0:T(8,128)S(1)} %get-tuple-element.22.before_ref), custom_call_target="tpu_custom_call" | custom-call | flops 268435456 | bytes 4194304 | tf_op jit(solution)/shard_map/output_late/pallas_call | solution.py:122
  102.3 0.0 all-to-all-done.4
  102.3 0.7 last_grads.1
Async XLA Ops:
  0.6 20.4 %copy-start.5 = (bf16[128,512]{1,0:T(8,128)(2,1)S(1)}, bf16[128,512]{1,0:T(8,128)(2,1)}, u32[]{:S(2)}) copy-start(bf16[128,512]{1,0:T(8,128)(2,1)} %cotangent_ref.3) | copy-start | bytes 393220
  4.3 19.6 %collective-permute-start = (bf16[8,256,128]{2,1,0:T(8,128)(2,1)}, bf16[8,256,128]{2,1,0:T(8,128)(2,1)S(1)}, u32[]{:S(2)}, u32[]{:S(2)}) collective-permute-start(bf16[8,256,128]{2,1,0:T(8,128)(2,1)} %get-tuple-element.16), channel_id=1, source_target_pairs={{0,1},{1,0},{2,3},{3,2},{4,5},{5,4},{6,7},{7,6},{8,9},{9,8},{10,11... | collective-permute-start | bytes 1572872 | tf_op jit(solution)/shard_map/ppermute | solution.py:414
  9.7 17.0 %all-to-all-start = ((bf16[32,24,128]{2,1,0:T(8,128)(2,1)}), bf16[32,24,128]{2,1,0:T(8,128)(2,1)S(1)}, u32[]{:S(2)}, u32[]{:S(2)}) async-start(bf16[32,24,128]{2,1,0:T(8,128)(2,1)} %get-tuple-element.14), calls=%async_computation | async-start | bytes 393216 | tf_op jit(solution)/shard_map/all_to_all | solution.py:406
  21.0 2.2 %copy-start = (bf16[4096,512]{1,0:T(8,128)(2,1)S(1)}, bf16[4096,512]{1,0:T(8,128)(2,1)}, u32[]{:S(2)}) copy-start(bf16[4096,512]{1,0:T(8,128)(2,1)} %param.8) | copy-start | bytes 12582916
  23.2 14.5 %copy-start.6 = (f32[256]{0:T(256)S(1)}, f32[256]{0:T(256)}, u32[]{:S(2)}) copy-start(f32[256]{0:T(256)} %param.7) | copy-start | bytes 3076
  26.8 24.1 %all-to-all-start.1 = ((bf16[8,256,128]{2,1,0:T(8,128)(2,1)}), bf16[8,256,128]{2,1,0:T(8,128)(2,1)S(1)}, u32[]{:S(2)}, u32[]{:S(2)}) async-start(bf16[8,256,128]{2,1,0:T(8,128)(2,1)} %total_share.1), calls=%async_computation.1 | async-start | bytes 1048576 | tf_op jit(solution)/shard_map/all_to_all | solution.py:410
  37.7 13.2 %copy-start.4 = (bf16[3,256,128]{2,1,0:T(8,128)(2,1)S(1)}, bf16[3,256,128]{2,1,0:T(8,128)(2,1)}, u32[]{:S(2)}) copy-start(bf16[3,256,128]{2,1,0:T(8,128)(2,1)} %projected_ref.7) | copy-start | bytes 589828
  42.8 3.2 %copy-start.2 = (bf16[8,128,4096]{2,1,0:T(8,128)(2,1)}, bf16[8,128,4096]{2,1,0:T(8,128)(2,1)S(1)}, u32[]{:S(2)}) copy-start(bf16[8,128,4096]{2,1,0:T(8,128)(2,1)S(1)} %get-tuple-element.18.toeplitz_ref) | copy-start | bytes 25165828
  66.1 17.2 %all-to-all-start.3 = ((bf16[8,256,128]{2,1,0:T(8,128)(2,1)}), bf16[8,256,128]{2,1,0:T(8,128)(2,1)S(1)}, u32[]{:S(2)}, u32[]{:S(2)}) async-start(bf16[8,256,128]{2,1,0:T(8,128)(2,1)} %spread_gated.1), calls=%async_computation.3 | async-start | bytes 1048576 | tf_op jit(solution)/shard_map/all_to_all | solution.py:410
  73.2 3.4 %copy-start.3 = (bf16[8,128,4096]{2,1,0:T(8,128)(2,1)S(1)}, bf16[8,128,4096]{2,1,0:T(8,128)(2,1)}, u32[]{:S(2)}) copy-start(bf16[8,128,4096]{2,1,0:T(8,128)(2,1)} %copy-done.2) | copy-start | bytes 25165828
  83.3 17.8 %collective-permute-start.1 = (bf16[8,256,128]{2,1,0:T(8,128)(2,1)S(1)}, bf16[8,256,128]{2,1,0:T(8,128)(2,1)S(1)}, u32[]{:S(2)}, u32[]{:S(2)}) collective-permute-start(bf16[8,256,128]{2,1,0:T(8,128)(2,1)S(1)} %all-to-all-done.3.gated_ref), channel_id=1, source_target_pairs={{0,1},{1,0},{2,3},{3,2},{4,5},{5,4},{6,7},{7,6},{8,9},{9,8},{10,11... | collective-permute-start | bytes 1572872 | tf_op jit(solution)/shard_map/ppermute | solution.py:425
  87.1 15.2 %all-to-all-start.4 = ((bf16[32,8,128]{2,1,0:T(8,128)(2,1)}), bf16[32,8,128]{2,1,0:T(8,128)(2,1)S(1)}, u32[]{:S(2)}, u32[]{:S(2)}) async-start(bf16[32,8,128]{2,1,0:T(8,128)(2,1)} %bitcast.3), calls=%async_computation.4 | async-start | bytes 131072 | tf_op jit(solution)/shard_map/all_to_all | solution.py:406
  98.2 2.2 %copy-start.1 = (bf16[4096,512]{1,0:T(8,128)(2,1)S(1)}, bf16[4096,512]{1,0:T(8,128)(2,1)}, u32[]{:S(2)}) copy-start(bf16[4096,512]{1,0:T(8,128)(2,1)} %param.8) | copy-start | bytes 12582916

commit v6 on v5

--- a/solution.py
+++ b/solution.py
@@ -10,9 +10,9 @@
 ROWS = (((0,), (0,)), ((), ()))
 VMEM_LIMIT = 8 << 20
 FIRST_LIMIT = 54 << 20
-FIRST_SUM = 7
+FIRST_SUM = 6
 FIRST_GATED = 5
-FIRST_SEQ = 18
+FIRST_SEQ = 19
 VMEM = pl.BlockSpec(memory_space=pltpu.VMEM)
 HBM = pl.BlockSpec(memory_space=pltpu.HBM)
 SMEM = pl.BlockSpec(memory_space=pltpu.SMEM)
@@ -289,17 +289,28 @@
     return array if by == 0 else jnp.concatenate([array[by:], array[:by]], axis=0)
 
 
+def toeplitz_block(taps, lag, before, upper):
+    spread = jnp.broadcast_to(taps[lag : lag + 1, :], (BLOCK, BLOCK))
+    turned = pltpu.roll(spread, 0, 1, stride=1, stride_axis=0)
+    return jnp.where(upper, turned, before).astype(jnp.bfloat16), turned
+
+
+def upper_half():
+    sub, lane = (lax.broadcasted_iota(jnp.int32, (BLOCK, BLOCK), axis) for axis in range(2))
+    return lane >= sub
+
+
 def causal(given, skip):
     chunks, rows, _ = given.shape
     per = rows // 3
 
-    def kernel(skip_ref, given_ref, inner_ref, toeplitz_ref, wide, shifted, collected):
-        wide[...] = given_ref[...].astype(jnp.float32).reshape(chunks * rows, BLOCK)
+    def kernel(skip_ref, given_ref, inner_ref, wide, shifted, collected):
+        wide[pl.ds(0, chunks * rows), :] = (
+            given_ref[...].astype(jnp.float32).reshape(chunks * rows, BLOCK)
+        )
         for part in range(2):
             shifted[part, pl.ds(0, chunks), :] = jnp.zeros((chunks, BLOCK), jnp.float32)
-        upper = lax.broadcasted_iota(jnp.int32, (BLOCK, BLOCK), 1) >= lax.broadcasted_iota(
-            jnp.int32, (BLOCK, BLOCK), 0
-        )
+        upper = upper_half()
 
         @pl.loop(0, per)
         def _(channel):
@@ -315,11 +326,7 @@
             for lag in range(0, chunks, 2):
                 blocks, signals = [], []
                 for one in (lag, lag + 1):
-                    spread = jnp.broadcast_to(taps[one : one + 1, :], (BLOCK, BLOCK))
-                    turned = pltpu.roll(spread, 0, 1, stride=1, stride_axis=0)
-                    block = jnp.where(upper, turned, before).astype(jnp.bfloat16)
-                    before = turned
-                    toeplitz_ref[channel, :, one * BLOCK : (one + 1) * BLOCK] = block
+                    block, before = toeplitz_block(taps, one, before, upper)
                     blocks.append(block)
                     parts = [shifted[part, chunks - one : 2 * chunks - one, :] for part in range(2)]
                     signals.append(jnp.concatenate(parts, axis=0).astype(jnp.bfloat16))
@@ -331,50 +338,62 @@
             inner = total[:chunks] + total[chunks:] + skip_ref[channel] * mixed
             collected[pl.ds(channel, chunks, stride=per), :] = turn(inner, FIRST_SEQ)
 
-        inner_ref[...] = collected[...].astype(jnp.bfloat16).reshape(inner_ref.shape)
+        inner = collected[pl.ds(0, chunks * per), :]
+        inner_ref[...] = inner.astype(jnp.bfloat16).reshape(inner_ref.shape)
 
     return call(
         kernel,
         [SMEM, VMEM],
-        [
-            jax.ShapeDtypeStruct((chunks // 2, 2 * per, BLOCK), jnp.bfloat16),
-            jax.ShapeDtypeStruct((per, BLOCK, chunks * BLOCK), jnp.bfloat16),
-        ],
+        jax.ShapeDtypeStruct((chunks // 2, 2 * per, BLOCK), jnp.bfloat16),
         16 * per * chunks * chunks * BLOCK * BLOCK,
         [
-            pltpu.VMEM((chunks * rows, BLOCK), jnp.float32),
+            pltpu.VMEM(((chunks + 1) * rows, BLOCK), jnp.float32),
             pltpu.VMEM((2, 2 * chunks, BLOCK), jnp.float32),
-            pltpu.VMEM((chunks * per, BLOCK), jnp.float32),
+            pltpu.VMEM(((chunks + 1) * per, BLOCK), jnp.float32),
         ],
         "causal_sum",
     )(skip, given)
 
 
-def adjoint(back, toeplitz, skip):
+def adjoint(given, back, skip):
     chunks, rows, _ = back.shape
     per = rows // 2
-
-    def kernel(skip_ref, back_ref, toeplitz_ref, out_ref, grads, shifted, collected):
-        grads[...] = back_ref[...].astype(jnp.float32).reshape(chunks * rows, BLOCK)
+    wide_rows = given.shape[1]
+
+    def kernel(skip_ref, given_ref, back_ref, out_ref, wide, grads, shifted, collected):
+        wide[pl.ds(0, chunks * wide_rows), :] = (
+            given_ref[...].astype(jnp.float32).reshape(chunks * wide_rows, BLOCK)
+        )
+        upper = upper_half()
+        grads[pl.ds(0, chunks * rows), :] = (
+            back_ref[...].astype(jnp.float32).reshape(chunks * rows, BLOCK)
+        )
         shifted[pl.ds(chunks, chunks), :] = jnp.zeros((chunks, BLOCK), jnp.float32)
 
         @pl.loop(0, per)
         def _(channel):
             grad_inner = turn(grads[pl.ds(per + channel, chunks, stride=rows), :], -FIRST_SEQ)
             shifted[pl.ds(0, chunks), :] = grad_inner
+            taps = turn(wide[pl.ds(2 * per + channel, chunks, stride=wide_rows), :], -FIRST_SEQ)
+            before = jnp.zeros((BLOCK, BLOCK), jnp.float32)
             total = jnp.zeros((chunks, BLOCK), jnp.float32)
             for lag in range(0, chunks, 2):
-                signals = [shifted[one : one + chunks, :] for one in (lag, lag + 1)]
+                blocks, signals = [], []
+                for one in (lag, lag + 1):
+                    block, before = toeplitz_block(taps, one, before, upper)
+                    blocks.append(block)
+                    signals.append(shifted[one : one + chunks, :])
                 total = total + lax.dot_general(
                     jnp.concatenate(signals, axis=1).astype(jnp.bfloat16),
-                    toeplitz_ref[channel, :, lag * BLOCK : (lag + 2) * BLOCK],
+                    jnp.concatenate(blocks, axis=1),
                     LANES,
                     preferred_element_type=jnp.float32,
                 )
             grad_mixed = total + skip_ref[channel] * grad_inner
             collected[pl.ds(channel, chunks, stride=per), :] = turn(grad_mixed, FIRST_SEQ)
 
-        out_ref[...] = collected[...].astype(jnp.bfloat16).reshape(out_ref.shape)
+        mixed = collected[pl.ds(0, chunks * per), :]
+        out_ref[...] = mixed.astype(jnp.bfloat16).reshape(out_ref.shape)
 
     return call(
         kernel,
@@ -382,12 +401,13 @@
         jax.ShapeDtypeStruct((chunks // 2, 2 * per, BLOCK), jnp.bfloat16),
         16 * per * chunks * chunks * BLOCK * BLOCK,
         [
-            pltpu.VMEM((chunks * rows, BLOCK), jnp.float32),
+            pltpu.VMEM(((chunks + 1) * wide_rows, BLOCK), jnp.float32),
+            pltpu.VMEM(((chunks + 1) * rows, BLOCK), jnp.float32),
             pltpu.VMEM((2 * chunks, BLOCK), jnp.float32),
-            pltpu.VMEM((chunks * per, BLOCK), jnp.float32),
+            pltpu.VMEM(((chunks + 1) * per, BLOCK), jnp.float32),
         ],
         "adjoint_sum",
-    )(skip, back, toeplitz)
+    )(skip, given, back)
 
 
 def per_device(projected, filters, skip, out_weight, cotangent):
@@ -415,12 +435,12 @@
     given = exchange_seq(packed)
     share_own = partial_half(own, weight, cotangent, jnp.float32)
     skip_here = lax.dynamic_slice(skip, ((lax.axis_index("seq") - FIRST_SEQ) % seq * per,), (per,))
-    inner, toeplitz = causal(given, skip_here)
+    inner = causal(given, skip_here)
     shares = exchange_z(total_share(share_own, received, FIRST_SUM), FIRST_SUM)
     packed, grad_gated = pack_middle(inner, shares, projected, seq)
     middle = exchange_seq(packed)
     gated_half = exchange_z(spread(middle, projected, planes), FIRST_GATED)
-    grads_there = adjoint(middle, toeplitz, skip_here)
+    grads_there = adjoint(given, middle, skip_here)
     grads_there, gated_half = lax.optimization_barrier((grads_there, gated_half))
     gated_other = lax.ppermute(gated_half, "chan", pairs)
     output, weight_other = project_half(own, gated_half, weight, FIRST_GATED)

time: 104 us -> 102 us (0.981)
  local copies, waits for them, and re-layouts: 11.1 us -> 4.45 us
  waiting for transfers between devices: 8.53 us -> 14.5 us
  starting transfers between devices: 49.5 us -> 48.3 us
    unnamed x14 -> x10, local copies, waits for them, and re-layouts: 11 us -> 4.38 us
    all_to_all x2, waiting for transfers between devices: 6.62 us -> 12.5 us  [exchange_z(): lax.all_to_all(array, 'chan', 0, 0, tiled=True, axis_index_groups=groups)]
    ppermute x1, starting transfers between devices: 3.78 us -> 2.65 us  [per_device(): gated_other = lax.ppermute(gated_half, 'chan', pairs)]
  transfers between devices with their start and end apart: 6 -> 6, of which waited for: 3 -> 3; matrix products, arithmetic and copies ran while one was open for 0% -> 0% of each run, Pallas kernels for 13% -> 14%
where the time goes in v6:
time: 102 us
  starting transfers between devices  48.3 us (47%)
  Pallas kernels  19.2 us (19%)
  waiting for transfers between devices  14.5 us (14%)
  blocking collectives  14.3 us (14%)
  local copies, waits for them, and re-layouts  4.45 us (4%)
    all_to_all x2, starting transfers between devices, exchange_seq(): lax.all_to_all(array, 'seq', 0, 0, tiled=True, axis_index_groups=groups)  22 us
    all_to_all x2, starting transfers between devices, exchange_z(): lax.all_to_all(array, 'chan', 0, 0, tiled=True, axis_index_groups=groups)  18.2 us
    all_to_all x1, blocking collectives, exchange_seq(): lax.all_to_all(array, 'seq', 0, 0, tiled=True, axis_index_groups=groups)  14.3 us
    all_to_all x2, waiting for transfers between devices, exchange_z(): lax.all_to_all(array, 'chan', 0, 0, tiled=True, axis_index_groups=groups)  12.5 us
    pallas_call x1, Pallas kernels, adjoint(): call(kernel, [SMEM, VMEM, VMEM], jax.ShapeDtypeStruct((chunks // 2, 2 * p...  5.74 us
    ppermute x1, starting transfers between devices, per_device(): received = lax.ppermute(share_other, 'chan', pairs)  5.48 us
    pallas_call x1, Pallas kernels, causal(): call(kernel, [SMEM, VMEM], jax.ShapeDtypeStruct((chunks // 2, 2 * per, BL...  4.72 us
    unnamed x10, local copies, waits for them, and re-layouts  4.38 us
  transfers between devices with their start and end apart: 6, of which 3 were waited for; matrix products, arithmetic and copies ran while one was open for 0% of the time, Pallas kernels for 14%

profile of v6, /device:TPU:1, one launch (start us, length us, event | category | flops | bytes accessed | tf_op | source)
XLA Modules:
  0.0 101.5 jit_solution(5923507810883366531)
XLA Ops:
  0.6 0.0 copy-start.3
  0.6 3.6 %first_share.1 = (bf16[8,256,128]{2,1,0:T(8,128)(2,1)}, bf16[32,24,128]{2,1,0:T(8,128)(2,1)}) custom-call(s32[1]{0:T(128)} %bitcast.half_ref, bf16[8,2,256,512]{3,2,1,0:T(8,128)(2,1)} %bitcast.5, bf16[128,512]{1,0:T(8,128)(2,1)} %cotangent_ref.3, bf16[3,256,128]{2,1,0:T(8,128)(2,1)} %projected_ref.7, f32[256,128]{1,0:T(8,128)} %filters_ref.1), custom_call_target="tpu_custom_call" | custom-call | flops 268435456 | bytes 4194304 | tf_op jit(solution)/shard_map/first_share/pallas_call | solution.py:191
  4.2 5.5 %collective-permute-start = (bf16[8,256,128]{2,1,0:T(8,128)(2,1)}, bf16[8,256,128]{2,1,0:T(8,128)(2,1)S(1)}, u32[]{:S(2)}, u32[]{:S(2)}) collective-permute-start(bf16[8,256,128]{2,1,0:T(8,128)(2,1)} %get-tuple-element.13), channel_id=1, source_target_pairs={{0,1},{1,0},{2,3},{3,2},{4,5},{5,4},{6,7},{7,6},{8,9},{9,8},{10,11... | collective-permute-start | bytes 1572872 | tf_op jit(solution)/shard_map/ppermute | solution.py:434
  9.7 11.0 %all-to-all-start = ((bf16[32,24,128]{2,1,0:T(8,128)(2,1)}), bf16[32,24,128]{2,1,0:T(8,128)(2,1)S(1)}, u32[]{:S(2)}, u32[]{:S(2)}) async-start(bf16[32,24,128]{2,1,0:T(8,128)(2,1)} %get-tuple-element.12), calls=%async_computation | async-start | bytes 393216 | tf_op jit(solution)/shard_map/all_to_all | solution.py:426
  20.7 0.0 copy-done.3
  20.7 0.0 copy-start
  20.7 2.2 %copy-done = bf16[4096,512]{1,0:T(8,128)(2,1)S(1)} copy-done((bf16[4096,512]{1,0:T(8,128)(2,1)S(1)}, bf16[4096,512]{1,0:T(8,128)(2,1)}, u32[]{:S(2)}) %copy-start) | copy-done | bytes 4194328
  22.9 0.0 copy-start.4
  22.9 0.7 partial_grad_gated.1.share_ref
  23.6 0.0 collective-permute-done.received_ref
  23.6 0.9 total_share.1
  24.5 2.0 %all-to-all-done.given_ref = bf16[32,24,128]{2,1,0:T(8,128)(2,1)S(1)} async-done(((bf16[32,24,128]{2,1,0:T(8,128)(2,1)}), bf16[32,24,128]{2,1,0:T(8,128)(2,1)S(1)}, u32[]{:S(2)}, u32[]{:S(2)}) %all-to-all-start) | async-done | bytes 196640 | tf_op jit(solution)/shard_map/all_to_all | solution.py:426
  26.5 10.6 %all-to-all-start.1 = ((bf16[8,256,128]{2,1,0:T(8,128)(2,1)}), bf16[8,256,128]{2,1,0:T(8,128)(2,1)S(1)}, u32[]{:S(2)}, u32[]{:S(2)}) async-start(bf16[8,256,128]{2,1,0:T(8,128)(2,1)} %total_share.1), calls=%async_computation.1 | async-start | bytes 1048576 | tf_op jit(solution)/shard_map/all_to_all | solution.py:430
  37.1 0.0 copy-start.2
  37.1 0.0 copy-done.4
  37.1 0.1 dynamic_slice.3.skip_ref
  37.1 4.7 %causal_sum.1.inner_ref = bf16[16,16,128]{2,1,0:T(8,128)(2,1)S(1)} custom-call(f32[8]{0:T(128)S(1)} %dynamic_slice.3.skip_ref, bf16[32,24,128]{2,1,0:T(8,128)(2,1)S(1)} %all-to-all-done.given_ref), custom_call_target="tpu_custom_call" | custom-call | flops 2147483648 | bytes 4194304 | tf_op jit(solution)/shard_map/causal_sum/pallas_call | solution.py:344
  41.9 7.2 %all-to-all-done.1.shares_ref = bf16[8,256,128]{2,1,0:T(8,128)(2,1)S(1)} async-done(((bf16[8,256,128]{2,1,0:T(8,128)(2,1)}), bf16[8,256,128]{2,1,0:T(8,128)(2,1)S(1)}, u32[]{:S(2)}, u32[]{:S(2)}) %all-to-all-start.1) | async-done | bytes 524320 | tf_op jit(solution)/shard_map/all_to_all | solution.py:430
  49.1 0.0 copy-done.2
  49.1 0.1 pack_middle.1
  49.2 14.3 %all_to_all.25.back_ref.middle_ref = bf16[32,16,128]{2,1,0:T(8,128)(2,1)S(1)} all-to-all(bf16[32,16,128]{2,1,0:T(8,128)(2,1)S(1)} %get-tuple-element.14), channel_id=1, replica_groups={{304,320,336,352,368,384,400,416,432,448,464,480,496,0,16,32,48,64,80,9..., dimensions={0} | all-to-all | bytes 262144 | tf_op jit(solution)/shard_map/all_to_all | solution.py:426
  63.5 0.9 spread_gated.1
  64.4 7.6 %all-to-all-start.3 = ((bf16[8,256,128]{2,1,0:T(8,128)(2,1)}), bf16[8,256,128]{2,1,0:T(8,128)(2,1)S(1)}, u32[]{:S(2)}, u32[]{:S(2)}) async-start(bf16[8,256,128]{2,1,0:T(8,128)(2,1)} %spread_gated.1), calls=%async_computation.3 | async-start | bytes 1048576 | tf_op jit(solution)/shard_map/all_to_all | solution.py:430
  72.0 5.7 %adjoint_sum.1 = bf16[16,16,128]{2,1,0:T(8,128)(2,1)} custom-call(f32[8]{0:T(128)S(1)} %dynamic_slice.3.skip_ref, bf16[32,24,128]{2,1,0:T(8,128)(2,1)S(1)} %all-to-all-done.given_ref, bf16[32,16,128]{2,1,0:T(8,128)(2,1)S(1)} %all_to_all.25.back_ref.middle_ref), custom_call_target="tpu_custom_call" | custom-call | flops 2147483648 | bytes 4194304 | tf_op jit(solution)/shard_map/adjoint_sum/pallas_call | solution.py:398
  77.7 5.3 %all-to-all-done.3.gated_ref = bf16[8,256,128]{2,1,0:T(8,128)(2,1)S(1)} async-done(((bf16[8,256,128]{2,1,0:T(8,128)(2,1)}), bf16[8,256,128]{2,1,0:T(8,128)(2,1)S(1)}, u32[]{:S(2)}, u32[]{:S(2)}) %all-to-all-start.3) | async-done | bytes 524320 | tf_op jit(solution)/shard_map/all_to_all | solution.py:430
  83.0 2.6 %collective-permute-start.1 = (bf16[8,256,128]{2,1,0:T(8,128)(2,1)S(1)}, bf16[8,256,128]{2,1,0:T(8,128)(2,1)S(1)}, u32[]{:S(2)}, u32[]{:S(2)}) collective-permute-start(bf16[8,256,128]{2,1,0:T(8,128)(2,1)S(1)} %all-to-all-done.3.gated_ref), channel_id=1, source_target_pairs={{0,1},{1,0},{2,3},{3,2},{4,5},{5,4},{6,7},{7,6},{8,9},{9,8},{10,11... | collective-permute-start | bytes 1572872 | tf_op jit(solution)/shard_map/ppermute | solution.py:445
  85.7 11.1 %all-to-all-start.4 = ((bf16[32,8,128]{2,1,0:T(8,128)(2,1)}), bf16[32,8,128]{2,1,0:T(8,128)(2,1)S(1)}, u32[]{:S(2)}, u32[]{:S(2)}) async-start(bf16[32,8,128]{2,1,0:T(8,128)(2,1)} %bitcast.3), calls=%async_computation.4 | async-start | bytes 131072 | tf_op jit(solution)/shard_map/all_to_all | solution.py:426
  96.7 0.0 copy-start.1
  96.8 2.2 %copy-done.1 = bf16[4096,512]{1,0:T(8,128)(2,1)S(1)} copy-done((bf16[4096,512]{1,0:T(8,128)(2,1)S(1)}, bf16[4096,512]{1,0:T(8,128)(2,1)}, u32[]{:S(2)}) %copy-start.1) | copy-done | bytes 4194328
  98.9 0.7 output_early.1
  99.6 0.0 collective-permute-done.1.gated_ref
  99.7 1.2 %output_late.1 = bf16[128,512]{1,0:T(8,128)(2,1)} custom-call(bf16[8,256,128]{2,1,0:T(8,128)(2,1)S(1)} %collective-permute-done.1.gated_ref, bf16[8,256,512]{2,1,0:T(8,128)(2,1)S(1)} %get-tuple-element.17.weight_ref, f32[128,512]{1,0:T(8,128)S(1)} %get-tuple-element.18.before_ref), custom_call_target="tpu_custom_call" | custom-call | flops 268435456 | bytes 4194304 | tf_op jit(solution)/shard_map/output_late/pallas_call | solution.py:122
  100.8 0.0 all-to-all-done.4
  100.8 0.7 last_grads.1
Async XLA Ops:
  0.6 20.1 %copy-start.3 = (bf16[128,512]{1,0:T(8,128)(2,1)S(1)}, bf16[128,512]{1,0:T(8,128)(2,1)}, u32[]{:S(2)}) copy-start(bf16[128,512]{1,0:T(8,128)(2,1)} %cotangent_ref.3) | copy-start | bytes 393220
  4.2 19.4 %collective-permute-start = (bf16[8,256,128]{2,1,0:T(8,128)(2,1)}, bf16[8,256,128]{2,1,0:T(8,128)(2,1)S(1)}, u32[]{:S(2)}, u32[]{:S(2)}) collective-permute-start(bf16[8,256,128]{2,1,0:T(8,128)(2,1)} %get-tuple-element.13), channel_id=1, source_target_pairs={{0,1},{1,0},{2,3},{3,2},{4,5},{5,4},{6,7},{7,6},{8,9},{9,8},{10,11... | collective-permute-start | bytes 1572872 | tf_op jit(solution)/shard_map/ppermute | solution.py:434
  9.7 16.7 %all-to-all-start = ((bf16[32,24,128]{2,1,0:T(8,128)(2,1)}), bf16[32,24,128]{2,1,0:T(8,128)(2,1)S(1)}, u32[]{:S(2)}, u32[]{:S(2)}) async-start(bf16[32,24,128]{2,1,0:T(8,128)(2,1)} %get-tuple-element.12), calls=%async_computation | async-start | bytes 393216 | tf_op jit(solution)/shard_map/all_to_all | solution.py:426
  20.7 2.2 %copy-start = (bf16[4096,512]{1,0:T(8,128)(2,1)S(1)}, bf16[4096,512]{1,0:T(8,128)(2,1)}, u32[]{:S(2)}) copy-start(bf16[4096,512]{1,0:T(8,128)(2,1)} %param.8) | copy-start | bytes 12582916
  22.9 14.2 %copy-start.4 = (f32[256]{0:T(256)S(1)}, f32[256]{0:T(256)}, u32[]{:S(2)}) copy-start(f32[256]{0:T(256)} %param.7) | copy-start | bytes 3076
  26.5 22.6 %all-to-all-start.1 = ((bf16[8,256,128]{2,1,0:T(8,128)(2,1)}), bf16[8,256,128]{2,1,0:T(8,128)(2,1)S(1)}, u32[]{:S(2)}, u32[]{:S(2)}) async-start(bf16[8,256,128]{2,1,0:T(8,128)(2,1)} %total_share.1), calls=%async_computation.1 | async-start | bytes 1048576 | tf_op jit(solution)/shard_map/all_to_all | solution.py:430
  37.1 12.0 %copy-start.2 = (bf16[3,256,128]{2,1,0:T(8,128)(2,1)S(1)}, bf16[3,256,128]{2,1,0:T(8,128)(2,1)}, u32[]{:S(2)}) copy-start(bf16[3,256,128]{2,1,0:T(8,128)(2,1)} %projected_ref.7) | copy-start | bytes 589828
  64.4 18.6 %all-to-all-start.3 = ((bf16[8,256,128]{2,1,0:T(8,128)(2,1)}), bf16[8,256,128]{2,1,0:T(8,128)(2,1)S(1)}, u32[]{:S(2)}, u32[]{:S(2)}) async-start(bf16[8,256,128]{2,1,0:T(8,128)(2,1)} %spread_gated.1), calls=%async_computation.3 | async-start | bytes 1048576 | tf_op jit(solution)/shard_map/all_to_all | solution.py:430
  83.0 16.6 %collective-permute-start.1 = (bf16[8,256,128]{2,1,0:T(8,128)(2,1)S(1)}, bf16[8,256,128]{2,1,0:T(8,128)(2,1)S(1)}, u32[]{:S(2)}, u32[]{:S(2)}) collective-permute-start(bf16[8,256,128]{2,1,0:T(8,128)(2,1)S(1)} %all-to-all-done.3.gated_ref), channel_id=1, source_target_pairs={{0,1},{1,0},{2,3},{3,2},{4,5},{5,4},{6,7},{7,6},{8,9},{9,8},{10,11... | collective-permute-start | bytes 1572872 | tf_op jit(solution)/shard_map/ppermute | solution.py:445
  85.7 15.2 %all-to-all-start.4 = ((bf16[32,8,128]{2,1,0:T(8,128)(2,1)}), bf16[32,8,128]{2,1,0:T(8,128)(2,1)S(1)}, u32[]{:S(2)}, u32[]{:S(2)}) async-start(bf16[32,8,128]{2,1,0:T(8,128)(2,1)} %bitcast.3), calls=%async_computation.4 | async-start | bytes 131072 | tf_op jit(solution)/shard_map/all_to_all | solution.py:426
  96.7 2.2 %copy-start.1 = (bf16[4096,512]{1,0:T(8,128)(2,1)S(1)}, bf16[4096,512]{1,0:T(8,128)(2,1)}, u32[]{:S(2)}) copy-start(bf16[4096,512]{1,0:T(8,128)(2,1)} %param.8) | copy-start | bytes 12582916

commit v7 on v6

--- a/solution.py
+++ b/solution.py
@@ -79,7 +79,7 @@
     def early(half_ref, gated_ref, weight_ref, out_ref, kept_ref, moved):
         copies = [
             pltpu.make_async_copy(
-                weight_ref.at[(plane + first) % planes, 1 - half_ref[0]],
+                weight_ref.at[lax.rem(half_ref[1] + 1 + plane, planes), 1 - half_ref[0]],
                 kept_ref.at[plane],
                 moved.at[plane],
             )
@@ -99,10 +99,14 @@
         for copy in copies:
             copy.wait()
 
-    def late(gated_ref, weight_ref, before_ref, out_ref):
+    def late(gated_ref, near_ref, weight_ref, before_ref, out_ref):
+        others = planes - 1
         total = before_ref[...] + lax.dot_general(
-            gated_ref[...].reshape(planes * rows, count),
-            weight_ref[...].reshape(planes * rows, width),
+            near_ref[...], weight_ref[others], ROWS, preferred_element_type=jnp.float32
+        )
+        total = total + lax.dot_general(
+            gated_ref[...].reshape(others * rows, count),
+            weight_ref[pl.ds(0, others)].reshape(others * rows, width),
             ROWS,
             preferred_element_type=jnp.float32,
         )
@@ -119,7 +123,7 @@
             [pltpu.SemaphoreType.DMA((planes,))],
             name="output_early",
         )(half, gated, weight)
-    return call(late, [VMEM] * 3, result, flops, name="output_late")(gated, weight, before)
+    return call(late, [VMEM] * 4, result, flops, name="output_late")(gated, *half, weight, before)
 
 
 def first(half, weight, cotangent, projected, filters, seq):
@@ -264,6 +268,33 @@
     )(middle, projected)
 
 
+def other_planes(start, gated):
+    planes, channels, count = gated.shape
+
+    def kernel(start_ref, gated_ref, out_ref, moved):
+        copies = [
+            pltpu.make_async_copy(
+                gated_ref.at[lax.rem(start_ref[0] + place, planes)],
+                out_ref.at[place],
+                moved.at[place],
+            )
+            for place in range(planes - 1)
+        ]
+        for copy in copies:
+            copy.start()
+        for copy in copies:
+            copy.wait()
+
+    return call(
+        kernel,
+        [SMEM, VMEM],
+        jax.ShapeDtypeStruct((planes - 1, channels, count), gated.dtype),
+        1 << 22,
+        [pltpu.SemaphoreType.DMA((planes - 1,))],
+        "other_planes",
+    )(start, gated)
+
+
 def last_grads(grad_mixed, middle, grad_gated, projected):
     seq, rows, count = middle.shape
     per = rows // 2
@@ -439,13 +470,19 @@
     shares = exchange_z(total_share(share_own, received, FIRST_SUM), FIRST_SUM)
     packed, grad_gated = pack_middle(inner, shares, projected, seq)
     middle = exchange_seq(packed)
-    gated_half = exchange_z(spread(middle, projected, planes), FIRST_GATED)
+    gated = spread(middle, projected, planes)
+    gated_half = exchange_z(gated, FIRST_GATED)
     grads_there = adjoint(given, middle, skip_here)
+    plane = lax.axis_index("chan") >> 1
+    grads_there, gated = lax.optimization_barrier((grads_there, gated))
+    near = lax.ppermute(gated[0], "chan", pairs)
     grads_there, gated_half = lax.optimization_barrier((grads_there, gated_half))
-    gated_other = lax.ppermute(gated_half, "chan", pairs)
-    output, weight_other = project_half(own, gated_half, weight, FIRST_GATED)
+    start = (plane - FIRST_GATED + 1) % planes
+    gated_other = lax.ppermute(other_planes(start.reshape(1), gated_half), "chan", pairs)
+    place = jnp.stack([half, plane])
+    output, weight_other = project_half(place, gated_half, weight, FIRST_GATED)
     grads = exchange_seq(grads_there.reshape(seq, per, count))
-    output = project_half(other, gated_other, weight_other, FIRST_GATED, output)
+    output = project_half((near,), gated_other, weight_other, FIRST_GATED, output)
     grads, output = lax.optimization_barrier((grads, output))
     grads = last_grads(grads.reshape(seq // 2, 2 * per, count), middle, grad_gated, projected)
     return output, grads

time: 102 us -> 108 us (1.059)
  starting transfers between devices: 48.3 us -> 51.6 us
  Pallas kernels: 19.2 us -> 20.4 us
    ppermute x1 -> x2, starting transfers between devices: 2.65 us -> 6.77 us  [the longest x1 4.1 us: per_device(): near = lax.ppermute(gated[0], 'chan', pairs)]
  transfers between devices with their start and end apart: 6 -> 7, of which waited for: 3 -> 3; matrix products, arithmetic and copies ran while one was open for 0% -> 1% of each run, Pallas kernels for 14% -> 14%
where the time goes in v7:
time: 108 us; the launch traced here: 107 us
  starting transfers between devices  51.6 us (48%)
  Pallas kernels  20.4 us (19%)
  waiting for transfers between devices  14.5 us (13%)
  blocking collectives  14.3 us (13%)
  local copies, waits for them, and re-layouts  5.3 us (5%)
    all_to_all x2, starting transfers between devices, exchange_seq(): lax.all_to_all(array, 'seq', 0, 0, tiled=True, axis_index_groups=groups)  21.2 us
    all_to_all x2, starting transfers between devices, exchange_z(): lax.all_to_all(array, 'chan', 0, 0, tiled=True, axis_index_groups=groups)  18.2 us
    all_to_all x1, blocking collectives, exchange_seq(): lax.all_to_all(array, 'seq', 0, 0, tiled=True, axis_index_groups=groups)  14.3 us
    all_to_all x2, waiting for transfers between devices, exchange_z(): lax.all_to_all(array, 'chan', 0, 0, tiled=True, axis_index_groups=groups)  12.5 us
    pallas_call x1, Pallas kernels, adjoint(): call(kernel, [SMEM, VMEM, VMEM], jax.ShapeDtypeStruct((chunks // 2, 2 * p...  5.74 us
    ppermute x1, starting transfers between devices, per_device(): received = lax.ppermute(share_other, 'chan', pairs)  5.48 us
    pallas_call x1, Pallas kernels, causal(): call(kernel, [SMEM, VMEM], jax.ShapeDtypeStruct((chunks // 2, 2 * per, BL...  4.73 us
    unnamed x10, local copies, waits for them, and re-layouts  4.38 us
  transfers between devices with their start and end apart: 7, of which 3 were waited for; matrix products, arithmetic and copies ran while one was open for 1% of the time, Pallas kernels for 14%

profile of v7, /device:TPU:1, one launch (start us, length us, event | category | flops | bytes accessed | tf_op | source)
XLA Modules:
  0.0 106.9 jit_solution(13099177602231941534)
XLA Ops:
  0.6 0.0 copy-start.3
  0.6 3.6 %first_share.1 = (bf16[8,256,128]{2,1,0:T(8,128)(2,1)}, bf16[32,24,128]{2,1,0:T(8,128)(2,1)}) custom-call(s32[1]{0:T(128)} %bitcast.half_ref, bf16[8,2,256,512]{3,2,1,0:T(8,128)(2,1)} %bitcast.9, bf16[128,512]{1,0:T(8,128)(2,1)} %cotangent_ref.3, bf16[3,256,128]{2,1,0:T(8,128)(2,1)} %projected_ref.7, f32[256,128]{1,0:T(8,128)} %filters_ref.1), custom_call_target="tpu_custom_call" | custom-call | flops 268435456 | bytes 4194304 | tf_op jit(solution)/shard_map/first_share/pallas_call | solution.py:195
  4.3 5.5 %collective-permute-start = (bf16[8,256,128]{2,1,0:T(8,128)(2,1)}, bf16[8,256,128]{2,1,0:T(8,128)(2,1)S(1)}, u32[]{:S(2)}, u32[]{:S(2)}) collective-permute-start(bf16[8,256,128]{2,1,0:T(8,128)(2,1)} %get-tuple-element.15), channel_id=1, source_target_pairs={{0,1},{1,0},{2,3},{3,2},{4,5},{5,4},{6,7},{7,6},{8,9},{9,8},{10,11... | collective-permute-start | bytes 1572872 | tf_op jit(solution)/shard_map/ppermute | solution.py:465
  9.7 11.0 %all-to-all-start = ((bf16[32,24,128]{2,1,0:T(8,128)(2,1)}), bf16[32,24,128]{2,1,0:T(8,128)(2,1)S(1)}, u32[]{:S(2)}, u32[]{:S(2)}) async-start(bf16[32,24,128]{2,1,0:T(8,128)(2,1)} %get-tuple-element.14), calls=%async_computation | async-start | bytes 393216 | tf_op jit(solution)/shard_map/all_to_all | solution.py:457
  20.7 0.0 copy-done.3
  20.7 0.0 copy-start
  20.7 2.2 %copy-done = bf16[4096,512]{1,0:T(8,128)(2,1)S(1)} copy-done((bf16[4096,512]{1,0:T(8,128)(2,1)S(1)}, bf16[4096,512]{1,0:T(8,128)(2,1)}, u32[]{:S(2)}) %copy-start) | copy-done | bytes 4194328
  22.9 0.0 copy-start.4
  22.9 0.7 partial_grad_gated.1.share_ref
  23.6 0.0 collective-permute-done.received_ref
  23.6 0.9 total_share.1
  24.5 2.0 %all-to-all-done.given_ref = bf16[32,24,128]{2,1,0:T(8,128)(2,1)S(1)} async-done(((bf16[32,24,128]{2,1,0:T(8,128)(2,1)}), bf16[32,24,128]{2,1,0:T(8,128)(2,1)S(1)}, u32[]{:S(2)}, u32[]{:S(2)}) %all-to-all-start) | async-done | bytes 196640 | tf_op jit(solution)/shard_map/all_to_all | solution.py:457
  26.5 10.6 %all-to-all-start.1 = ((bf16[8,256,128]{2,1,0:T(8,128)(2,1)}), bf16[8,256,128]{2,1,0:T(8,128)(2,1)S(1)}, u32[]{:S(2)}, u32[]{:S(2)}) async-start(bf16[8,256,128]{2,1,0:T(8,128)(2,1)} %total_share.1), calls=%async_computation.1 | async-start | bytes 1048576 | tf_op jit(solution)/shard_map/all_to_all | solution.py:461
  37.1 0.0 copy-start.2
  37.1 0.0 copy-done.4
  37.1 0.1 dynamic_slice.3.skip_ref
  37.1 4.7 %causal_sum.1.inner_ref = bf16[16,16,128]{2,1,0:T(8,128)(2,1)S(1)} custom-call(f32[8]{0:T(128)S(1)} %dynamic_slice.3.skip_ref, bf16[32,24,128]{2,1,0:T(8,128)(2,1)S(1)} %all-to-all-done.given_ref), custom_call_target="tpu_custom_call" | custom-call | flops 2147483648 | bytes 4194304 | tf_op jit(solution)/shard_map/causal_sum/pallas_call | solution.py:375
  41.9 7.2 %all-to-all-done.1.shares_ref = bf16[8,256,128]{2,1,0:T(8,128)(2,1)S(1)} async-done(((bf16[8,256,128]{2,1,0:T(8,128)(2,1)}), bf16[8,256,128]{2,1,0:T(8,128)(2,1)S(1)}, u32[]{:S(2)}, u32[]{:S(2)}) %all-to-all-start.1) | async-done | bytes 524320 | tf_op jit(solution)/shard_map/all_to_all | solution.py:461
  49.1 0.0 copy-done.2
  49.1 0.1 pack_middle.1
  49.2 14.3 %all_to_all.25.back_ref.middle_ref = bf16[32,16,128]{2,1,0:T(8,128)(2,1)S(1)} all-to-all(bf16[32,16,128]{2,1,0:T(8,128)(2,1)S(1)} %get-tuple-element.16), channel_id=1, replica_groups={{304,320,336,352,368,384,400,416,432,448,464,480,496,0,16,32,48,64,80,9..., dimensions={0} | all-to-all | bytes 262144 | tf_op jit(solution)/shard_map/all_to_all | solution.py:457
  63.5 0.9 spread_gated.1
  64.4 7.6 %all-to-all-start.3 = ((bf16[8,256,128]{2,1,0:T(8,128)(2,1)}), bf16[8,256,128]{2,1,0:T(8,128)(2,1)S(1)}, u32[]{:S(2)}, u32[]{:S(2)}) async-start(bf16[8,256,128]{2,1,0:T(8,128)(2,1)} %spread_gated.1), calls=%async_computation.3 | async-start | bytes 1048576 | tf_op jit(solution)/shard_map/all_to_all | solution.py:461
  72.0 5.7 %adjoint_sum.1 = bf16[16,16,128]{2,1,0:T(8,128)(2,1)} custom-call(f32[8]{0:T(128)S(1)} %dynamic_slice.3.skip_ref, bf16[32,24,128]{2,1,0:T(8,128)(2,1)S(1)} %all-to-all-done.given_ref, bf16[32,16,128]{2,1,0:T(8,128)(2,1)S(1)} %all_to_all.25.back_ref.middle_ref), custom_call_target="tpu_custom_call" | custom-call | flops 2147483648 | bytes 4194304 | tf_op jit(solution)/shard_map/adjoint_sum/pallas_call | solution.py:429
  77.7 5.3 %all-to-all-done.3.gated_ref = bf16[8,256,128]{2,1,0:T(8,128)(2,1)S(1)} async-done(((bf16[8,256,128]{2,1,0:T(8,128)(2,1)}), bf16[8,256,128]{2,1,0:T(8,128)(2,1)S(1)}, u32[]{:S(2)}, u32[]{:S(2)}) %all-to-all-start.3) | async-done | bytes 524320 | tf_op jit(solution)/shard_map/all_to_all | solution.py:461
  83.0 0.6 other_planes.1
  83.7 2.7 %collective-permute-start.1 = (bf16[7,256,128]{2,1,0:T(8,128)(2,1)S(1)}, bf16[7,256,128]{2,1,0:T(8,128)(2,1)S(1)}, u32[]{:S(2)}, u32[]{:S(2)}) collective-permute-start(bf16[7,256,128]{2,1,0:T(8,128)(2,1)S(1)} %other_planes.1), channel_id=1, source_target_pairs={{0,1},{1,0},{2,3},{3,2},{4,5},{5,4},{6,7},{7,6},{8,9},{9,8},{10,11... | collective-permute-start | bytes 1376264 | tf_op jit(solution)/shard_map/ppermute | solution.py:481
  86.4 0.8 slice_bitcast_fusion
  87.2 4.1 %collective-permute-start.2 = (bf16[256,128]{1,0:T(8,128)(2,1)S(1)}, bf16[256,128]{1,0:T(8,128)(2,1)S(1)}, u32[]{:S(2)}, u32[]{:S(2)}) collective-permute-start(bf16[256,128]{1,0:T(8,128)(2,1)S(1)} %slice_bitcast_fusion), channel_id=1, source_target_pairs={{0,1},{1,0},{2,3},{3,2},{4,5},{5,4},{6,7},{7,6},{8,9},{9,8},{10,11... | collective-permute-start | bytes 196616 | tf_op jit(solution)/shard_map/ppermute | solution.py:478
  91.3 10.2 %all-to-all-start.4 = ((bf16[32,8,128]{2,1,0:T(8,128)(2,1)}), bf16[32,8,128]{2,1,0:T(8,128)(2,1)S(1)}, u32[]{:S(2)}, u32[]{:S(2)}) async-start(bf16[32,8,128]{2,1,0:T(8,128)(2,1)} %bitcast.3), calls=%async_computation.4 | async-start | bytes 131072 | tf_op jit(solution)/shard_map/all_to_all | solution.py:457
  101.5 0.1 pad_add_fusion.half_ref
  101.6 0.0 copy-start.1
  101.6 2.2 %copy-done.1 = bf16[4096,512]{1,0:T(8,128)(2,1)S(1)} copy-done((bf16[4096,512]{1,0:T(8,128)(2,1)S(1)}, bf16[4096,512]{1,0:T(8,128)(2,1)}, u32[]{:S(2)}) %copy-start.1) | copy-done | bytes 4194328
  103.8 1.3 %output_early.1 = (f32[128,512]{1,0:T(8,128)S(1)}, bf16[8,256,512]{2,1,0:T(8,128)(2,1)S(1)}) custom-call(s32[2]{0:T(128)S(1)} %pad_add_fusion.half_ref, bf16[8,256,128]{2,1,0:T(8,128)(2,1)S(1)} %all-to-all-done.3.gated_ref, bf16[8,2,256,512]{3,2,1,0:T(8,128)(2,1)S(1)} %bitcast.11), custom_call_target="tpu_custom_call" | custom-call | flops 268435456 | bytes 4194304 | tf_op jit(solution)/shard_map/output_early/pallas_call | solution.py:118
  105.1 0.0 collective-permute-done.2.near_ref
  105.1 0.0 collective-permute-done.1.gated_ref
  105.1 1.1 %output_late.1 = bf16[128,512]{1,0:T(8,128)(2,1)} custom-call(bf16[7,256,128]{2,1,0:T(8,128)(2,1)S(1)} %collective-permute-done.1.gated_ref, bf16[256,128]{1,0:T(8,128)(2,1)S(1)} %collective-permute-done.2.near_ref, bf16[8,256,512]{2,1,0:T(8,128)(2,1)S(1)} %get-tuple-element.21.weight_ref, f32[128,512]{1,0:T(8,128)S(1)} %get-tuple-element.22.before_ref), custom_call_target="tpu_custom_call" | custom-call | flops 268435456 | bytes 4194304 | tf_op jit(solution)/shard_map/output_late/pallas_call | solution.py:126
  106.2 0.0 all-to-all-done.4
  106.2 0.7 last_grads.1
Async XLA Ops:
  0.6 20.1 %copy-start.3 = (bf16[128,512]{1,0:T(8,128)(2,1)S(1)}, bf16[128,512]{1,0:T(8,128)(2,1)}, u32[]{:S(2)}) copy-start(bf16[128,512]{1,0:T(8,128)(2,1)} %cotangent_ref.3) | copy-start | bytes 393220
  4.3 19.4 %collective-permute-start = (bf16[8,256,128]{2,1,0:T(8,128)(2,1)}, bf16[8,256,128]{2,1,0:T(8,128)(2,1)S(1)}, u32[]{:S(2)}, u32[]{:S(2)}) collective-permute-start(bf16[8,256,128]{2,1,0:T(8,128)(2,1)} %get-tuple-element.15), channel_id=1, source_target_pairs={{0,1},{1,0},{2,3},{3,2},{4,5},{5,4},{6,7},{7,6},{8,9},{9,8},{10,11... | collective-permute-start | bytes 1572872 | tf_op jit(solution)/shard_map/ppermute | solution.py:465
  9.7 16.7 %all-to-all-start = ((bf16[32,24,128]{2,1,0:T(8,128)(2,1)}), bf16[32,24,128]{2,1,0:T(8,128)(2,1)S(1)}, u32[]{:S(2)}, u32[]{:S(2)}) async-start(bf16[32,24,128]{2,1,0:T(8,128)(2,1)} %get-tuple-element.14), calls=%async_computation | async-start | bytes 393216 | tf_op jit(solution)/shard_map/all_to_all | solution.py:457
  20.7 2.2 %copy-start = (bf16[4096,512]{1,0:T(8,128)(2,1)S(1)}, bf16[4096,512]{1,0:T(8,128)(2,1)}, u32[]{:S(2)}) copy-start(bf16[4096,512]{1,0:T(8,128)(2,1)} %param.8) | copy-start | bytes 12582916
  22.9 14.2 %copy-start.4 = (f32[256]{0:T(256)S(1)}, f32[256]{0:T(256)}, u32[]{:S(2)}) copy-start(f32[256]{0:T(256)} %param.7) | copy-start | bytes 3076
  26.5 22.6 %all-to-all-start.1 = ((bf16[8,256,128]{2,1,0:T(8,128)(2,1)}), bf16[8,256,128]{2,1,0:T(8,128)(2,1)S(1)}, u32[]{:S(2)}, u32[]{:S(2)}) async-start(bf16[8,256,128]{2,1,0:T(8,128)(2,1)} %total_share.1), calls=%async_computation.1 | async-start | bytes 1048576 | tf_op jit(solution)/shard_map/all_to_all | solution.py:461
  37.1 12.0 %copy-start.2 = (bf16[3,256,128]{2,1,0:T(8,128)(2,1)S(1)}, bf16[3,256,128]{2,1,0:T(8,128)(2,1)}, u32[]{:S(2)}) copy-start(bf16[3,256,128]{2,1,0:T(8,128)(2,1)} %projected_ref.7) | copy-start | bytes 589828
  64.4 18.6 %all-to-all-start.3 = ((bf16[8,256,128]{2,1,0:T(8,128)(2,1)}), bf16[8,256,128]{2,1,0:T(8,128)(2,1)S(1)}, u32[]{:S(2)}, u32[]{:S(2)}) async-start(bf16[8,256,128]{2,1,0:T(8,128)(2,1)} %spread_gated.1), calls=%async_computation.3 | async-start | bytes 1048576 | tf_op jit(solution)/shard_map/all_to_all | solution.py:461
  83.7 21.4 %collective-permute-start.1 = (bf16[7,256,128]{2,1,0:T(8,128)(2,1)S(1)}, bf16[7,256,128]{2,1,0:T(8,128)(2,1)S(1)}, u32[]{:S(2)}, u32[]{:S(2)}) collective-permute-start(bf16[7,256,128]{2,1,0:T(8,128)(2,1)S(1)} %other_planes.1), channel_id=1, source_target_pairs={{0,1},{1,0},{2,3},{3,2},{4,5},{5,4},{6,7},{7,6},{8,9},{9,8},{10,11... | collective-permute-start | bytes 1376264 | tf_op jit(solution)/shard_map/ppermute | solution.py:481
  87.2 17.9 %collective-permute-start.2 = (bf16[256,128]{1,0:T(8,128)(2,1)S(1)}, bf16[256,128]{1,0:T(8,128)(2,1)S(1)}, u32[]{:S(2)}, u32[]{:S(2)}) collective-permute-start(bf16[256,128]{1,0:T(8,128)(2,1)S(1)} %slice_bitcast_fusion), channel_id=1, source_target_pairs={{0,1},{1,0},{2,3},{3,2},{4,5},{5,4},{6,7},{7,6},{8,9},{9,8},{10,11... | collective-permute-start | bytes 196616 | tf_op jit(solution)/shard_map/ppermute | solution.py:478
  91.3 14.9 %all-to-all-start.4 = ((bf16[32,8,128]{2,1,0:T(8,128)(2,1)}), bf16[32,8,128]{2,1,0:T(8,128)(2,1)S(1)}, u32[]{:S(2)}, u32[]{:S(2)}) async-start(bf16[32,8,128]{2,1,0:T(8,128)(2,1)} %bitcast.3), calls=%async_computation.4 | async-start | bytes 131072 | tf_op jit(solution)/shard_map/all_to_all | solution.py:457
  101.6 2.2 %copy-start.1 = (bf16[4096,512]{1,0:T(8,128)(2,1)S(1)}, bf16[4096,512]{1,0:T(8,128)(2,1)}, u32[]{:S(2)}) copy-start(bf16[4096,512]{1,0:T(8,128)(2,1)} %param.8) | copy-start | bytes 12582916

commit v8 on v7

--- a/solution.py
+++ b/solution.py
@@ -476,7 +476,7 @@
     plane = lax.axis_index("chan") >> 1
     grads_there, gated = lax.optimization_barrier((grads_there, gated))
     near = lax.ppermute(gated[0], "chan", pairs)
-    grads_there, gated_half = lax.optimization_barrier((grads_there, gated_half))
+    grads_there, gated_half, near = lax.optimization_barrier((grads_there, gated_half, near))
     start = (plane - FIRST_GATED + 1) % planes
     gated_other = lax.ppermute(other_planes(start.reshape(1), gated_half), "chan", pairs)
     place = jnp.stack([half, plane])

time: 108 us -> 105 us (0.972)
  waiting for transfers between devices: 14.5 us -> 12.4 us
    all_to_all x2, waiting for transfers between devices: 12.5 us -> 7.22 us  [exchange_z(): lax.all_to_all(array, 'chan', 0, 0, tiled=True, axis_index_groups=groups)]
    ppermute x1, waiting for transfers between devices: 0.01 us -> 3.19 us  [per_device(): near = lax.ppermute(gated[0], 'chan', pairs)]
where the time goes in v8:
time: 105 us
  starting transfers between devices  51.3 us (49%)
  Pallas kernels  20.4 us (19%)
  blocking collectives  14.3 us (14%)
  waiting for transfers between devices  12.4 us (12%)
  local copies, waits for them, and re-layouts  5.3 us (5%)
    all_to_all x2, starting transfers between devices, exchange_seq(): lax.all_to_all(array, 'seq', 0, 0, tiled=True, axis_index_groups=groups)  21 us
    all_to_all x2, starting transfers between devices, exchange_z(): lax.all_to_all(array, 'chan', 0, 0, tiled=True, axis_index_groups=groups)  18.2 us
    all_to_all x1, blocking collectives, exchange_seq(): lax.all_to_all(array, 'seq', 0, 0, tiled=True, axis_index_groups=groups)  14.3 us
    all_to_all x2, waiting for transfers between devices, exchange_z(): lax.all_to_all(array, 'chan', 0, 0, tiled=True, axis_index_groups=groups)  7.22 us
    pallas_call x1, Pallas kernels, adjoint(): call(kernel, [SMEM, VMEM, VMEM], jax.ShapeDtypeStruct((chunks // 2, 2 * p...  5.74 us
    ppermute x1, starting transfers between devices, per_device(): received = lax.ppermute(share_other, 'chan', pairs)  5.48 us
    pallas_call x1, Pallas kernels, causal(): call(kernel, [SMEM, VMEM], jax.ShapeDtypeStruct((chunks // 2, 2 * per, BL...  4.73 us
    unnamed x10, local copies, waits for them, and re-layouts  4.38 us
  transfers between devices with their start and end apart: 7, of which 3 were waited for; matrix products, arithmetic and copies ran while one was open for 1% of the time, Pallas kernels for 14%

profile of v8, /device:TPU:1, one launch (start us, length us, event | category | flops | bytes accessed | tf_op | source)
XLA Modules:
  0.0 104.5 jit_solution(11860557594161811703)
XLA Ops:
  0.6 0.0 copy-start.3
  0.6 3.6 %first_share.1 = (bf16[8,256,128]{2,1,0:T(8,128)(2,1)}, bf16[32,24,128]{2,1,0:T(8,128)(2,1)}) custom-call(s32[1]{0:T(128)} %bitcast.half_ref, bf16[8,2,256,512]{3,2,1,0:T(8,128)(2,1)} %bitcast.9, bf16[128,512]{1,0:T(8,128)(2,1)} %cotangent_ref.3, bf16[3,256,128]{2,1,0:T(8,128)(2,1)} %projected_ref.7, f32[256,128]{1,0:T(8,128)} %filters_ref.1), custom_call_target="tpu_custom_call" | custom-call | flops 268435456 | bytes 4194304 | tf_op jit(solution)/shard_map/first_share/pallas_call | solution.py:195
  4.3 5.5 %collective-permute-start = (bf16[8,256,128]{2,1,0:T(8,128)(2,1)}, bf16[8,256,128]{2,1,0:T(8,128)(2,1)S(1)}, u32[]{:S(2)}, u32[]{:S(2)}) collective-permute-start(bf16[8,256,128]{2,1,0:T(8,128)(2,1)} %get-tuple-element.16), channel_id=1, source_target_pairs={{0,1},{1,0},{2,3},{3,2},{4,5},{5,4},{6,7},{7,6},{8,9},{9,8},{10,11... | collective-permute-start | bytes 1572872 | tf_op jit(solution)/shard_map/ppermute | solution.py:465
  9.7 11.0 %all-to-all-start = ((bf16[32,24,128]{2,1,0:T(8,128)(2,1)}), bf16[32,24,128]{2,1,0:T(8,128)(2,1)S(1)}, u32[]{:S(2)}, u32[]{:S(2)}) async-start(bf16[32,24,128]{2,1,0:T(8,128)(2,1)} %get-tuple-element.15), calls=%async_computation | async-start | bytes 393216 | tf_op jit(solution)/shard_map/all_to_all | solution.py:457
  20.7 0.0 copy-done.3
  20.7 0.0 copy-start
  20.7 2.2 %copy-done = bf16[4096,512]{1,0:T(8,128)(2,1)S(1)} copy-done((bf16[4096,512]{1,0:T(8,128)(2,1)S(1)}, bf16[4096,512]{1,0:T(8,128)(2,1)}, u32[]{:S(2)}) %copy-start) | copy-done | bytes 4194328
  22.9 0.0 copy-start.4
  22.9 0.7 partial_grad_gated.1.share_ref
  23.6 0.0 collective-permute-done.received_ref
  23.6 0.9 total_share.1
  24.5 2.0 %all-to-all-done.given_ref = bf16[32,24,128]{2,1,0:T(8,128)(2,1)S(1)} async-done(((bf16[32,24,128]{2,1,0:T(8,128)(2,1)}), bf16[32,24,128]{2,1,0:T(8,128)(2,1)S(1)}, u32[]{:S(2)}, u32[]{:S(2)}) %all-to-all-start) | async-done | bytes 196640 | tf_op jit(solution)/shard_map/all_to_all | solution.py:457
  26.5 10.6 %all-to-all-start.1 = ((bf16[8,256,128]{2,1,0:T(8,128)(2,1)}), bf16[8,256,128]{2,1,0:T(8,128)(2,1)S(1)}, u32[]{:S(2)}, u32[]{:S(2)}) async-start(bf16[8,256,128]{2,1,0:T(8,128)(2,1)} %total_share.1), calls=%async_computation.1 | async-start | bytes 1048576 | tf_op jit(solution)/shard_map/all_to_all | solution.py:461
  37.1 0.0 copy-start.2
  37.1 0.0 copy-done.4
  37.1 0.1 dynamic_slice.3.skip_ref
  37.1 4.7 %causal_sum.1.inner_ref = bf16[16,16,128]{2,1,0:T(8,128)(2,1)S(1)} custom-call(f32[8]{0:T(128)S(1)} %dynamic_slice.3.skip_ref, bf16[32,24,128]{2,1,0:T(8,128)(2,1)S(1)} %all-to-all-done.given_ref), custom_call_target="tpu_custom_call" | custom-call | flops 2147483648 | bytes 4194304 | tf_op jit(solution)/shard_map/causal_sum/pallas_call | solution.py:375
  41.9 7.2 %all-to-all-done.1.shares_ref = bf16[8,256,128]{2,1,0:T(8,128)(2,1)S(1)} async-done(((bf16[8,256,128]{2,1,0:T(8,128)(2,1)}), bf16[8,256,128]{2,1,0:T(8,128)(2,1)S(1)}, u32[]{:S(2)}, u32[]{:S(2)}) %all-to-all-start.1) | async-done | bytes 524320 | tf_op jit(solution)/shard_map/all_to_all | solution.py:461
  49.1 0.0 copy-done.2
  49.1 0.1 pack_middle.1
  49.2 14.3 %all_to_all.25.back_ref.middle_ref = bf16[32,16,128]{2,1,0:T(8,128)(2,1)S(1)} all-to-all(bf16[32,16,128]{2,1,0:T(8,128)(2,1)S(1)} %get-tuple-element.17), channel_id=1, replica_groups={{304,320,336,352,368,384,400,416,432,448,464,480,496,0,16,32,48,64,80,9..., dimensions={0} | all-to-all | bytes 262144 | tf_op jit(solution)/shard_map/all_to_all | solution.py:457
  63.5 0.9 spread_gated.1
  64.4 7.6 %all-to-all-start.3 = ((bf16[8,256,128]{2,1,0:T(8,128)(2,1)}), bf16[8,256,128]{2,1,0:T(8,128)(2,1)S(1)}, u32[]{:S(2)}, u32[]{:S(2)}) async-start(bf16[8,256,128]{2,1,0:T(8,128)(2,1)} %spread_gated.1), calls=%async_computation.3 | async-start | bytes 1048576 | tf_op jit(solution)/shard_map/all_to_all | solution.py:461
  72.0 5.7 %adjoint_sum.1 = bf16[16,16,128]{2,1,0:T(8,128)(2,1)} custom-call(f32[8]{0:T(128)S(1)} %dynamic_slice.3.skip_ref, bf16[32,24,128]{2,1,0:T(8,128)(2,1)S(1)} %all-to-all-done.given_ref, bf16[32,16,128]{2,1,0:T(8,128)(2,1)S(1)} %all_to_all.25.back_ref.middle_ref), custom_call_target="tpu_custom_call" | custom-call | flops 2147483648 | bytes 4194304 | tf_op jit(solution)/shard_map/adjoint_sum/pallas_call | solution.py:429
  77.7 0.8 slice_bitcast_fusion
  78.6 3.3 %collective-permute-start.1 = (bf16[256,128]{1,0:T(8,128)(2,1)S(1)}, bf16[256,128]{1,0:T(8,128)(2,1)S(1)}, u32[]{:S(2)}, u32[]{:S(2)}) collective-permute-start(bf16[256,128]{1,0:T(8,128)(2,1)S(1)} %slice_bitcast_fusion), channel_id=1, source_target_pairs={{0,1},{1,0},{2,3},{3,2},{4,5},{5,4},{6,7},{7,6},{8,9},{9,8},{10,11... | collective-permute-start | bytes 196616 | tf_op jit(solution)/shard_map/ppermute | solution.py:478
  81.9 3.2 %collective-permute-done.1.near_ref = bf16[256,128]{1,0:T(8,128)(2,1)S(1)} collective-permute-done((bf16[256,128]{1,0:T(8,128)(2,1)S(1)}, bf16[256,128]{1,0:T(8,128)(2,1)S(1)}, u32[]{:S(2)}, u32[]{:S(2)}) %collective-permute-start.1) | collective-permute-done | bytes 65568 | tf_op jit(solution)/shard_map/ppermute | solution.py:478
  85.1 0.0 all-to-all-done.3.gated_ref
  85.1 0.7 other_planes.1
  85.7 3.4 %collective-permute-start.2 = (bf16[7,256,128]{2,1,0:T(8,128)(2,1)S(1)}, bf16[7,256,128]{2,1,0:T(8,128)(2,1)S(1)}, u32[]{:S(2)}, u32[]{:S(2)}) collective-permute-start(bf16[7,256,128]{2,1,0:T(8,128)(2,1)S(1)} %other_planes.1), channel_id=1, source_target_pairs={{0,1},{1,0},{2,3},{3,2},{4,5},{5,4},{6,7},{7,6},{8,9},{9,8},{10,11... | collective-permute-start | bytes 1376264 | tf_op jit(solution)/shard_map/ppermute | solution.py:481
  89.1 10.0 %all-to-all-start.4 = ((bf16[32,8,128]{2,1,0:T(8,128)(2,1)}), bf16[32,8,128]{2,1,0:T(8,128)(2,1)S(1)}, u32[]{:S(2)}, u32[]{:S(2)}) async-start(bf16[32,8,128]{2,1,0:T(8,128)(2,1)} %bitcast.4), calls=%async_computation.4 | async-start | bytes 131072 | tf_op jit(solution)/shard_map/all_to_all | solution.py:457
  99.1 0.1 pad_add_fusion.half_ref
  99.2 0.0 copy-start.1
  99.2 2.2 %copy-done.1 = bf16[4096,512]{1,0:T(8,128)(2,1)S(1)} copy-done((bf16[4096,512]{1,0:T(8,128)(2,1)S(1)}, bf16[4096,512]{1,0:T(8,128)(2,1)}, u32[]{:S(2)}) %copy-start.1) | copy-done | bytes 4194328
  101.4 1.3 %output_early.1 = (f32[128,512]{1,0:T(8,128)S(1)}, bf16[8,256,512]{2,1,0:T(8,128)(2,1)S(1)}) custom-call(s32[2]{0:T(128)S(1)} %pad_add_fusion.half_ref, bf16[8,256,128]{2,1,0:T(8,128)(2,1)S(1)} %all-to-all-done.3.gated_ref, bf16[8,2,256,512]{3,2,1,0:T(8,128)(2,1)S(1)} %bitcast.11), custom_call_target="tpu_custom_call" | custom-call | flops 268435456 | bytes 4194304 | tf_op jit(solution)/shard_map/output_early/pallas_call | solution.py:118
  102.7 0.0 collective-permute-done.2.gated_ref
  102.7 1.1 %output_late.1 = bf16[128,512]{1,0:T(8,128)(2,1)} custom-call(bf16[7,256,128]{2,1,0:T(8,128)(2,1)S(1)} %collective-permute-done.2.gated_ref, bf16[256,128]{1,0:T(8,128)(2,1)S(1)} %collective-permute-done.1.near_ref, bf16[8,256,512]{2,1,0:T(8,128)(2,1)S(1)} %get-tuple-element.23.weight_ref, f32[128,512]{1,0:T(8,128)S(1)} %get-tuple-element.24.before_ref), custom_call_target="tpu_custom_call" | custom-call | flops 268435456 | bytes 4194304 | tf_op jit(solution)/shard_map/output_late/pallas_call | solution.py:126
  103.8 0.0 all-to-all-done.4
  103.8 0.7 last_grads.1
Async XLA Ops:
  0.6 20.1 %copy-start.3 = (bf16[128,512]{1,0:T(8,128)(2,1)S(1)}, bf16[128,512]{1,0:T(8,128)(2,1)}, u32[]{:S(2)}) copy-start(bf16[128,512]{1,0:T(8,128)(2,1)} %cotangent_ref.3) | copy-start | bytes 393220
  4.3 19.4 %collective-permute-start = (bf16[8,256,128]{2,1,0:T(8,128)(2,1)}, bf16[8,256,128]{2,1,0:T(8,128)(2,1)S(1)}, u32[]{:S(2)}, u32[]{:S(2)}) collective-permute-start(bf16[8,256,128]{2,1,0:T(8,128)(2,1)} %get-tuple-element.16), channel_id=1, source_target_pairs={{0,1},{1,0},{2,3},{3,2},{4,5},{5,4},{6,7},{7,6},{8,9},{9,8},{10,11... | collective-permute-start | bytes 1572872 | tf_op jit(solution)/shard_map/ppermute | solution.py:465
  9.7 16.7 %all-to-all-start = ((bf16[32,24,128]{2,1,0:T(8,128)(2,1)}), bf16[32,24,128]{2,1,0:T(8,128)(2,1)S(1)}, u32[]{:S(2)}, u32[]{:S(2)}) async-start(bf16[32,24,128]{2,1,0:T(8,128)(2,1)} %get-tuple-element.15), calls=%async_computation | async-start | bytes 393216 | tf_op jit(solution)/shard_map/all_to_all | solution.py:457
  20.7 2.2 %copy-start = (bf16[4096,512]{1,0:T(8,128)(2,1)S(1)}, bf16[4096,512]{1,0:T(8,128)(2,1)}, u32[]{:S(2)}) copy-start(bf16[4096,512]{1,0:T(8,128)(2,1)} %param.8) | copy-start | bytes 12582916
  22.9 14.2 %copy-start.4 = (f32[256]{0:T(256)S(1)}, f32[256]{0:T(256)}, u32[]{:S(2)}) copy-start(f32[256]{0:T(256)} %param.7) | copy-start | bytes 3076
  26.5 22.6 %all-to-all-start.1 = ((bf16[8,256,128]{2,1,0:T(8,128)(2,1)}), bf16[8,256,128]{2,1,0:T(8,128)(2,1)S(1)}, u32[]{:S(2)}, u32[]{:S(2)}) async-start(bf16[8,256,128]{2,1,0:T(8,128)(2,1)} %total_share.1), calls=%async_computation.1 | async-start | bytes 1048576 | tf_op jit(solution)/shard_map/all_to_all | solution.py:461
  37.1 12.0 %copy-start.2 = (bf16[3,256,128]{2,1,0:T(8,128)(2,1)S(1)}, bf16[3,256,128]{2,1,0:T(8,128)(2,1)}, u32[]{:S(2)}) copy-start(bf16[3,256,128]{2,1,0:T(8,128)(2,1)} %projected_ref.7) | copy-start | bytes 589828
  64.4 20.7 %all-to-all-start.3 = ((bf16[8,256,128]{2,1,0:T(8,128)(2,1)}), bf16[8,256,128]{2,1,0:T(8,128)(2,1)S(1)}, u32[]{:S(2)}, u32[]{:S(2)}) async-start(bf16[8,256,128]{2,1,0:T(8,128)(2,1)} %spread_gated.1), calls=%async_computation.3 | async-start | bytes 1048576 | tf_op jit(solution)/shard_map/all_to_all | solution.py:461
  78.6 6.5 %collective-permute-start.1 = (bf16[256,128]{1,0:T(8,128)(2,1)S(1)}, bf16[256,128]{1,0:T(8,128)(2,1)S(1)}, u32[]{:S(2)}, u32[]{:S(2)}) collective-permute-start(bf16[256,128]{1,0:T(8,128)(2,1)S(1)} %slice_bitcast_fusion), channel_id=1, source_target_pairs={{0,1},{1,0},{2,3},{3,2},{4,5},{5,4},{6,7},{7,6},{8,9},{9,8},{10,11... | collective-permute-start | bytes 196616 | tf_op jit(solution)/shard_map/ppermute | solution.py:478
  85.7 17.0 %collective-permute-start.2 = (bf16[7,256,128]{2,1,0:T(8,128)(2,1)S(1)}, bf16[7,256,128]{2,1,0:T(8,128)(2,1)S(1)}, u32[]{:S(2)}, u32[]{:S(2)}) collective-permute-start(bf16[7,256,128]{2,1,0:T(8,128)(2,1)S(1)} %other_planes.1), channel_id=1, source_target_pairs={{0,1},{1,0},{2,3},{3,2},{4,5},{5,4},{6,7},{7,6},{8,9},{9,8},{10,11... | collective-permute-start | bytes 1376264 | tf_op jit(solution)/shard_map/ppermute | solution.py:481
  89.1 14.7 %all-to-all-start.4 = ((bf16[32,8,128]{2,1,0:T(8,128)(2,1)}), bf16[32,8,128]{2,1,0:T(8,128)(2,1)S(1)}, u32[]{:S(2)}, u32[]{:S(2)}) async-start(bf16[32,8,128]{2,1,0:T(8,128)(2,1)} %bitcast.4), calls=%async_computation.4 | async-start | bytes 131072 | tf_op jit(solution)/shard_map/all_to_all | solution.py:457
  99.2 2.2 %copy-start.1 = (bf16[4096,512]{1,0:T(8,128)(2,1)S(1)}, bf16[4096,512]{1,0:T(8,128)(2,1)}, u32[]{:S(2)}) copy-start(bf16[4096,512]{1,0:T(8,128)(2,1)} %param.8) | copy-start | bytes 12582916
